TPU v7x, 32 devices: a whole 2x2x4 slice. The times are simulated.
32 devices in a mesh: space: 4 (over z), rep: 8 (over y, x, core).
Axes of the slice: x: 2, y: 2, z: 4, core: 2. Of those that a mesh axis runs over, the one named last changes fastest.
Arguments:
- features: bfloat16 [8, 20, 96, 1024], P('rep', 'space'), may hold values from -4 to 4.5
- labels: int32 [8, 20, 96], P('rep', 'space'), may hold values from 0 to 2
- w_in: bfloat16 [29, 1024, 256], replicated, may hold values from -0.0625 to 0.0625
- w_proj: bfloat16 [1280, 256], replicated, may hold values from -0.15625 to 0.15625
- w_cls: bfloat16 [256, 3], replicated, may hold values from -0.375 to 0.375
- class_weight: float32 [3], replicated, may hold values from 0.5 to 4
- matching: int32 [8], replicated, may hold values from 0 to 7, as said below
Outputs:
- avg_in: float32 [8, 29696, 256], P('rep', 'space')
- avg_proj: float32 [8, 1280, 256], P('rep', 'space')
- avg_cls: float32 [8, 256, 3], P('rep', 'space')
Inputs may be any that keep to these rules, and one draw needn't show every extreme that they name: matching[i] = i XOR matching[0] with matching[0] nonzero, so replicas are matched in pairs.
All inputs are finite; a program needn't handle non-finite values.
Results may differ from a plain program's by a relative error of at most 0.025.
The roundings to bfloat16 on the way count: a program that leaves them out, or rounds other values in their place, can miss the bound.
Values may be sent and summed in bfloat16 or wider, within the bound.
No kernel may reach another device: no remote copies, remote signals or barrier semaphores. Data moves between devices by JAX's collectives and lax.ppermute only.
A program may use at most 256 MiB of HBM per device.

v0:
```python
import functools

import jax
import jax.numpy as jnp
import numpy as np
from jax import lax
from jax.experimental import pallas as pl
from jax.experimental.pallas import tpu as pltpu
from jax.sharding import PartitionSpec as P

LOSS_SCALE = 1024.0
RATE = 12
EDGE = 40
EXTRA = 16
BF16 = jnp.bfloat16
F32 = jnp.float32
BLOCK_VMEM = 32 * 1024 * 1024
FIELD_VMEM = 44 * 1024 * 1024


def nn(a, b):
    return lax.dot_general(a, b, (((1,), (0,)), ((), ())), preferred_element_type=F32)


def nt(a, b):
    return lax.dot_general(a, b, (((1,), (1,)), ((), ())), preferred_element_type=F32)


def identity(size):
    rows = lax.broadcasted_iota(jnp.int32, (size, size), 0)
    cols = lax.broadcasted_iota(jnp.int32, (size, size), 1)
    return (rows == cols).astype(F32).astype(BF16)


class Plan:
    def __init__(self, n, reps, rows, cols, c_in, c_out, classes):
        self.n, self.reps, self.rows, self.cols = n, reps, rows, cols
        self.c_in, self.c_out, self.classes = c_in, c_out, classes
        self.height = rows * n
        self.pix = rows * cols
        self.total = self.pix * n
        self.shifted = [k for k in (1, 2, 3) if RATE * k < self.height]
        self.direct = [k for k in range(4) if k not in self.shifted]
        self.n_sh = len(self.shifted)
        row = lambda k, a: [1 + 9 * (k - 1) + 3 * a + b for b in range(3)]
        still = [row(k, 1) for k in self.direct[1:]]
        self.loads = [[0] + (still[0] if still else [])] + still[1:]
        for k in self.shifted:
            self.loads += [row(k, a) for a in range(3)]
        self.units = 29
        self.unit_rows = c_in // n
        self.proj_rows = 5 * c_out // n
        self.cls_rows = c_out // n
        tables = [self.table(s) for s in range(n)]
        self.n_slots = max(t[1] for t in tables)
        self.depth = max(t[2] for t in tables)
        self.tables = np.array([
            sum((c + [[0] * 6] * (self.depth - len(c)) for c in t[0]), []) for t in tables
        ], np.int32).reshape(n, -1)
        self.flags = self.tables.shape[1]
        self.tables = np.concatenate([
            self.tables,
            np.array([[len(c) for c in t[0]] + t[3] + [s] for s, t in enumerate(tables)], np.int32),
        ], axis=1)

    def tap(self, t):
        if t == 0:
            return (0, 1, 1)
        if t == 28:
            return None
        k, rest = (t - 1) // 9 + 1, (t - 1) % 9
        a, b = rest // 3, rest % 3
        if a != 1 and k not in self.shifted:
            return "zero"
        return (k, a, b)

    def table(self, s):
        parts = [[] for _ in range(self.n)]
        slots = {}
        for local in range(self.units):
            unit = s * self.units + local
            c, tap = unit % self.n, self.tap(unit // self.n)
            if tap is None or tap == "zero":
                parts[c].append([0, 0, 0, 0, 1 if tap is None else 2, local])
                continue
            k, a, b = tap
            move = (a - 1) * RATE * k
            valid = [
                j for j in range(self.n)
                if any(0 <= self.rows * j + i - move < self.height for i in range(self.rows))
            ]
            slot = slots.setdefault((k, b), len(slots))
            parts[c].append([slot, move, valid[0], valid[-1] + 1, 0, local])
        want = [slots.get((k, b), -1) for k in range(4) for b in range(3)]
        return parts, len(slots), max(len(c) for c in parts), want


def pack_kernel(pix, x_ref, lab_ref, out_ref):
    x = x_ref[...]
    out_ref[:pix, :] = x
    total = jnp.sum(x.astype(F32), axis=0, keepdims=True)
    head = total.astype(BF16).astype(F32)
    mid = (total - head).astype(BF16).astype(F32)
    row = lax.broadcasted_iota(jnp.int32, (EXTRA, x.shape[1]), 0)
    extra = jnp.zeros((EXTRA, x.shape[1]), F32)
    for at, value in enumerate((head, mid, total - head - mid, lab_ref[...])):
        extra = jnp.where(row == at, value, extra)
    out_ref[pix:, :] = extra.astype(BF16)


def block_kernel(plan, n_cand, aliased, meta, *refs):
    rows, cols, c_in, c_out = plan.rows, plan.cols, plan.c_in, plan.c_out
    pix = plan.pix
    cands = refs[:n_cand]
    w_hbm = refs[n_cand]
    refs = refs[n_cand + 1 + (4 if aliased else 0):]
    xt_out, cat_out, s_out, aux_out = refs[:4]
    xin, wbuf, xtb, catb, sb, res, sem_x, sem_w, sem_o, sem_s = refs[4:]
    xbuf = xin.at[pl.ds(0, pix)]
    step = pl.program_id(0)
    source, block, field = meta[step, 0], meta[step, 1], meta[step, 2]

    for c in range(n_cand):
        @pl.when(source == c)
        def _(c=c):
            pltpu.make_async_copy(cands[c], xin, sem_x).start()

    def weights(group, taps):
        return [
            pltpu.make_async_copy(
                w_hbm.at[tap], wbuf.at[group, :, pl.ds(i * c_out, c_out)], sem_w.at[group, i]
            )
            for i, tap in enumerate(taps)
        ]

    @pl.when(step == 0)
    def _():
        for group, taps in enumerate(plan.loads):
            for copy in weights(group, taps):
                copy.start()
        res[:, :EDGE, :] = jnp.zeros((rows, EDGE, res.shape[2]), F32)
        res[:, EDGE + cols:, :] = jnp.zeros((rows, EDGE, res.shape[2]), F32)

    pltpu.make_async_copy(cands[0], xin, sem_x).wait()
    aux_copy = pltpu.make_async_copy(
        xin.at[pl.ds(pix, EXTRA)], aux_out.at[field, block], sem_o.at[2]
    )
    aux_copy.start()
    eye = identity(256)
    for c in range(c_in // 256):
        part = slice(c * 256, (c + 1) * 256)
        xtb[part, :] = nt(eye, xbuf[:, part]).astype(BF16)
    xt_copy = pltpu.make_async_copy(xtb, xt_out.at[field, block], sem_o.at[0])
    xt_copy.start()

    def in_field(move):
        first = block * rows + move
        return jnp.logical_and(first + rows - 1 >= 0, first < plan.height)

    def loaded(group, taps):
        @pl.when(step == 0)
        def _():
            for copy in weights(group, taps):
                copy.wait()

    def columns(k, first):
        r = RATE * k
        part = [slice(first + i * c_out, first + (i + 1) * c_out) for i in range(3)]
        return (
            res[:, EDGE - r:EDGE - r + cols, part[0]]
            + res[:, EDGE:EDGE + cols, part[1]]
            + res[:, EDGE + r:EDGE + r + cols, part[2]]
        )

    def relu_to(k, value):
        at = plan.direct.index(k)
        catb[:, at * c_out:(at + 1) * c_out] = (
            jnp.maximum(value, 0.0).astype(BF16).reshape(pix, c_out)
        )

    def shifted_copy(at):
        return pltpu.make_async_copy(
            sb.at[at], s_out.at[at, field, pl.ds(block * rows, rows)], sem_s.at[at]
        )

    group = 0
    first = c_out
    loaded(0, plan.loads[0])
    width = len(plan.loads[0]) * c_out
    res[:, EDGE:EDGE + cols, :width] = nn(xbuf[...], wbuf[0, :, :width]).reshape(
        rows, cols, width
    )
    relu_to(0, res[:, EDGE:EDGE + cols, :c_out])
    group = 1
    for k in plan.direct[1:]:
        if first + 3 * c_out > width:
            loaded(group, plan.loads[group])
            width, first = 3 * c_out, 0
            res[:, EDGE:EDGE + cols, :width] = nn(xbuf[...], wbuf[group, :, :width]).reshape(
                rows, cols, width
            )
            group += 1
        relu_to(k, columns(k, first))
        first += 3 * c_out
    cat_copy = pltpu.make_async_copy(catb, cat_out.at[field, block], sem_o.at[1])
    cat_copy.start()
    width = 3 * c_out
    for at, k in enumerate(plan.shifted):
        for a in range(3):
            loaded(group + 3 * at + a, plan.loads[group + 3 * at + a])

        def one(a, _, k=k, at=at, base=group + 3 * at):
            @pl.when(in_field((1 - a) * RATE * k))
            def _():
                res[:, EDGE:EDGE + cols, :width] = nn(
                    xbuf[...], wbuf[base + a, :, :width]
                ).reshape(rows, cols, width)
                sb[3 * at + a] = columns(k, 0)
                shifted_copy(3 * at + a).start()
            return 0

        lax.fori_loop(0, 3, one, 0)
    aux_copy.wait()
    xt_copy.wait()
    cat_copy.wait()
    for at, k in enumerate(plan.shifted):
        for a in range(3):
            @pl.when(in_field((1 - a) * RATE * k))
            def _(at=at, a=a):
                shifted_copy(3 * at + a).wait()


def run_blocks(plan, slots, w_in, state):
    arrays, meta = [], []
    for cands, (source, block, field) in slots:
        meta.append(jnp.stack([
            jnp.asarray(v, jnp.int32) for v in (source + len(arrays), block, field)
        ]))
        arrays.extend(cands)
    meta = jnp.stack(meta)
    n, rows, cols, pix = plan.n, plan.rows, plan.cols, plan.pix
    c_in, c_out, n_sh = plan.c_in, plan.c_out, plan.n_sh
    shapes = [
        jax.ShapeDtypeStruct((2, n, c_in, pix), BF16),
        jax.ShapeDtypeStruct((2, n, pix, len(plan.direct) * c_out), BF16),
        jax.ShapeDtypeStruct((3 * n_sh, 2, n * rows, cols, c_out), F32),
        jax.ShapeDtypeStruct((2, n, EXTRA, c_in), BF16),
    ]
    aliased = state is not None
    operands = [*arrays, w_in] + (list(state) if aliased else [])
    aliases = {1 + len(arrays) + 1 + i: i for i in range(4)} if aliased else {}
    widest = max(len(g) for g in plan.loads) * c_out
    return pl.pallas_call(
        functools.partial(block_kernel, plan, len(arrays), aliased),
        grid_spec=pltpu.PrefetchScalarGridSpec(
            num_scalar_prefetch=1,
            grid=(len(slots),),
            in_specs=[pl.BlockSpec(memory_space=pl.ANY)] * len(operands),
            out_specs=[pl.BlockSpec(memory_space=pl.ANY)] * 4,
            scratch_shapes=[
                pltpu.VMEM((pix + EXTRA, c_in), BF16),
                pltpu.VMEM((len(plan.loads), c_in, widest), BF16),
                pltpu.VMEM((c_in, pix), BF16),
                pltpu.VMEM((pix, len(plan.direct) * c_out), BF16),
                pltpu.VMEM((3 * n_sh, rows, cols, c_out), F32),
                pltpu.VMEM((rows, cols + 2 * EDGE, widest), F32),
                pltpu.SemaphoreType.DMA,
                pltpu.SemaphoreType.DMA((len(plan.loads), 4)),
                pltpu.SemaphoreType.DMA((3,)),
                pltpu.SemaphoreType.DMA((3 * n_sh,)),
            ],
        ),
        out_shape=shapes,
        input_output_aliases=aliases,
        compiler_params=pltpu.CompilerParams(
            dimension_semantics=("arbitrary",), vmem_limit_bytes=BLOCK_VMEM
        ),
        cost_estimate=pl.CostEstimate(
            flops=len(slots) * 2 * pix * c_in * c_out * (10 + 6 * n_sh),
            bytes_accessed=20_000_000 + len(slots) * 20_000_000,
            transcendentals=0,
        ),
        name="block_forward",
    )(meta, *operands)


def field_kernel(plan, last, tab, *refs):
    n, rows, cols, pix = plan.n, plan.rows, plan.cols, plan.pix
    c_in, c_out, n_sh = plan.c_in, plan.c_out, plan.n_sh
    n_rows_in = 2 * n_sh * rows
    unit_rows, depth, flags = plan.unit_rows, plan.depth, plan.flags
    cat_ref = refs[0]
    mid_refs = refs[1:1 + n_sh]
    s_refs = refs[1 + n_sh:1 + n_sh + n_rows_in]
    refs = refs[1 + n_sh + n_rows_in:]
    aux_ref, all_ref, w28_ref, wproj_ref, wcls_ref, cw_ref, xt_ref = refs[:7]
    refs = refs[7:]
    if last:
        prev_g, prev_p, prev_c = refs[:3]
        refs = refs[3:]
    g_out, p_out, c_ref_out = refs[:3]
    dbuf, pad, mean, gpt, gp, gc, sdy, spool, pact, cat5, acc, stage, sems = refs[3:]
    step = pl.program_id(0)
    edge_rows = rows - 1

    def finish(value, prev):
        grad = value.astype(BF16)
        if not last:
            return grad
        return (prev.astype(F32) + grad.astype(F32)) * 0.5

    @pl.when(step == 0)
    def _():
        zero = jnp.zeros((edge_rows, cols, c_out), BF16)
        for slot in range(plan.n_slots):
            dbuf[slot, :edge_rows] = zero
            dbuf[slot, edge_rows + plan.height:] = zero
        pad[:, :EDGE, :] = jnp.zeros((rows, EDGE, c_out), F32)
        pad[:, EDGE + cols:, :] = jnp.zeros((rows, EDGE, c_out), F32)
        gpt[...] = jnp.zeros_like(gpt)
        gc[...] = jnp.zeros_like(gc)
        sdy[...] = jnp.zeros_like(sdy)
        total = jnp.zeros((1, c_in), F32)
        for j in range(n):
            extra = all_ref[j].astype(F32)
            total = total + ((extra[2:3] + extra[1:2]) + extra[0:1])
        mean_in = (total / plan.total).astype(BF16)
        mean[...] = jnp.broadcast_to(mean_in.astype(F32), (16, c_in))
        pact[...] = nn(mean[...].astype(BF16), w28_ref[0])

    @pl.when(step < n)
    def _():
        block = step
        for k in range(4):
            part = slice(k * c_out, (k + 1) * c_out)
            if k in plan.shifted:
                at = plan.shifted.index(k)
                r = RATE * k
                pre = mid_refs[at]
                for i in range(rows):
                    h = block * rows + i
                    line = pre[i]
                    for side, src in ((0, h - r), (1, h + r)):
                        ok = jnp.logical_and(src >= 0, src < plan.height)
                        ref = s_refs[(2 * at + side) * rows + i]
                        line = line + jnp.where(ok, ref[...], 0.0)
                    cat5[i * cols:(i + 1) * cols, part] = jnp.maximum(line, 0.0).astype(BF16)
            else:
                at = plan.direct.index(k)
                cat5[:, part] = cat_ref[:, at * c_out:(at + 1) * c_out]
        pool_act = jnp.maximum(pact[0:1, :], 0.0).astype(BF16)
        cat5[:, 4 * c_out:] = jnp.broadcast_to(pool_act, (pix, c_out))
        y_pre = nn(cat5[...], wproj_ref[...])
        y_act = jnp.maximum(y_pre, 0.0).astype(BF16)
        logits = nn(y_act, wcls_ref[...])
        lane = lax.broadcasted_iota(jnp.int32, (pix, 128), 1)
        live = lane < plan.classes
        expo = jnp.where(live, jnp.exp(logits), 0.0)
        prob = expo / jnp.sum(expo, axis=1, keepdims=True)
        names = aux_ref[3:4, :512].astype(F32)
        label = jnp.broadcast_to(names, (128, 512)).T[:pix]
        onehot = jnp.where(label == lane.astype(F32), 1.0, 0.0)
        weight = jnp.zeros((pix, 128), F32)
        for c in range(plan.classes):
            weight = jnp.where(label == float(c), cw_ref[c], weight)
        d_logits = jnp.where(
            live, (prob - onehot) * weight * (LOSS_SCALE / plan.total), 0.0
        ).astype(BF16)
        d_y = jnp.where(y_pre > 0, nt(d_logits, wcls_ref[...]), 0.0).astype(BF16)
        sdy[0:1, :] += jnp.sum(d_y.astype(F32), axis=0, keepdims=True)
        gpt[...] += nn(nt(identity(c_out), d_y).astype(BF16), cat5[...])
        gc[...] += nn(nt(identity(128), d_logits).astype(BF16), y_act)
        for k in range(4):
            want = [tab[flags + n + 3 * k + b] for b in range(3)]
            part = slice(k * c_out, (k + 1) * c_out)

            @pl.when((want[0] >= 0) | (want[1] >= 0) | (want[2] >= 0))
            def _(k=k, want=want, part=part):
                d_cat = nt(d_y, wproj_ref[part, :])
                d_k = jnp.where(cat5[:, part] > 0, d_cat, 0.0).astype(BF16)
                d_k = d_k.reshape(rows, cols, c_out)
                if k > 0:
                    pad[:, EDGE:EDGE + cols, :] = d_k.astype(F32)
                at = pl.ds(block * rows + edge_rows, rows)
                for b in range(3):
                    if k == 0 and b != 1:
                        continue

                    @pl.when(want[b] >= 0)
                    def _(b=b):
                        slot = jnp.maximum(want[b], 0)
                        if b == 1:
                            dbuf[slot, at] = d_k
                        else:
                            first = EDGE + (1 - b) * RATE * k
                            dbuf[slot, at] = pad[:, first:first + cols, :].astype(BF16)

    @pl.when(step == n - 1)
    def _():
        pool = wproj_ref[4 * c_out:, :]
        rest = sdy[...]
        total = jnp.zeros(sdy.shape, F32)
        for _i in range(3):
            head = rest.astype(BF16)
            total = total + nt(head, pool)
            rest = rest - head.astype(F32)
        spool[...] = jnp.where(pact[...] > 0, jnp.broadcast_to(total[0:1, :], total.shape), 0.0)
        for c in range(5):
            gp[c * c_out:(c + 1) * c_out, :] = gpt[:, c * c_out:(c + 1) * c_out].T
        index = tab[flags + n + 12]
        first = pl.multiple_of(index * plan.proj_rows, plan.proj_rows)
        p_out[...] = finish(gp[pl.ds(first, plan.proj_rows), :], prev_p[...] if last else None)
        gp[:c_out, :128] = gc[...].T
        first = pl.multiple_of(index * plan.cls_rows, plan.cls_rows)
        c_ref_out[...] = finish(
            gp[pl.ds(first, plan.cls_rows), :128], prev_c[...] if last else None
        )

    def out_copy(part, slot, t):
        row = tab[(part * depth + t) * 6 + 5] * unit_rows
        return pltpu.make_async_copy(
            stage.at[slot, t],
            g_out.at[pl.ds(pl.multiple_of(row, unit_rows), unit_rows)],
            sems.at[slot, t],
        )

    @pl.when(step >= n)
    def _():
        part = step - n
        parity = lax.rem(part, 2)

        def one(t, _):
            base = (part * depth + t) * 6
            slot, move, low, high = tab[base], tab[base + 1], tab[base + 2], tab[base + 3]
            kind = tab[base + 4]

            def term(j):
                first = j * rows - move + edge_rows
                return nn(xt_ref[j], dbuf[slot, pl.ds(first, rows)].reshape(pix, c_out))

            whole = jnp.logical_and(low == 0, high == n)

            @pl.when(whole)
            def _():
                total = term(0)
                for j in range(1, n):
                    total = total + term(j)
                acc[...] = total

            @pl.when(jnp.logical_not(whole))
            def _():
                acc[...] = jnp.zeros_like(acc)

                def add(j, _):
                    acc[...] += term(j)
                    return 0

                lax.fori_loop(low, high, add, 0)

            @pl.when(kind == 1)
            def _():
                first = pl.multiple_of(part * unit_rows, unit_rows)
                row = mean[0:1, pl.ds(first, unit_rows)]
                column = jnp.broadcast_to(row, (128, unit_rows)).T
                for c in range(c_out // 128):
                    lanes = slice(c * 128, (c + 1) * 128)
                    acc[:, lanes] = column * spool[0:1, lanes]

            if last:
                stage[parity, t] = finish(acc[...], prev_g[t])
                out_copy(part, parity, t).start()
            else:
                g_out[t] = finish(acc[...], None)
            return 0

        lax.fori_loop(0, tab[flags + part], one, 0)

        if last:
            def drain(which, slot):
                def one(t, _):
                    out_copy(which, slot, t).wait()
                    return 0
                lax.fori_loop(0, tab[flags + which], one, 0)

            @pl.when(part > 0)
            def _():
                drain(part - 1, 1 - parity)

            @pl.when(part == n - 1)
            def _():
                drain(part, parity)


def run_field(plan, field, tab, state, w_in, w_proj, wcls, cw, prev):
    n, rows, cols, pix = plan.n, plan.rows, plan.cols, plan.pix
    c_in, c_out, n_sh = plan.c_in, plan.c_out, plan.n_sh
    unit_rows, depth = plan.unit_rows, plan.depth
    last = prev is not None
    xt, cat, s, aux = state

    def blk(i):
        return jnp.minimum(i, n - 1)

    def part(i):
        return jnp.maximum(i - n, 0)

    in_specs = [
        pl.BlockSpec(
            (None, None, pix, len(plan.direct) * c_out), lambda i, t: (field, blk(i), 0, 0)
        ),
    ]
    operands = [cat]
    for at in range(n_sh):
        in_specs.append(pl.BlockSpec(
            (None, None, rows, cols, c_out),
            lambda i, t, at=at: (3 * at + 1, field, blk(i), 0, 0),
        ))
        operands.append(s)
    for at, k in enumerate(plan.shifted):
        for side in range(2):
            move = (2 * side - 1) * RATE * k
            for row in range(rows):
                def index(i, t, at=at, side=side, move=move, row=row):
                    h = jnp.clip(blk(i) * rows + row + move, 0, plan.height - 1)
                    return (3 * at + 2 * side, field, h, 0, 0)
                in_specs.append(pl.BlockSpec((None, None, None, cols, c_out), index))
                operands.append(s)
    in_specs += [
        pl.BlockSpec((None, None, EXTRA, c_in), lambda i, t: (field, blk(i), 0, 0)),
        pl.BlockSpec((None, n, EXTRA, c_in), lambda i, t: (field, 0, 0, 0)),
        pl.BlockSpec((1, c_in, c_out), lambda i, t: (28, 0, 0)),
        pl.BlockSpec((5 * c_out, c_out), lambda i, t: (0, 0)),
        pl.BlockSpec((c_out, 128), lambda i, t: (0, 0)),
        pl.BlockSpec(memory_space=pltpu.SMEM),
        pl.BlockSpec((None, n, unit_rows, pix), lambda i, t: (field, 0, part(i), 0)),
    ]
    operands += [aux, aux, w_in, w_proj, wcls, cw, xt]
    kind = F32 if last else BF16
    inner = pl.BlockSpec((None, depth, unit_rows, c_out), lambda i, t: (part(i), 0, 0, 0))
    small = [
        pl.BlockSpec((plan.proj_rows, c_out), lambda i, t: (0, 0)),
        pl.BlockSpec((plan.cls_rows, 128), lambda i, t: (0, 0)),
    ]
    if last:
        in_specs += [inner] + small
        operands += list(prev)
        main_spec = pl.BlockSpec(memory_space=pl.ANY)
        main_shape = jax.ShapeDtypeStruct((plan.units * unit_rows, c_out), F32)
    else:
        main_spec = inner
        main_shape = jax.ShapeDtypeStruct((n, depth, unit_rows, c_out), BF16)
    return pl.pallas_call(
        functools.partial(field_kernel, plan, last),
        grid_spec=pltpu.PrefetchScalarGridSpec(
            num_scalar_prefetch=1,
            grid=(2 * n,),
            in_specs=in_specs,
            out_specs=[main_spec] + small,
            scratch_shapes=[
                pltpu.VMEM((plan.n_slots, plan.height + 2 * (rows - 1), cols, c_out), BF16),
                pltpu.VMEM((rows, cols + 2 * EDGE, c_out), F32),
                pltpu.VMEM((16, c_in), F32),
                pltpu.VMEM((c_out, 5 * c_out), F32),
                pltpu.VMEM((5 * c_out, c_out), F32),
                pltpu.VMEM((128, c_out), F32),
                pltpu.VMEM((16, c_out), F32),
                pltpu.VMEM((16, c_out), F32),
                pltpu.VMEM((16, c_out), F32),
                pltpu.VMEM((pix, 5 * c_out), BF16),
                pltpu.VMEM((unit_rows, c_out), F32),
                pltpu.VMEM((2, depth if last else 1, unit_rows, c_out), F32),
                pltpu.SemaphoreType.DMA((2, depth)),
            ],
        ),
        out_shape=[
            main_shape,
            jax.ShapeDtypeStruct((plan.proj_rows, c_out), kind),
            jax.ShapeDtypeStruct((plan.cls_rows, 128), kind),
        ],
        compiler_params=pltpu.CompilerParams(
            dimension_semantics=("arbitrary",), vmem_limit_bytes=FIELD_VMEM
        ),
        cost_estimate=pl.CostEstimate(
            flops=10_000_000_000, bytes_accessed=90_000_000, transcendentals=0
        ),
        name="field_grads",
    )(tab, *operands)


def after(value, *others):
    return lax.optimization_barrier((value, *others))[0]


def per_device(plan, features, labels, w_in, w_proj, w_cls, class_weight, matching):
    n, reps, rows, pix, c_in = plan.n, plan.reps, plan.rows, plan.pix, plan.c_in
    names = jnp.pad(labels[0].reshape(1, pix).astype(F32), ((0, 0), (0, c_in - pix)))
    x = pl.pallas_call(
        functools.partial(pack_kernel, pix),
        out_shape=jax.ShapeDtypeStruct((pix + EXTRA, c_in), BF16),
        name="pack",
    )(features[0].reshape(pix, c_in), names)
    here = lax.axis_index("space")
    n_bits = reps.bit_length() - 1
    bits = [jnp.bitwise_and(jnp.right_shift(matching[0], b), 1) == 1 for b in range(n_bits)]
    top = jnp.int32(0)
    for b in range(n_bits):
        top = jnp.where(bits[b], n_bits - 1 - b, top)
    tab = jnp.asarray(plan.tables)[here]
    wcls = jnp.pad(w_cls, ((0, 0), (0, 128 - plan.classes)))

    def along(value, way, step):
        pairs = [
            (i, i + way) for i in range(n)
            if 0 <= i + way < n and 0 <= i - way * (step - 1) < n
        ]
        return lax.ppermute(value, "space", pairs)

    def hop(value, b):
        return lax.ppermute(value, "rep", [(r, r ^ (1 << b)) for r in range(reps)])

    order = np.array(
        [sorted(range(n), key=lambda j: (abs(j - s), j)) for s in range(n)], np.int32
    )
    blocks = jnp.asarray(order)[here]

    def arrival(q, ups, downs):
        value = None
        for s in range(n):
            j = int(order[s, q])
            arrived = ups[s - j] if j < s else downs[j - s]
            value = arrived if value is None else jnp.where(here == s, arrived, value)
        return value

    common = (w_in, w_proj, wcls, class_weight)
    ups, downs, items = [x], [x], [x]
    values, moves = {}, {q: [] for q in range(n)}
    state, grads = None, None

    def pair(q):
        return (moves[q], (top, blocks[q], 1))

    for t in range(1, n + n_bits - 1):
        q = t - 1
        if t < n:
            ups.append(along(ups[-1], 1, t))
            downs.append(along(downs[-1], -1, t))
        tie = []
        if q < n:
            moved = hop(items[q], 0)
            moves[q].insert(0, moved)
            values[q] = jnp.where(bits[0], moved, items[q])
            tie = [values[q]]
        sent = []
        for b in range(1, n_bits):
            if 0 <= t - b < n:
                moves[t - b].insert(0, hop(values[t - b], b))
                sent.append((t - b, b))
        if q < n:
            slots = [([after(items[q], *tie)], (0, blocks[q], 0))]
            if t >= n_bits:
                slots.append(pair(t - n_bits))
            state = run_blocks(plan, slots, w_in, state)
        if q == n:
            grads = tuple(run_field(plan, 0, tab, state, *common, None))
        for at, b in sent:
            if b + 1 < n_bits:
                values[at] = jnp.where(bits[b], moves[at][0], values[at])
        if t < n:
            items.append(arrival(t, ups, downs))
        live = (ups, downs, items, values, moves, state, grads)
        ups, downs, items, values, moves, state, grads = lax.optimization_barrier(live)
    if grads is None:
        grads = tuple(run_field(plan, 0, tab, state, *common, None))
        state, grads = lax.optimization_barrier((state, grads))
    done = max(0, n - n_bits + 1)
    state = run_blocks(plan, [pair(q) for q in range(done, n)], w_in, state)
    avg_in, avg_proj, avg_cls = run_field(plan, 1, tab, state, *common, grads)
    return avg_in[None], avg_proj[None], avg_cls[None, :, :plan.classes]


def solution(mesh):
    n, reps = mesh.shape["space"], mesh.shape["rep"]

    def build(features, labels, w_in, w_proj, w_cls, class_weight, matching):
        _, rows, cols, c_in = features.shape
        plan = Plan(n, reps, rows // n, cols, c_in, w_proj.shape[1], w_cls.shape[1])
        return jax.shard_map(
            functools.partial(per_device, plan),
            mesh=mesh,
            in_specs=(P("rep", "space", None, None), P("rep", "space", None), P(), P(), P(), P(), P()),
            out_specs=(P("rep", "space", None), P("rep", "space", None), P("rep", "space", None)),
            check_vma=False,
        )(features, labels, w_in, w_proj, w_cls, class_weight, matching)

    return build
```

profile of v0, /device:TPU:0, one launch (start us, length us, event | category | flops | bytes accessed | tf_op | source)
XLA Modules:
  0.0 284.9 jit_solution(4588518000023749013)
XLA Ops:
  2.0 2.3 pack.1.refs_0_
  4.8 5.5 %collective-permute-start = (bf16[496,1024]{1,0:T(8,128)(2,1)}, bf16[496,1024]{1,0:T(8,128)(2,1)}, u32[]{:S(2)}, u32[]{:S(2)}) collective-permute-start(bf16[496,1024]{1,0:T(8,128)(2,1)} %pack.1.refs_0_), channel_id=1, source_target_pairs={{0,8},{8,16},{16,24},{1,9},{9,17},{17,25},{2,10},{10,18},{18,26},{... | collective-permute-start | bytes 3047432 | tf_op jit(solution)/shard_map/ppermute | solution.py:616
  10.3 1.3 collective-permute-start.1
  12.9 1.3 broadcast_select_fusion.3
  14.2 1.5 collective-permute-start.3
  17.0 1.4 fusion.1
  18.4 13.6 %collective-permute-done = bf16[496,1024]{1,0:T(8,128)(2,1)} collective-permute-done((bf16[496,1024]{1,0:T(8,128)(2,1)}, bf16[496,1024]{1,0:T(8,128)(2,1)}, u32[]{:S(2)}, u32[]{:S(2)}) %collective-permute-start) | collective-permute-done | bytes 1015840 | tf_op jit(solution)/shard_map/ppermute | solution.py:616
  32.0 5.1 %collective-permute-done.1 = bf16[496,1024]{1,0:T(8,128)(2,1)} collective-permute-done((bf16[496,1024]{1,0:T(8,128)(2,1)}, bf16[496,1024]{1,0:T(8,128)(2,1)}, u32[]{:S(2)}, u32[]{:S(2)}) %collective-permute-start.1) | collective-permute-done | bytes 1015840 | tf_op jit(solution)/shard_map/ppermute | solution.py:616
  37.0 1.6 select_select_fusion.1.refs_0_
  39.9 8.1 %block_forward.5 = (bf16[2,4,1024,480]{3,2,1,0:T(8,128)(2,1)S(1)}, bf16[2,4,480,768]{3,2,1,0:T(8,128)(2,1)S(1)}, f32[3,2,20,96,256]{4,3,2,1,0:T(8,128)}, bf16[2,4,16,1024]{3,2,1,0:T(8,128)(2,1)S(1)}) custom-call(s32[1,3]{1,0:T(1,128)S(1)} %get-tuple-element.184.meta, bf16[496,1024]{1,0:T(8,128)(2,1)S(1)} %copy-done.14, bf16[29,1024,256]{2,1,0:T(8,128)(2,1)} %refs_14_.3), custom_call_target="tpu_custom_call" | custom-call | flops 4026531840 | bytes 40000000 | tf_op jit(solution)/shard_map/block_forward/pallas_call | solution.py:253
  48.2 1.6 collective-permute-start.4
  49.9 1.3 collective-permute-start.5
  51.3 1.6 collective-permute-start.7
  52.8 1.5 collective-permute-start.8
  54.4 23.9 %collective-permute-done.5 = bf16[496,1024]{1,0:T(8,128)(2,1)} collective-permute-done((bf16[496,1024]{1,0:T(8,128)(2,1)}, bf16[496,1024]{1,0:T(8,128)(2,1)}, u32[]{:S(2)}, u32[]{:S(2)}) %collective-permute-start.5) | collective-permute-done | bytes 1015840 | tf_op jit(solution)/shard_map/ppermute | solution.py:616
  78.3 1.7 fusion.refs_0_
  80.0 8.1 %block_forward.6 = (bf16[2,4,1024,480]{3,2,1,0:T(8,128)(2,1)S(1)}, bf16[2,4,480,768]{3,2,1,0:T(8,128)(2,1)S(1)}, f32[3,2,20,96,256]{4,3,2,1,0:T(8,128)}, bf16[2,4,16,1024]{3,2,1,0:T(8,128)(2,1)S(1)}) custom-call(s32[1,3]{1,0:T(1,128)S(1)} %get-tuple-element.185.meta, ...), custom_call_target="tpu_custom_call", output_to_operand_aliasing={{0}: (3, {}), {1}: (4, {}), {2}: (5, {}), {3}: (6, {})} | custom-call | flops 4026531840 | bytes 40000000 | tf_op jit(solution)/shard_map/block_forward/pallas_call | solution.py:253
  88.1 3.2 %copy-done = bf16[2,4,1024,480]{3,2,1,0:T(8,128)(2,1)} copy-done((bf16[2,4,1024,480]{3,2,1,0:T(8,128)(2,1)}, bf16[2,4,1024,480]{3,2,1,0:T(8,128)(2,1)S(1)}, u32[]{:S(2)}) %copy-start) | copy-done | bytes 7864344
  91.3 2.6 copy-done.6
  96.0 1.3 collective-permute-start.10
  97.3 1.6 collective-permute-start.9
  99.0 1.7 fusion.3
  100.7 1.6 collective-permute-start.13
  102.3 1.3 broadcast_select_fusion.1
  103.6 1.6 collective-permute-start.12
  105.1 17.9 %collective-permute-done.10 = bf16[496,1024]{1,0:T(8,128)(2,1)} collective-permute-done((bf16[496,1024]{1,0:T(8,128)(2,1)}, bf16[496,1024]{1,0:T(8,128)(2,1)}, u32[]{:S(2)}, u32[]{:S(2)}) %collective-permute-start.10) | collective-permute-done | bytes 1015840 | tf_op jit(solution)/shard_map/ppermute | solution.py:616
  123.1 1.4 select_select_fusion.2.refs_0_
  124.5 3.4 %copy-done.1 = bf16[2,4,1024,480]{3,2,1,0:T(8,128)(2,1)S(1)} copy-done((bf16[2,4,1024,480]{3,2,1,0:T(8,128)(2,1)S(1)}, bf16[2,4,1024,480]{3,2,1,0:T(8,128)(2,1)}, u32[]{:S(2)}) %copy-start.1) | copy-done | bytes 7864344
  127.9 14.7 %block_forward.7 = (bf16[2,4,1024,480]{3,2,1,0:T(8,128)(2,1)S(1)}, bf16[2,4,480,768]{3,2,1,0:T(8,128)(2,1)S(1)}, f32[3,2,20,96,256]{4,3,2,1,0:T(8,128)}, bf16[2,4,16,1024]{3,2,1,0:T(8,128)(2,1)S(1)}) custom-call(s32[2,3]{1,0:T(2,128)S(1)} %pad_add_fusion.1.meta, ...), custom_call_target="tpu_custom_call", output_to_operand_aliasing={{0}: (6, {}), {1}: (7, {}), {2}: (8, {}), {3}: (9, {})} | custom-call | flops 8053063680 | bytes 60000000 | tf_op jit(solution)/shard_map/block_forward/pallas_call | solution.py:253
  142.6 3.2 %copy-done.2 = bf16[2,4,1024,480]{3,2,1,0:T(8,128)(2,1)} copy-done((bf16[2,4,1024,480]{3,2,1,0:T(8,128)(2,1)}, bf16[2,4,1024,480]{3,2,1,0:T(8,128)(2,1)S(1)}, u32[]{:S(2)}) %copy-start.2) | copy-done | bytes 7864344
  145.8 2.6 copy-done.7
  149.6 1.3 fusion.4
  151.0 1.3 collective-permute-done.14.refs_5_
  153.3 1.5 collective-permute-start.15
  156.9 1.5 collective-permute-start.16
  158.5 3.4 %copy-done.3 = bf16[2,4,1024,480]{3,2,1,0:T(8,128)(2,1)S(1)} copy-done((bf16[2,4,1024,480]{3,2,1,0:T(8,128)(2,1)S(1)}, bf16[2,4,1024,480]{3,2,1,0:T(8,128)(2,1)}, u32[]{:S(2)}) %copy-start.3) | copy-done | bytes 7864344
  161.8 2.7 copy-done.8
  169.4 14.6 %block_forward.8 = (bf16[2,4,1024,480]{3,2,1,0:T(8,128)(2,1)S(1)}, bf16[2,4,480,768]{3,2,1,0:T(8,128)(2,1)S(1)}, f32[3,2,20,96,256]{4,3,2,1,0:T(8,128)}, bf16[2,4,16,1024]{3,2,1,0:T(8,128)(2,1)S(1)}) custom-call(s32[2,3]{1,0:T(2,128)S(1)} %pad_add_fusion.2.meta, ...), custom_call_target="tpu_custom_call", output_to_operand_aliasing={{0}: (6, {}), {1}: (7, {}), {2}: (8, {}), {3}: (9, {})} | custom-call | flops 8053063680 | bytes 60000000 | tf_op jit(solution)/shard_map/block_forward/pallas_call | solution.py:253
  184.0 3.2 %copy-done.4 = bf16[2,4,1024,480]{3,2,1,0:T(8,128)(2,1)} copy-done((bf16[2,4,1024,480]{3,2,1,0:T(8,128)(2,1)}, bf16[2,4,1024,480]{3,2,1,0:T(8,128)(2,1)S(1)}, u32[]{:S(2)}) %copy-start.4) | copy-done | bytes 7864344
  187.1 2.6 copy-done.9
  191.3 31.2 %field_grads.2 = (bf16[4,8,256,256]{3,2,1,0:T(8,128)(2,1)S(1)}, bf16[320,256]{1,0:T(8,128)(2,1)S(1)}, bf16[64,128]{1,0:T(8,128)(2,1)S(1)}) custom-call(s32[209]{0:T(256)S(1)} %bitcast.37, bf16[2,4,480,768]{3,2,1,0:T(8,128)(2,1)} %copy-done.9, ...), custom_call_target="tpu_custom_call" | custom-call | flops 10000000000 | bytes 90000000 | tf_op jit(solution)/shard_map/field_grads/pallas_call | solution.py:552
  222.6 2.1 copy-done.15
  224.7 2.7 copy-done.10
  227.3 15.6 %block_forward.9 = (bf16[2,4,1024,480]{3,2,1,0:T(8,128)(2,1)S(1)}, bf16[2,4,480,768]{3,2,1,0:T(8,128)(2,1)S(1)}, f32[3,2,20,96,256]{4,3,2,1,0:T(8,128)}, bf16[2,4,16,1024]{3,2,1,0:T(8,128)(2,1)S(1)}) custom-call(s32[2,3]{1,0:T(2,128)S(1)} %pad_add_fusion.meta, ...), custom_call_target="tpu_custom_call", output_to_operand_aliasing={{0}: (8, {}), {1}: (9, {}), {2}: (10, {}), {3}: (11, {})} | custom-call | flops 8053063680 | bytes 60000000 | tf_op jit(solution)/shard_map/block_forward/pallas_call | solution.py:253
  242.9 3.2 %copy-done.5 = bf16[2,4,1024,480]{3,2,1,0:T(8,128)(2,1)} copy-done((bf16[2,4,1024,480]{3,2,1,0:T(8,128)(2,1)}, bf16[2,4,1024,480]{3,2,1,0:T(8,128)(2,1)S(1)}, u32[]{:S(2)}) %copy-start.5) | copy-done | bytes 7864344
  246.1 2.5 copy-done.11
  248.7 2.2 copy-done.16
  250.9 33.4 %field_grads.3 = (f32[7424,256]{1,0:T(8,128)}, f32[320,256]{1,0:T(8,128)}, f32[64,128]{1,0:T(8,128)S(1)}) custom-call(s32[209]{0:T(256)S(1)} %bitcast.38, bf16[2,4,480,768]{3,2,1,0:T(8,128)(2,1)} %copy-done.11, f32[3,2,20,96,256]{4,3,2,1,0:T(8,128)} %get-tuple-element.168.refs_1_.refs_2_.refs_3_.refs_4_.refs_5_.refs_6_.refs_7_.refs_8_.refs_9_.refs_10_.refs_11_, ...), custom_call_target="tpu_custom_call" | custom-call | flops 10000000000 | bytes 90000000 | tf_op jit(solution)/shard_map/field_grads/pallas_call | solution.py:552
  (104 shorter events, 18.4 us)
Async XLA Ops:
  4.3 8.5 %collective-permute-start.2 = (bf16[496,1024]{1,0:T(8,128)(2,1)}, bf16[496,1024]{1,0:T(8,128)(2,1)S(1)}, u32[]{:S(2)}, u32[]{:S(2)}) collective-permute-start(bf16[496,1024]{1,0:T(8,128)(2,1)} %pack.1.refs_0_), channel_id=1, source_target_pairs={{0,1},{1,0},{2,3},{3,2},{4,5},{5,4},{6,7},{7,6},{8,9},{9,8},{10,11... | collective-permute-start | bytes 3047432 | tf_op jit(solution)/shard_map/ppermute | solution.py:619
  4.8 27.2 %collective-permute-start = (bf16[496,1024]{1,0:T(8,128)(2,1)}, bf16[496,1024]{1,0:T(8,128)(2,1)}, u32[]{:S(2)}, u32[]{:S(2)}) collective-permute-start(bf16[496,1024]{1,0:T(8,128)(2,1)} %pack.1.refs_0_), channel_id=1, source_target_pairs={{0,8},{8,16},{16,24},{1,9},{9,17},{17,25},{2,10},{10,18},{18,26},{... | collective-permute-start | bytes 3047432 | tf_op jit(solution)/shard_map/ppermute | solution.py:616
  10.3 26.8 %collective-permute-start.1 = (bf16[496,1024]{1,0:T(8,128)(2,1)}, bf16[496,1024]{1,0:T(8,128)(2,1)}, u32[]{:S(2)}, u32[]{:S(2)}) collective-permute-start(bf16[496,1024]{1,0:T(8,128)(2,1)} %pack.1.refs_0_), channel_id=1, source_target_pairs={{8,0},{16,8},{24,16},{9,1},{17,9},{25,17},{10,2},{18,10},{26,18},{... | collective-permute-start | bytes 3047432 | tf_op jit(solution)/shard_map/ppermute | solution.py:616
  12.9 35.1 %copy-start.17 = (bf16[496,1024]{1,0:T(8,128)(2,1)}, bf16[496,1024]{1,0:T(8,128)(2,1)S(1)}, u32[]{:S(2)}) copy-start(bf16[496,1024]{1,0:T(8,128)(2,1)S(1)} %collective-permute-done.2.refs_3_) | copy-start | bytes 3047428
  14.2 33.8 %collective-permute-start.3 = (bf16[496,1024]{1,0:T(8,128)(2,1)}, bf16[496,1024]{1,0:T(8,128)(2,1)S(1)}, u32[]{:S(2)}, u32[]{:S(2)}) collective-permute-start(bf16[496,1024]{1,0:T(8,128)(2,1)} %broadcast_select_fusion.3), channel_id=1, source_target_pairs={{0,2},{1,3},{2,0},{3,1},{4,6},{5,7},{6,4},{7,5},{8,10},{9,11},{10,... | collective-permute-start | bytes 3047432 | tf_op jit(solution)/shard_map/ppermute | solution.py:619
  48.0 6.4 %copy-start.23 = (bf16[496,1024]{1,0:T(8,128)(2,1)}, bf16[496,1024]{1,0:T(8,128)(2,1)S(1)}, u32[]{:S(2)}) copy-start(bf16[496,1024]{1,0:T(8,128)(2,1)S(1)} %collective-permute-done.3.refs_2_) | copy-start | bytes 3047428
  48.2 3.0 %collective-permute-start.6 = (bf16[496,1024]{1,0:T(8,128)(2,1)S(1)}, bf16[496,1024]{1,0:T(8,128)(2,1)S(1)}, u32[]{:S(2)}, u32[]{:S(2)}) collective-permute-start(bf16[496,1024]{1,0:T(8,128)(2,1)S(1)} %select_select_fusion.1.refs_0_), channel_id=1, source_target_pairs={{0,1},{1,0},{2,3},{3,2},{4,5},{5,4},{6,7},{7,6},{8,9},{9,8},{10,11... | collective-permute-start | bytes 3047432 | tf_op jit(solution)/shard_map/ppermute | solution.py:619
  48.2 6.1 %collective-permute-start.4 = (bf16[496,1024]{1,0:T(8,128)(2,1)}, bf16[496,1024]{1,0:T(8,128)(2,1)}, u32[]{:S(2)}, u32[]{:S(2)}) collective-permute-start(bf16[496,1024]{1,0:T(8,128)(2,1)} %collective-permute-done), channel_id=1, source_target_pairs={{8,16},{16,24},{9,17},{17,25},{10,18},{18,26},{11,19},{19,27},{12,... | collective-permute-start | bytes 3047432 | tf_op jit(solution)/shard_map/ppermute | solution.py:616
  49.9 28.5 %collective-permute-start.5 = (bf16[496,1024]{1,0:T(8,128)(2,1)}, bf16[496,1024]{1,0:T(8,128)(2,1)}, u32[]{:S(2)}, u32[]{:S(2)}) collective-permute-start(bf16[496,1024]{1,0:T(8,128)(2,1)} %collective-permute-done.1), channel_id=1, source_target_pairs={{8,0},{16,8},{9,1},{17,9},{10,2},{18,10},{11,3},{19,11},{12,4},{20... | collective-permute-start | bytes 3047432 | tf_op jit(solution)/shard_map/ppermute | solution.py:616
  51.2 37.0 %copy-start.19 = (bf16[496,1024]{1,0:T(8,128)(2,1)}, bf16[496,1024]{1,0:T(8,128)(2,1)S(1)}, u32[]{:S(2)}) copy-start(bf16[496,1024]{1,0:T(8,128)(2,1)S(1)} %collective-permute-done.6.refs_3_) | copy-start | bytes 3047428
  51.3 42.6 %collective-permute-start.7 = (bf16[496,1024]{1,0:T(8,128)(2,1)S(1)}, bf16[496,1024]{1,0:T(8,128)(2,1)S(1)}, u32[]{:S(2)}, u32[]{:S(2)}) collective-permute-start(bf16[496,1024]{1,0:T(8,128)(2,1)S(1)} %broadcast_select_fusion.2), channel_id=1, source_target_pairs={{0,2},{1,3},{2,0},{3,1},{4,6},{5,7},{6,4},{7,5},{8,10},{9,11},{10,... | collective-permute-start | bytes 3047432 | tf_op jit(solution)/shard_map/ppermute | solution.py:619
  52.8 42.1 %collective-permute-start.8 = (bf16[496,1024]{1,0:T(8,128)(2,1)S(1)}, bf16[496,1024]{1,0:T(8,128)(2,1)S(1)}, u32[]{:S(2)}, u32[]{:S(2)}) collective-permute-start(bf16[496,1024]{1,0:T(8,128)(2,1)S(1)} %broadcast_select_fusion.7), channel_id=1, source_target_pairs={{0,4},{1,5},{2,6},{3,7},{4,0},{5,1},{6,2},{7,3},{8,12},{9,13},{10,... | collective-permute-start | bytes 3047432 | tf_op jit(solution)/shard_map/ppermute | solution.py:619
  80.0 18.9 %copy-start.34 = (s32[8]{0:T(128)S(1)}, s32[8]{0:T(128)}, u32[]{:S(2)}) copy-start(s32[8]{0:T(128)} %param.15) | copy-start | bytes 100
  88.1 3.2 %copy-start = (bf16[2,4,1024,480]{3,2,1,0:T(8,128)(2,1)}, bf16[2,4,1024,480]{3,2,1,0:T(8,128)(2,1)S(1)}, u32[]{:S(2)}) copy-start(bf16[2,4,1024,480]{3,2,1,0:T(8,128)(2,1)S(1)} %get-tuple-element.120.refs_5_) | copy-start | bytes 23592964
  91.3 2.6 copy-start.6
  93.9 30.6 %slice-start.2 = ((s8[5898240]{0:T(1024)(128)(4,1)}), s8[1703936]{0:T(1024)(128)(4,1)S(1)}, s32[]{:S(2)}) async-start(s8[5898240]{0:T(1024)(128)(4,1)} %bitcast.35), calls=%async_computation.2 | async-start | bytes 3407872
  96.0 6.3 %collective-permute-start.11 = (bf16[496,1024]{1,0:T(8,128)(2,1)S(1)}, bf16[496,1024]{1,0:T(8,128)(2,1)}, u32[]{:S(2)}, u32[]{:S(2)}) collective-permute-start(bf16[496,1024]{1,0:T(8,128)(2,1)S(1)} %fusion.refs_0_), channel_id=1, source_target_pairs={{0,1},{1,0},{2,3},{3,2},{4,5},{5,4},{6,7},{7,6},{8,9},{9,8},{10,11... | collective-permute-start | bytes 3047432 | tf_op jit(solution)/shard_map/ppermute | solution.py:619
  96.0 27.1 %collective-permute-start.10 = (bf16[496,1024]{1,0:T(8,128)(2,1)}, bf16[496,1024]{1,0:T(8,128)(2,1)}, u32[]{:S(2)}, u32[]{:S(2)}) collective-permute-start(bf16[496,1024]{1,0:T(8,128)(2,1)} %collective-permute-done.5), channel_id=1, source_target_pairs={{8,0},{9,1},{10,2},{11,3},{12,4},{13,5},{14,6},{15,7}} | collective-permute-start | bytes 3047432 | tf_op jit(solution)/shard_map/ppermute | solution.py:616
  97.3 25.8 %collective-permute-start.9 = (bf16[496,1024]{1,0:T(8,128)(2,1)}, bf16[496,1024]{1,0:T(8,128)(2,1)}, u32[]{:S(2)}, u32[]{:S(2)}) collective-permute-start(bf16[496,1024]{1,0:T(8,128)(2,1)} %collective-permute-done.4), channel_id=1, source_target_pairs={{16,24},{17,25},{18,26},{19,27},{20,28},{21,29},{22,30},{23,31}} | collective-permute-start | bytes 3047432 | tf_op jit(solution)/shard_map/ppermute | solution.py:616
  99.0 25.5 %copy-start.18 = (bf16[496,1024]{1,0:T(8,128)(2,1)S(1)}, bf16[496,1024]{1,0:T(8,128)(2,1)}, u32[]{:S(2)}) copy-start(bf16[496,1024]{1,0:T(8,128)(2,1)} %copy-done.17) | copy-start | bytes 3047428
  99.0 25.5 %copy-start.24 = (bf16[496,1024]{1,0:T(8,128)(2,1)S(1)}, bf16[496,1024]{1,0:T(8,128)(2,1)}, u32[]{:S(2)}) copy-start(bf16[496,1024]{1,0:T(8,128)(2,1)} %copy-done.23) | copy-start | bytes 3047428
  99.0 25.5 %copy-start.29 = (bf16[496,1024]{1,0:T(8,128)(2,1)S(1)}, bf16[496,1024]{1,0:T(8,128)(2,1)}, u32[]{:S(2)}) copy-start(bf16[496,1024]{1,0:T(8,128)(2,1)} %copy-done.28) | copy-start | bytes 3047428
  100.7 23.8 %slice-start.3 = ((s8[5898240]{0:T(1024)(128)(4,1)}), s8[4194304]{0:T(1024)(128)(4,1)S(1)}, s32[]{:S(2)}) async-start(s8[5898240]{0:T(1024)(128)(4,1)} %bitcast.35), calls=%async_computation.3 | async-start | bytes 8388608
  100.7 49.0 %collective-permute-start.13 = (bf16[496,1024]{1,0:T(8,128)(2,1)}, bf16[496,1024]{1,0:T(8,128)(2,1)S(1)}, u32[]{:S(2)}, u32[]{:S(2)}) collective-permute-start(bf16[496,1024]{1,0:T(8,128)(2,1)} %broadcast_select_fusion.6), channel_id=1, source_target_pairs={{0,4},{1,5},{2,6},{3,7},{4,0},{5,1},{6,2},{7,3},{8,12},{9,13},{10,... | collective-permute-start | bytes 3047432 | tf_op jit(solution)/shard_map/ppermute | solution.py:619
  103.6 44.8 %collective-permute-start.12 = (bf16[496,1024]{1,0:T(8,128)(2,1)S(1)}, bf16[496,1024]{1,0:T(8,128)(2,1)S(1)}, u32[]{:S(2)}, u32[]{:S(2)}) collective-permute-start(bf16[496,1024]{1,0:T(8,128)(2,1)S(1)} %broadcast_select_fusion.1), channel_id=1, source_target_pairs={{0,2},{1,3},{2,0},{3,1},{4,6},{5,7},{6,4},{7,5},{8,10},{9,11},{10,... | collective-permute-start | bytes 3047432 | tf_op jit(solution)/shard_map/ppermute | solution.py:619
  124.5 3.4 %copy-start.1 = (bf16[2,4,1024,480]{3,2,1,0:T(8,128)(2,1)S(1)}, bf16[2,4,1024,480]{3,2,1,0:T(8,128)(2,1)}, u32[]{:S(2)}) copy-start(bf16[2,4,1024,480]{3,2,1,0:T(8,128)(2,1)} %copy-done) | copy-start | bytes 23592964
  127.9 24.4 %copy-start.12 = (bf16[496,1024]{1,0:T(8,128)(2,1)}, bf16[496,1024]{1,0:T(8,128)(2,1)S(1)}, u32[]{:S(2)}) copy-start(bf16[496,1024]{1,0:T(8,128)(2,1)S(1)} %select_select_fusion.2.refs_0_) | copy-start | bytes 3047428
  127.9 27.6 %copy-start.33 = (bf16[256,3]{0,1:T(4,128)(2,1)S(1)}, bf16[256,3]{0,1:T(4,128)(2,1)}, u32[]{:S(2)}) copy-start(bf16[256,3]{0,1:T(4,128)(2,1)} %param.13) | copy-start | bytes 4612
  142.6 3.2 %copy-start.2 = (bf16[2,4,1024,480]{3,2,1,0:T(8,128)(2,1)}, bf16[2,4,1024,480]{3,2,1,0:T(8,128)(2,1)S(1)}, u32[]{:S(2)}) copy-start(bf16[2,4,1024,480]{3,2,1,0:T(8,128)(2,1)S(1)} %get-tuple-element.136.refs_5_) | copy-start | bytes 23592964
  145.8 2.6 copy-start.7
  148.4 5.0 %copy-start.25 = (bf16[496,1024]{1,0:T(8,128)(2,1)}, bf16[496,1024]{1,0:T(8,128)(2,1)S(1)}, u32[]{:S(2)}) copy-start(bf16[496,1024]{1,0:T(8,128)(2,1)S(1)} %collective-permute-done.12.refs_1_) | copy-start | bytes 3047428
  149.6 5.2 %copy-start.30 = (bf16[496,1024]{1,0:T(8,128)(2,1)}, bf16[496,1024]{1,0:T(8,128)(2,1)S(1)}, u32[]{:S(2)}) copy-start(bf16[496,1024]{1,0:T(8,128)(2,1)S(1)} %collective-permute-done.13.refs_1_) | copy-start | bytes 3047428
  149.6 2.6 collective-permute-start.14
  153.3 36.4 %collective-permute-start.15 = (bf16[496,1024]{1,0:T(8,128)(2,1)}, bf16[496,1024]{1,0:T(8,128)(2,1)S(1)}, u32[]{:S(2)}, u32[]{:S(2)}) collective-permute-start(bf16[496,1024]{1,0:T(8,128)(2,1)} %broadcast_select_fusion), channel_id=1, source_target_pairs={{0,2},{1,3},{2,0},{3,1},{4,6},{5,7},{6,4},{7,5},{8,10},{9,11},{10,... | collective-permute-start | bytes 3047432 | tf_op jit(solution)/shard_map/ppermute | solution.py:619
  156.9 33.9 %collective-permute-start.16 = (bf16[496,1024]{1,0:T(8,128)(2,1)}, bf16[496,1024]{1,0:T(8,128)(2,1)S(1)}, u32[]{:S(2)}, u32[]{:S(2)}) collective-permute-start(bf16[496,1024]{1,0:T(8,128)(2,1)} %broadcast_select_fusion.5), channel_id=1, source_target_pairs={{0,4},{1,5},{2,6},{3,7},{4,0},{5,1},{6,2},{7,3},{8,12},{9,13},{10,... | collective-permute-start | bytes 3047432 | tf_op jit(solution)/shard_map/ppermute | solution.py:619
  158.5 3.4 %copy-start.3 = (bf16[2,4,1024,480]{3,2,1,0:T(8,128)(2,1)S(1)}, bf16[2,4,1024,480]{3,2,1,0:T(8,128)(2,1)}, u32[]{:S(2)}) copy-start(bf16[2,4,1024,480]{3,2,1,0:T(8,128)(2,1)} %copy-done.2) | copy-start | bytes 23592964
  161.8 2.7 copy-start.8
  169.4 21.9 %copy-start.27 = (bf16[1280,256]{1,0:T(8,128)(2,1)S(1)}, bf16[1280,256]{1,0:T(8,128)(2,1)}, u32[]{:S(2)}) copy-start(bf16[1280,256]{1,0:T(8,128)(2,1)} %refs_15_.3) | copy-start | bytes 1966084
  169.4 21.9 %copy-start.32 = (f32[3]{0:T(128)S(1)}, f32[3]{0:T(128)}, u32[]{:S(2)}) copy-start(f32[3]{0:T(128)} %refs_17_.3) | copy-start | bytes 40
  183.9 3.2 %copy-start.4 = (bf16[2,4,1024,480]{3,2,1,0:T(8,128)(2,1)}, bf16[2,4,1024,480]{3,2,1,0:T(8,128)(2,1)S(1)}, u32[]{:S(2)}) copy-start(bf16[2,4,1024,480]{3,2,1,0:T(8,128)(2,1)S(1)} %get-tuple-element.163.refs_18_.refs_7_) | copy-start | bytes 23592964
  187.1 2.6 copy-start.9
  189.7 34.9 %slice-start = ((s8[8388608]{0:T(1024)(128)(4,1)}), s8[4194304]{0:T(1024)(128)(4,1)S(1)}, s32[]{:S(2)}) async-start(s8[8388608]{0:T(1024)(128)(4,1)} %bitcast.33), calls=%async_computation | async-start | bytes 8388608
  190.8 33.9 %collective-permute-start.17 = (bf16[496,1024]{1,0:T(8,128)(2,1)}, bf16[496,1024]{1,0:T(8,128)(2,1)}, u32[]{:S(2)}, u32[]{:S(2)}) collective-permute-start(bf16[496,1024]{1,0:T(8,128)(2,1)} %broadcast_select_fusion.4), channel_id=1, source_target_pairs={{0,4},{1,5},{2,6},{3,7},{4,0},{5,1},{6,2},{7,3},{8,12},{9,13},{10,... | collective-permute-start | bytes 3047432 | tf_op jit(solution)/shard_map/ppermute | solution.py:619
  191.3 33.4 %slice-start.1 = ((s8[8388608]{0:T(1024)(128)(4,1)}), s8[4194304]{0:T(1024)(128)(4,1)S(1)}, s32[]{:S(2)}) async-start(s8[8388608]{0:T(1024)(128)(4,1)} %bitcast.33), calls=%async_computation.1 | async-start | bytes 8388608
  191.3 33.3 %copy-start.26 = (bf16[496,1024]{1,0:T(8,128)(2,1)S(1)}, bf16[496,1024]{1,0:T(8,128)(2,1)}, u32[]{:S(2)}) copy-start(bf16[496,1024]{1,0:T(8,128)(2,1)} %copy-done.25) | copy-start | bytes 3047428
  224.7 2.7 copy-start.10
  242.9 3.2 %copy-start.5 = (bf16[2,4,1024,480]{3,2,1,0:T(8,128)(2,1)}, bf16[2,4,1024,480]{3,2,1,0:T(8,128)(2,1)S(1)}, u32[]{:S(2)}) copy-start(bf16[2,4,1024,480]{3,2,1,0:T(8,128)(2,1)S(1)} %get-tuple-element.170.refs_18_) | copy-start | bytes 23592964
  246.1 2.5 copy-start.11
  (9 other events, 13.4 us)
where the time goes:
time: 286 us; the launch traced here: 285 us
  Pallas kernels  128 us (45%)
  waiting for transfers between devices  61.8 us (22%)
  local copies, waits for them, and re-layouts  50 us (17%)
  starting transfers between devices  24.3 us (8%)
  other arithmetic  18.3 us (6%)
    pallas_call x2, Pallas kernels, run_field(): pl.pallas_call(functools.partial(field_kernel, plan, last), grid_spec=plt...  64.7 us
    pallas_call x5, Pallas kernels, run_blocks(): pl.pallas_call(functools.partial(block_kernel, plan, len(arrays), aliased...  61 us
    ppermute x6, waiting for transfers between devices, along(): return lax.ppermute(value, 'space', pairs)  60.5 us
    unnamed x80, local copies, waits for them, and re-layouts  47.3 us
    ppermute x6, starting transfers between devices, along(): return lax.ppermute(value, 'space', pairs)  12.6 us
    ppermute x12, starting transfers between devices, hop(): return lax.ppermute(value, 'rep', [(r, r ^ 1 << b) for r in range(reps)])  11.7 us
  transfers between devices with their start and end apart: 18, of which 5 were waited for; matrix products, arithmetic and copies ran while one was open for 7% of the time, Pallas kernels for 27%

commit v1 on v0

--- a/solution.py
+++ b/solution.py
@@ -14,8 +14,8 @@
 EXTRA = 16
 BF16 = jnp.bfloat16
 F32 = jnp.float32
-BLOCK_VMEM = 32 * 1024 * 1024
-FIELD_VMEM = 44 * 1024 * 1024
+BLOCK_VMEM = 60 * 1024 * 1024
+FIELD_VMEM = 60 * 1024 * 1024
 
 
 def nn(a, b):
@@ -51,6 +51,10 @@
         self.unit_rows = c_in // n
         self.proj_rows = 5 * c_out // n
         self.cls_rows = c_out // n
+        starts = [self.proj_rows * s // 128 * 128 for s in range(n)]
+        ends = [-(-self.proj_rows * (s + 1) // 128) * 128 for s in range(n)]
+        self.window = max(e - b for b, e in zip(starts, ends))
+        self.starts = [min(b, 5 * c_out - self.window) for b in starts]
         tables = [self.table(s) for s in range(n)]
         self.n_slots = max(t[1] for t in tables)
         self.depth = max(t[2] for t in tables)
@@ -60,7 +64,9 @@
         self.flags = self.tables.shape[1]
         self.tables = np.concatenate([
             self.tables,
-            np.array([[len(c) for c in t[0]] + t[3] + [s] for s, t in enumerate(tables)], np.int32),
+            np.array([
+                [len(c) for c in t[0]] + t[3] + [s, self.starts[s]] for s, t in enumerate(tables)
+            ], np.int32),
         ], axis=1)
 
     def tap(self, t):
@@ -76,10 +82,19 @@
 
     def table(self, s):
         parts = [[] for _ in range(self.n)]
+        here = range(s * self.units, (s + 1) * self.units)
         slots = {}
-        for local in range(self.units):
-            unit = s * self.units + local
+        for k in range(4):
+            for b in ((1,) if k == 0 else range(3)):
+                if any(
+                    isinstance(self.tap(u // self.n), tuple)
+                    and (self.tap(u // self.n)[0], self.tap(u // self.n)[2]) == (k, b)
+                    for u in here
+                ):
+                    slots[(k, b)] = len(slots)
+        for unit in here:
             c, tap = unit % self.n, self.tap(unit // self.n)
+            local = unit - s * self.units
             if tap is None or tap == "zero":
                 parts[c].append([0, 0, 0, 0, 1 if tap is None else 2, local])
                 continue
@@ -89,8 +104,15 @@
                 j for j in range(self.n)
                 if any(0 <= self.rows * j + i - move < self.height for i in range(self.rows))
             ]
-            slot = slots.setdefault((k, b), len(slots))
-            parts[c].append([slot, move, valid[0], valid[-1] + 1, 0, local])
+            entry = [slots[(k, b)], move, valid[0], valid[-1] + 1, 0, local]
+            if b == 2 and len(parts[c]) > 1 and all(
+                e[4] == 0 and e[:4] == [entry[0] - back] + entry[1:4]
+                for back, e in ((1, parts[c][-1]), (2, parts[c][-2]))
+            ):
+                parts[c][-2][4] = 3
+                parts[c][-1][4] = 4
+                entry[4] = 4
+            parts[c].append(entry)
         want = [slots.get((k, b), -1) for k in range(4) for b in range(3)]
         return parts, len(slots), max(len(c) for c in parts), want
 
@@ -311,10 +333,9 @@
 
     @pl.when(step == 0)
     def _():
-        zero = jnp.zeros((edge_rows, cols, c_out), BF16)
-        for slot in range(plan.n_slots):
-            dbuf[slot, :edge_rows] = zero
-            dbuf[slot, edge_rows + plan.height:] = zero
+        zero = jnp.zeros((edge_rows, cols, dbuf.shape[2]), BF16)
+        dbuf[:edge_rows] = zero
+        dbuf[edge_rows + plan.height:] = zero
         pad[:, :EDGE, :] = jnp.zeros((rows, EDGE, c_out), F32)
         pad[:, EDGE + cols:, :] = jnp.zeros((rows, EDGE, c_out), F32)
         gpt[...] = jnp.zeros_like(gpt)
@@ -368,7 +389,8 @@
         ).astype(BF16)
         d_y = jnp.where(y_pre > 0, nt(d_logits, wcls_ref[...]), 0.0).astype(BF16)
         sdy[0:1, :] += jnp.sum(d_y.astype(F32), axis=0, keepdims=True)
-        gpt[...] += nn(nt(identity(c_out), d_y).astype(BF16), cat5[...])
+        window = pl.ds(pl.multiple_of(tab[flags + n + 13], 128), plan.window)
+        gpt[...] += nn(nt(identity(c_out), d_y).astype(BF16), cat5[:, window])
         gc[...] += nn(nt(identity(128), d_logits).astype(BF16), y_act)
         for k in range(4):
             want = [tab[flags + n + 3 * k + b] for b in range(3)]
@@ -388,12 +410,12 @@
 
                     @pl.when(want[b] >= 0)
                     def _(b=b):
-                        slot = jnp.maximum(want[b], 0)
+                        lanes = pl.ds(pl.multiple_of(jnp.maximum(want[b], 0) * c_out, c_out), c_out)
                         if b == 1:
-                            dbuf[slot, at] = d_k
+                            dbuf[at, :, lanes] = d_k
                         else:
                             first = EDGE + (1 - b) * RATE * k
-                            dbuf[slot, at] = pad[:, first:first + cols, :].astype(BF16)
+                            dbuf[at, :, lanes] = pad[:, first:first + cols, :].astype(BF16)
 
     @pl.when(step == n - 1)
     def _():
@@ -405,10 +427,9 @@
             total = total + nt(head, pool)
             rest = rest - head.astype(F32)
         spool[...] = jnp.where(pact[...] > 0, jnp.broadcast_to(total[0:1, :], total.shape), 0.0)
-        for c in range(5):
-            gp[c * c_out:(c + 1) * c_out, :] = gpt[:, c * c_out:(c + 1) * c_out].T
+        gp[:plan.window, :] = gpt[...].T
         index = tab[flags + n + 12]
-        first = pl.multiple_of(index * plan.proj_rows, plan.proj_rows)
+        first = pl.multiple_of(index * plan.proj_rows - tab[flags + n + 13], 32)
         p_out[...] = finish(gp[pl.ds(first, plan.proj_rows), :], prev_p[...] if last else None)
         gp[:c_out, :128] = gc[...].T
         first = pl.multiple_of(index * plan.cls_rows, plan.cls_rows)
@@ -434,28 +455,44 @@
             slot, move, low, high = tab[base], tab[base + 1], tab[base + 2], tab[base + 3]
             kind = tab[base + 4]
 
-            def term(j):
-                first = j * rows - move + edge_rows
-                return nn(xt_ref[j], dbuf[slot, pl.ds(first, rows)].reshape(pix, c_out))
-
-            whole = jnp.logical_and(low == 0, high == n)
-
-            @pl.when(whole)
-            def _():
-                total = term(0)
-                for j in range(1, n):
-                    total = total + term(j)
-                acc[...] = total
-
-            @pl.when(jnp.logical_not(whole))
-            def _():
-                acc[...] = jnp.zeros_like(acc)
-
-                def add(j, _):
-                    acc[...] += term(j)
-                    return 0
-
-                lax.fori_loop(low, high, add, 0)
+            def product(taps):
+                width = taps * c_out
+                lanes = pl.ds(pl.multiple_of(slot * c_out, c_out), width)
+
+                def term(j):
+                    first = j * rows - move + edge_rows
+                    return nn(xt_ref[j], dbuf[pl.ds(first, rows), :, lanes].reshape(pix, width))
+
+                whole = jnp.logical_and(low == 0, high == n)
+
+                @pl.when(whole)
+                def _():
+                    total = term(0)
+                    for j in range(1, n):
+                        total = total + term(j)
+                    acc[:, :width] = total
+
+                @pl.when(jnp.logical_not(whole))
+                def _():
+                    acc[:, :width] = jnp.zeros((unit_rows, width), F32)
+
+                    def add(j, _):
+                        acc[:, :width] += term(j)
+                        return 0
+
+                    lax.fori_loop(low, high, add, 0)
+
+            @pl.when(kind == 3)
+            def _():
+                product(3)
+
+            @pl.when(kind == 0)
+            def _():
+                product(1)
+
+            @pl.when(kind == 2)
+            def _():
+                acc[:, :c_out] = jnp.zeros((unit_rows, c_out), F32)
 
             @pl.when(kind == 1)
             def _():
@@ -466,11 +503,22 @@
                     lanes = slice(c * 128, (c + 1) * 128)
                     acc[:, lanes] = column * spool[0:1, lanes]
 
-            if last:
-                stage[parity, t] = finish(acc[...], prev_g[t])
-                out_copy(part, parity, t).start()
-            else:
-                g_out[t] = finish(acc[...], None)
+            def emit(at, lanes):
+                if last:
+                    stage[parity, at] = finish(acc[:, lanes], prev_g[at])
+                    out_copy(part, parity, at).start()
+                else:
+                    g_out[at] = finish(acc[:, lanes], None)
+
+            @pl.when(kind != 4)
+            def _():
+                emit(t, slice(0, c_out))
+
+            @pl.when(kind == 3)
+            def _():
+                for b in (1, 2):
+                    emit(t + b, slice(b * c_out, (b + 1) * c_out))
+
             return 0
 
         lax.fori_loop(0, tab[flags + part], one, 0)
@@ -557,17 +605,17 @@
             in_specs=in_specs,
             out_specs=[main_spec] + small,
             scratch_shapes=[
-                pltpu.VMEM((plan.n_slots, plan.height + 2 * (rows - 1), cols, c_out), BF16),
+                pltpu.VMEM((plan.height + 2 * (rows - 1), cols, plan.n_slots * c_out), BF16),
                 pltpu.VMEM((rows, cols + 2 * EDGE, c_out), F32),
                 pltpu.VMEM((16, c_in), F32),
-                pltpu.VMEM((c_out, 5 * c_out), F32),
-                pltpu.VMEM((5 * c_out, c_out), F32),
+                pltpu.VMEM((c_out, plan.window), F32),
+                pltpu.VMEM((max(plan.window, c_out), c_out), F32),
                 pltpu.VMEM((128, c_out), F32),
                 pltpu.VMEM((16, c_out), F32),
                 pltpu.VMEM((16, c_out), F32),
                 pltpu.VMEM((16, c_out), F32),
                 pltpu.VMEM((pix, 5 * c_out), BF16),
-                pltpu.VMEM((unit_rows, c_out), F32),
+                pltpu.VMEM((unit_rows, 3 * c_out), F32),
                 pltpu.VMEM((2, depth if last else 1, unit_rows, c_out), F32),
                 pltpu.SemaphoreType.DMA((2, depth)),
             ],
@@ -603,8 +651,8 @@
     n_bits = reps.bit_length() - 1
     bits = [jnp.bitwise_and(jnp.right_shift(matching[0], b), 1) == 1 for b in range(n_bits)]
     top = jnp.int32(0)
-    for b in range(n_bits):
-        top = jnp.where(bits[b], n_bits - 1 - b, top)
+    for at, b in enumerate(list(range(1, n_bits)) + [0]):
+        top = jnp.where(bits[b], n_bits - 1 - at, top)
     tab = jnp.asarray(plan.tables)[here]
     wcls = jnp.pad(w_cls, ((0, 0), (0, 128 - plan.classes)))
 
@@ -632,48 +680,37 @@
         return value
 
     common = (w_in, w_proj, wcls, class_weight)
-    ups, downs, items = [x], [x], [x]
-    values, moves = {}, {q: [] for q in range(n)}
+    hops = list(range(1, n_bits)) + [0]
+    rounds = n + n_bits - 1
+    up = down = x
+    ups, downs = [x], [x]
+    values, moves = {0: x}, {q: [] for q in range(n)}
     state, grads = None, None
-
-    def pair(q):
-        return (moves[q], (top, blocks[q], 1))
-
-    for t in range(1, n + n_bits - 1):
+    for t in range(1, rounds + 1):
         q = t - 1
+        if 0 < q < n:
+            values[q] = arrival(q, ups, downs)
+        for i in range(1, n_bits):
+            if 0 <= q - i < n:
+                values[q - i] = jnp.where(bits[hops[i - 1]], moves[q - i][0], values[q - i])
         if t < n:
             ups.append(along(ups[-1], 1, t))
             downs.append(along(downs[-1], -1, t))
-        tie = []
+        for i in range(n_bits):
+            if 0 <= q - i < n:
+                moves[q - i].insert(0, hop(values[q - i], hops[i]))
+        slots = []
         if q < n:
-            moved = hop(items[q], 0)
-            moves[q].insert(0, moved)
-            values[q] = jnp.where(bits[0], moved, items[q])
-            tie = [values[q]]
-        sent = []
-        for b in range(1, n_bits):
-            if 0 <= t - b < n:
-                moves[t - b].insert(0, hop(values[t - b], b))
-                sent.append((t - b, b))
-        if q < n:
-            slots = [([after(items[q], *tie)], (0, blocks[q], 0))]
-            if t >= n_bits:
-                slots.append(pair(t - n_bits))
-            state = run_blocks(plan, slots, w_in, state)
-        if q == n:
+            slots.append(([values[q]], (0, blocks[q], 0)))
+        if t >= n_bits:
+            at = t - n_bits
+            slots.append((moves[at], (top, blocks[at], 1)))
+        state = run_blocks(plan, slots, w_in, state)
+        if q == min(n, rounds - 1):
             grads = tuple(run_field(plan, 0, tab, state, *common, None))
-        for at, b in sent:
-            if b + 1 < n_bits:
-                values[at] = jnp.where(bits[b], moves[at][0], values[at])
-        if t < n:
-            items.append(arrival(t, ups, downs))
-        live = (ups, downs, items, values, moves, state, grads)
-        ups, downs, items, values, moves, state, grads = lax.optimization_barrier(live)
-    if grads is None:
-        grads = tuple(run_field(plan, 0, tab, state, *common, None))
-        state, grads = lax.optimization_barrier((state, grads))
-    done = max(0, n - n_bits + 1)
-    state = run_blocks(plan, [pair(q) for q in range(done, n)], w_in, state)
+        if t < rounds:
+            live = (ups, downs, values, moves, state, grads)
+            ups, downs, values, moves, state, grads = lax.optimization_barrier(live)
     avg_in, avg_proj, avg_cls = run_field(plan, 1, tab, state, *common, grads)
     return avg_in[None], avg_proj[None], avg_cls[None, :, :plan.classes]
 

time: 286 us -> 227 us (0.79)
  local copies, waits for them, and re-layouts: 50 us -> 6.44 us
  waiting for transfers between devices: 61.8 us -> 39.7 us
  Pallas kernels: 128 us -> 132 us
    unnamed x80 -> x32, local copies, waits for them, and re-layouts: 47.3 us -> 1.79 us
    ppermute x6, waiting for transfers between devices: 60.5 us -> 19.1 us  [along(): return lax.ppermute(value, 'space', pairs)]
    ppermute x12, waiting for transfers between devices: 1.31 us -> 20.6 us  [hop(): return lax.ppermute(value, 'rep', [(r, r ^ 1 << b) for r in range(reps)])]
    pallas_call x5 -> x6, Pallas kernels: 61 us -> 70 us  [run_blocks(): pl.pallas_call(functools.partial(block_kernel, plan, len(arrays), aliased...]
    pallas_call x2, Pallas kernels: 64.7 us -> 59.3 us  [run_field(): pl.pallas_call(functools.partial(field_kernel, plan, last), grid_spec=plt...]
  transfers between devices with their start and end apart: 18 -> 18, of which waited for: 5 -> 11; matrix products, arithmetic and copies ran while one was open for 7% -> 8% of each run, Pallas kernels for 27% -> 40%
where the time goes in v1:
time: 227 us; the launch traced here: 224 us
  Pallas kernels  132 us (58%)
  waiting for transfers between devices  39.7 us (17%)
  starting transfers between devices  24 us (11%)
  other arithmetic  20.8 us (9%)
  local copies, waits for them, and re-layouts  6.44 us (3%)
    pallas_call x6, Pallas kernels, run_blocks(): pl.pallas_call(functools.partial(block_kernel, plan, len(arrays), aliased...  70 us
    pallas_call x2, Pallas kernels, run_field(): pl.pallas_call(functools.partial(field_kernel, plan, last), grid_spec=plt...  59.3 us
    ppermute x12, waiting for transfers between devices, hop(): return lax.ppermute(value, 'rep', [(r, r ^ 1 << b) for r in range(reps)])  20.6 us
    ppermute x6, waiting for transfers between devices, along(): return lax.ppermute(value, 'space', pairs)  19.1 us
    ppermute x6, starting transfers between devices, along(): return lax.ppermute(value, 'space', pairs)  13.2 us
    ppermute x12, starting transfers between devices, hop(): return lax.ppermute(value, 'rep', [(r, r ^ 1 << b) for r in range(reps)])  10.8 us
    another operation x7, other arithmetic, run_blocks(): meta = jnp.stack(meta)  7.93 us
    select_n x8, other arithmetic, per_device(): values[q - i] = jnp.where(bits[hops[i - 1]], moves[q - i][0], values[q - i])  7.11 us
  transfers between devices with their start and end apart: 18, of which 11 were waited for; matrix products, arithmetic and copies ran while one was open for 8% of the time, Pallas kernels for 40%

profile of v1, /device:TPU:0, one launch (start us, length us, event | category | flops | bytes accessed | tf_op | source)
XLA Modules:
  0.0 224.2 jit_solution(17087514096792816422)
XLA Ops:
  2.0 2.3 %pack.1.refs_0_ = bf16[496,1024]{1,0:T(8,128)(2,1)} custom-call(bf16[480,1024]{1,0:T(8,128)(2,1)} %bitcast.32, f32[1,1024]{1,0:T(1,128)} %pad.8.lab_ref), custom_call_target="tpu_custom_call" | custom-call | tf_op jit(solution)/shard_map/pack/pallas_call | solution.py:645
  4.3 5.9 %collective-permute-start = (bf16[496,1024]{1,0:T(8,128)(2,1)}, bf16[496,1024]{1,0:T(8,128)(2,1)}, u32[]{:S(2)}, u32[]{:S(2)}) collective-permute-start(bf16[496,1024]{1,0:T(8,128)(2,1)} %pack.1.refs_0_), channel_id=1, source_target_pairs={{0,8},{8,16},{16,24},{1,9},{9,17},{17,25},{2,10},{10,18},{18,26},{... | collective-permute-start | bytes 3047432 | tf_op jit(solution)/shard_map/ppermute | solution.py:664
  10.2 1.3 collective-permute-start.1
  11.5 1.6 collective-permute-start.2
  15.0 1.9 fusion.1
  16.9 10.3 %block_forward.6 = (bf16[2,4,1024,480]{3,2,1,0:T(8,128)(2,1)}, bf16[2,4,480,768]{3,2,1,0:T(8,128)(2,1)}, f32[3,2,20,96,256]{4,3,2,1,0:T(8,128)}, bf16[2,4,16,1024]{3,2,1,0:T(8,128)(2,1)}) custom-call(s32[1,3]{1,0:T(1,128)} %get-tuple-element.174.meta, bf16[496,1024]{1,0:T(8,128)(2,1)} %pack.1.refs_0_, bf16[29,1024,256]{2,1,0:T(8,128)(2,1)} %refs_14_.3), custom_call_target="tpu_custom_call" | custom-call | flops 4026531840 | bytes 40000000 | tf_op jit(solution)/shard_map/block_forward/pallas_call | solution.py:275
  27.3 4.0 %collective-permute-done = bf16[496,1024]{1,0:T(8,128)(2,1)} collective-permute-done((bf16[496,1024]{1,0:T(8,128)(2,1)}, bf16[496,1024]{1,0:T(8,128)(2,1)}, u32[]{:S(2)}, u32[]{:S(2)}) %collective-permute-start) | collective-permute-done | bytes 1015840 | tf_op jit(solution)/shard_map/ppermute | solution.py:664
  31.3 5.1 %collective-permute-done.1 = bf16[496,1024]{1,0:T(8,128)(2,1)} collective-permute-done((bf16[496,1024]{1,0:T(8,128)(2,1)}, bf16[496,1024]{1,0:T(8,128)(2,1)}, u32[]{:S(2)}, u32[]{:S(2)}) %collective-permute-start.1) | collective-permute-done | bytes 1015840 | tf_op jit(solution)/shard_map/ppermute | solution.py:664
  36.4 2.0 select_select_fusion.1.refs_0_
  38.4 1.6 collective-permute-start.6
  39.9 1.1 broadcast_select_fusion.3
  41.0 1.5 collective-permute-start.5
  42.5 1.6 collective-permute-start.3
  44.2 1.3 collective-permute-start.4
  45.5 10.2 %block_forward.7 = (bf16[2,4,1024,480]{3,2,1,0:T(8,128)(2,1)}, bf16[2,4,480,768]{3,2,1,0:T(8,128)(2,1)}, f32[3,2,20,96,256]{4,3,2,1,0:T(8,128)}, bf16[2,4,16,1024]{3,2,1,0:T(8,128)(2,1)}) custom-call(s32[1,3]{1,0:T(1,128)} %get-tuple-element.175.meta, ...), custom_call_target="tpu_custom_call", output_to_operand_aliasing={{0}: (3, {}), {1}: (4, {}), {2}: (5, {}), {3}: (6, {})} | custom-call | flops 4026531840 | bytes 40000000 | tf_op jit(solution)/shard_map/block_forward/pallas_call | solution.py:275
  55.7 5.7 %collective-permute-done.6.refs_3_ = bf16[496,1024]{1,0:T(8,128)(2,1)S(1)} collective-permute-done((bf16[496,1024]{1,0:T(8,128)(2,1)S(1)}, bf16[496,1024]{1,0:T(8,128)(2,1)S(1)}, u32[]{:S(2)}, u32[]{:S(2)}) %collective-permute-start.6) | collective-permute-done | bytes 1015840 | tf_op jit(solution)/shard_map/ppermute | solution.py:667
  61.4 2.5 %collective-permute-done.5.refs_2_ = bf16[496,1024]{1,0:T(8,128)(2,1)S(1)} collective-permute-done((bf16[496,1024]{1,0:T(8,128)(2,1)}, bf16[496,1024]{1,0:T(8,128)(2,1)S(1)}, u32[]{:S(2)}, u32[]{:S(2)}) %collective-permute-start.5) | collective-permute-done | bytes 1015840 | tf_op jit(solution)/shard_map/ppermute | solution.py:667
  63.9 6.3 %collective-permute-done.4 = bf16[496,1024]{1,0:T(8,128)(2,1)} collective-permute-done((bf16[496,1024]{1,0:T(8,128)(2,1)}, bf16[496,1024]{1,0:T(8,128)(2,1)}, u32[]{:S(2)}, u32[]{:S(2)}) %collective-permute-start.4) | collective-permute-done | bytes 1015840 | tf_op jit(solution)/shard_map/ppermute | solution.py:664
  70.2 1.1 broadcast_select_fusion.7
  71.4 1.7 fusion.refs_0_
  73.7 1.1 broadcast_select_fusion.2
  75.2 1.6 collective-permute-start.7
  76.9 1.5 collective-permute-start.8
  78.4 1.4 fusion.3
  80.3 14.7 %block_forward.8 = (bf16[2,4,1024,480]{3,2,1,0:T(8,128)(2,1)}, bf16[2,4,480,768]{3,2,1,0:T(8,128)(2,1)}, f32[3,2,20,96,256]{4,3,2,1,0:T(8,128)}, bf16[2,4,16,1024]{3,2,1,0:T(8,128)(2,1)}) custom-call(s32[2,3]{1,0:T(2,128)} %pad_add_fusion.meta, bf16[496,1024]{1,0:T(8,128)(2,1)} %copy-done, ...), custom_call_target="tpu_custom_call", output_to_operand_aliasing={{0}: (6, {}), {1}: (7, {}), {2}: (8, {}), {3}: (9, {})} | custom-call | flops 8053063680 | bytes 60000000 | tf_op jit(solution)/shard_map/block_forward/pallas_call | solution.py:275
  95.1 2.9 %collective-permute-done.11.refs_2_ = bf16[496,1024]{1,0:T(8,128)(2,1)S(1)} collective-permute-done((bf16[496,1024]{1,0:T(8,128)(2,1)S(1)}, bf16[496,1024]{1,0:T(8,128)(2,1)S(1)}, u32[]{:S(2)}, u32[]{:S(2)}) %collective-permute-start.11) | collective-permute-done | bytes 1015840 | tf_op jit(solution)/shard_map/ppermute | solution.py:667
  98.0 1.6 collective-permute-done.10.refs_2_
  99.6 3.8 %collective-permute-done.8 = bf16[496,1024]{1,0:T(8,128)(2,1)} collective-permute-done((bf16[496,1024]{1,0:T(8,128)(2,1)}, bf16[496,1024]{1,0:T(8,128)(2,1)}, u32[]{:S(2)}, u32[]{:S(2)}) %collective-permute-start.8) | collective-permute-done | bytes 1015840 | tf_op jit(solution)/shard_map/ppermute | solution.py:664
  103.4 1.3 broadcast_select_fusion.6
  104.8 1.4 select_select_fusion.2.refs_0_
  106.2 1.6 collective-permute-start.14
  107.8 1.1 broadcast_select_fusion.1
  108.9 1.5 collective-permute-start.13
  110.4 1.2 fusion.4
  112.2 14.9 %block_forward.9 = (bf16[2,4,1024,480]{3,2,1,0:T(8,128)(2,1)}, bf16[2,4,480,768]{3,2,1,0:T(8,128)(2,1)}, f32[3,2,20,96,256]{4,3,2,1,0:T(8,128)}, bf16[2,4,16,1024]{3,2,1,0:T(8,128)(2,1)}) custom-call(s32[2,3]{1,0:T(2,128)} %pad_add_fusion.1.meta, ...), custom_call_target="tpu_custom_call", output_to_operand_aliasing={{0}: (6, {}), {1}: (7, {}), {2}: (8, {}), {3}: (9, {})} | custom-call | flops 8053063680 | bytes 60000000 | tf_op jit(solution)/shard_map/block_forward/pallas_call | solution.py:275
  127.1 4.1 %collective-permute-done.14.refs_2_ = bf16[496,1024]{1,0:T(8,128)(2,1)S(1)} collective-permute-done((bf16[496,1024]{1,0:T(8,128)(2,1)S(1)}, bf16[496,1024]{1,0:T(8,128)(2,1)S(1)}, u32[]{:S(2)}, u32[]{:S(2)}) %collective-permute-start.14) | collective-permute-done | bytes 1015840 | tf_op jit(solution)/shard_map/ppermute | solution.py:667
  131.1 2.5 %collective-permute-done.13.refs_1_ = bf16[496,1024]{1,0:T(8,128)(2,1)S(1)} collective-permute-done((bf16[496,1024]{1,0:T(8,128)(2,1)}, bf16[496,1024]{1,0:T(8,128)(2,1)S(1)}, u32[]{:S(2)}, u32[]{:S(2)}) %collective-permute-start.13) | collective-permute-done | bytes 1015840 | tf_op jit(solution)/shard_map/ppermute | solution.py:667
  133.7 1.2 broadcast_select_fusion.5
  135.7 1.2 fusion.8.meta
  136.9 1.3 constant_dynamic-slice_fusion.1
  138.3 1.6 collective-permute-start.16
  139.8 9.9 %block_forward.10 = (bf16[2,4,1024,480]{3,2,1,0:T(8,128)(2,1)}, bf16[2,4,480,768]{3,2,1,0:T(8,128)(2,1)}, f32[3,2,20,96,256]{4,3,2,1,0:T(8,128)}, bf16[2,4,16,1024]{3,2,1,0:T(8,128)(2,1)}) custom-call(s32[1,3]{1,0:T(1,128)} %fusion.8.meta, ...), custom_call_target="tpu_custom_call", output_to_operand_aliasing={{0}: (5, {}), {1}: (6, {}), {2}: (7, {}), {3}: (8, {})} | custom-call | flops 4026531840 | bytes 40000000 | tf_op jit(solution)/shard_map/block_forward/pallas_call | solution.py:275
  149.8 28.9 %field_grads.2 = (bf16[4,8,256,256]{3,2,1,0:T(8,128)(2,1)}, bf16[320,256]{1,0:T(8,128)(2,1)}, bf16[64,128]{1,0:T(8,128)(2,1)}) custom-call(s32[210]{0:T(256)} %bitcast.33, bf16[2,4,480,768]{3,2,1,0:T(8,128)(2,1)} %get-tuple-element.154.refs_0_.refs_5_, ...), custom_call_target="tpu_custom_call" | custom-call | flops 10000000000 | bytes 90000000 | tf_op jit(solution)/shard_map/field_grads/pallas_call | solution.py:600
  179.1 1.1 fusion.5.meta
  180.2 1.2 collective-permute-done.17.refs_0_
  181.5 1.0 copy-done.12
  182.4 9.9 %block_forward.11 = (bf16[2,4,1024,480]{3,2,1,0:T(8,128)(2,1)}, bf16[2,4,480,768]{3,2,1,0:T(8,128)(2,1)}, f32[3,2,20,96,256]{4,3,2,1,0:T(8,128)}, bf16[2,4,16,1024]{3,2,1,0:T(8,128)(2,1)}) custom-call(s32[1,3]{1,0:T(1,128)} %fusion.5.meta, bf16[496,1024]{1,0:T(8,128)(2,1)} %copy-done.12, ...), custom_call_target="tpu_custom_call", output_to_operand_aliasing={{0}: (5, {}), {1}: (6, {}), {2}: (7, {}), {3}: (8, {})} | custom-call | flops 4026531840 | bytes 40000000 | tf_op jit(solution)/shard_map/block_forward/pallas_call | solution.py:275
  192.3 30.5 %field_grads.3 = (f32[7424,256]{1,0:T(8,128)}, f32[320,256]{1,0:T(8,128)}, f32[64,128]{1,0:T(8,128)}) custom-call(s32[210]{0:T(256)} %bitcast.34, bf16[2,4,480,768]{3,2,1,0:T(8,128)(2,1)} %get-tuple-element.157.refs_0_, f32[3,2,20,96,256]{4,3,2,1,0:T(8,128)} %get-tuple-element.158.refs_1_.refs_2_.refs_3_.refs_4_.refs_5_.refs_6_.refs_7_.refs_8_.refs_9_.refs_10_.refs_11_, ...), custom_call_target="tpu_custom_call" | custom-call | flops 10000000000 | bytes 90000000 | tf_op jit(solution)/shard_map/field_grads/pallas_call | solution.py:600
  (55 shorter events, 7.8 us)
Async XLA Ops:
  4.3 26.9 %collective-permute-start = (bf16[496,1024]{1,0:T(8,128)(2,1)}, bf16[496,1024]{1,0:T(8,128)(2,1)}, u32[]{:S(2)}, u32[]{:S(2)}) collective-permute-start(bf16[496,1024]{1,0:T(8,128)(2,1)} %pack.1.refs_0_), channel_id=1, source_target_pairs={{0,8},{8,16},{16,24},{1,9},{9,17},{17,25},{2,10},{10,18},{18,26},{... | collective-permute-start | bytes 3047432 | tf_op jit(solution)/shard_map/ppermute | solution.py:664
  10.2 26.1 %collective-permute-start.1 = (bf16[496,1024]{1,0:T(8,128)(2,1)}, bf16[496,1024]{1,0:T(8,128)(2,1)}, u32[]{:S(2)}, u32[]{:S(2)}) collective-permute-start(bf16[496,1024]{1,0:T(8,128)(2,1)} %pack.1.refs_0_), channel_id=1, source_target_pairs={{8,0},{16,8},{24,16},{9,1},{17,9},{25,17},{10,2},{18,10},{26,18},{... | collective-permute-start | bytes 3047432 | tf_op jit(solution)/shard_map/ppermute | solution.py:664
  11.5 24.8 %collective-permute-start.2 = (bf16[496,1024]{1,0:T(8,128)(2,1)}, bf16[496,1024]{1,0:T(8,128)(2,1)S(1)}, u32[]{:S(2)}, u32[]{:S(2)}) collective-permute-start(bf16[496,1024]{1,0:T(8,128)(2,1)} %pack.1.refs_0_), channel_id=1, source_target_pairs={{0,2},{1,3},{2,0},{3,1},{4,6},{5,7},{6,4},{7,5},{8,10},{9,11},{10,... | collective-permute-start | bytes 3047432 | tf_op jit(solution)/shard_map/ppermute | solution.py:667
  16.9 23.0 %copy-start.4 = (bf16[496,1024]{1,0:T(8,128)(2,1)S(1)}, bf16[496,1024]{1,0:T(8,128)(2,1)}, u32[]{:S(2)}) copy-start(bf16[496,1024]{1,0:T(8,128)(2,1)} %pack.1.refs_0_) | copy-start | bytes 3047428
  16.9 28.5 %copy-start.14 = (s32[8]{0:T(128)S(1)}, s32[8]{0:T(128)}, u32[]{:S(2)}) copy-start(s32[8]{0:T(128)} %param.15) | copy-start | bytes 100
  36.4 19.4 %copy-start.6 = (bf16[496,1024]{1,0:T(8,128)(2,1)}, bf16[496,1024]{1,0:T(8,128)(2,1)S(1)}, u32[]{:S(2)}) copy-start(bf16[496,1024]{1,0:T(8,128)(2,1)S(1)} %collective-permute-done.2.refs_3_) | copy-start | bytes 3047428
  38.4 7.1 %copy-start.3 = (bf16[496,1024]{1,0:T(8,128)(2,1)}, bf16[496,1024]{1,0:T(8,128)(2,1)S(1)}, u32[]{:S(2)}) copy-start(bf16[496,1024]{1,0:T(8,128)(2,1)S(1)} %select_select_fusion.1.refs_0_) | copy-start | bytes 3047428
  38.4 23.1 %collective-permute-start.6 = (bf16[496,1024]{1,0:T(8,128)(2,1)S(1)}, bf16[496,1024]{1,0:T(8,128)(2,1)S(1)}, u32[]{:S(2)}, u32[]{:S(2)}) collective-permute-start(bf16[496,1024]{1,0:T(8,128)(2,1)S(1)} %select_select_fusion.1.refs_0_), channel_id=1, source_target_pairs={{0,2},{1,3},{2,0},{3,1},{4,6},{5,7},{6,4},{7,5},{8,10},{9,11},{10,... | collective-permute-start | bytes 3047432 | tf_op jit(solution)/shard_map/ppermute | solution.py:667
  41.0 22.9 %collective-permute-start.5 = (bf16[496,1024]{1,0:T(8,128)(2,1)}, bf16[496,1024]{1,0:T(8,128)(2,1)S(1)}, u32[]{:S(2)}, u32[]{:S(2)}) collective-permute-start(bf16[496,1024]{1,0:T(8,128)(2,1)} %broadcast_select_fusion.3), channel_id=1, source_target_pairs={{0,4},{1,5},{2,6},{3,7},{4,0},{5,1},{6,2},{7,3},{8,12},{9,13},{10,... | collective-permute-start | bytes 3047432 | tf_op jit(solution)/shard_map/ppermute | solution.py:667
  42.5 21.4 %collective-permute-start.3 = (bf16[496,1024]{1,0:T(8,128)(2,1)}, bf16[496,1024]{1,0:T(8,128)(2,1)}, u32[]{:S(2)}, u32[]{:S(2)}) collective-permute-start(bf16[496,1024]{1,0:T(8,128)(2,1)} %collective-permute-done), channel_id=1, source_target_pairs={{8,16},{16,24},{9,17},{17,25},{10,18},{18,26},{11,19},{19,27},{12,... | collective-permute-start | bytes 3047432 | tf_op jit(solution)/shard_map/ppermute | solution.py:664
  44.2 26.1 %collective-permute-start.4 = (bf16[496,1024]{1,0:T(8,128)(2,1)}, bf16[496,1024]{1,0:T(8,128)(2,1)}, u32[]{:S(2)}, u32[]{:S(2)}) collective-permute-start(bf16[496,1024]{1,0:T(8,128)(2,1)} %collective-permute-done.1), channel_id=1, source_target_pairs={{8,0},{16,8},{9,1},{17,9},{10,2},{18,10},{11,3},{19,11},{12,4},{20... | collective-permute-start | bytes 3047432 | tf_op jit(solution)/shard_map/ppermute | solution.py:664
  61.4 33.6 %copy-start.5 = (bf16[496,1024]{1,0:T(8,128)(2,1)}, bf16[496,1024]{1,0:T(8,128)(2,1)S(1)}, u32[]{:S(2)}) copy-start(bf16[496,1024]{1,0:T(8,128)(2,1)S(1)} %collective-permute-done.6.refs_3_) | copy-start | bytes 3047428
  63.9 7.4 %copy-start.9 = (bf16[496,1024]{1,0:T(8,128)(2,1)}, bf16[496,1024]{1,0:T(8,128)(2,1)S(1)}, u32[]{:S(2)}) copy-start(bf16[496,1024]{1,0:T(8,128)(2,1)S(1)} %collective-permute-done.5.refs_2_) | copy-start | bytes 3047428
  71.4 9.0 %collective-permute-start.9 = (bf16[496,1024]{1,0:T(8,128)(2,1)}, bf16[496,1024]{1,0:T(8,128)(2,1)}, u32[]{:S(2)}, u32[]{:S(2)}) collective-permute-start(bf16[496,1024]{1,0:T(8,128)(2,1)} %broadcast_select_fusion.7), channel_id=1, source_target_pairs={{0,1},{1,0},{2,3},{3,2},{4,5},{5,4},{6,7},{7,6},{8,9},{9,8},{10,11... | collective-permute-start | bytes 3047432 | tf_op jit(solution)/shard_map/ppermute | solution.py:667
  73.0 7.3 %copy-start = (bf16[496,1024]{1,0:T(8,128)(2,1)}, bf16[496,1024]{1,0:T(8,128)(2,1)S(1)}, u32[]{:S(2)}) copy-start(bf16[496,1024]{1,0:T(8,128)(2,1)S(1)} %fusion.refs_0_) | copy-start | bytes 3047428
  73.1 24.9 %collective-permute-start.11 = (bf16[496,1024]{1,0:T(8,128)(2,1)S(1)}, bf16[496,1024]{1,0:T(8,128)(2,1)S(1)}, u32[]{:S(2)}, u32[]{:S(2)}) collective-permute-start(bf16[496,1024]{1,0:T(8,128)(2,1)S(1)} %fusion.refs_0_), channel_id=1, source_target_pairs={{0,2},{1,3},{2,0},{3,1},{4,6},{5,7},{6,4},{7,5},{8,10},{9,11},{10,... | collective-permute-start | bytes 3047432 | tf_op jit(solution)/shard_map/ppermute | solution.py:667
  74.7 24.9 %collective-permute-start.10 = (bf16[496,1024]{1,0:T(8,128)(2,1)}, bf16[496,1024]{1,0:T(8,128)(2,1)}, u32[]{:S(2)}, u32[]{:S(2)}) collective-permute-start(bf16[496,1024]{1,0:T(8,128)(2,1)} %broadcast_select_fusion.2), channel_id=1, source_target_pairs={{0,4},{1,5},{2,6},{3,7},{4,0},{5,1},{6,2},{7,3},{8,12},{9,13},{10,... | collective-permute-start | bytes 3047432 | tf_op jit(solution)/shard_map/ppermute | solution.py:667
  75.2 24.4 %collective-permute-start.7 = (bf16[496,1024]{1,0:T(8,128)(2,1)}, bf16[496,1024]{1,0:T(8,128)(2,1)}, u32[]{:S(2)}, u32[]{:S(2)}) collective-permute-start(bf16[496,1024]{1,0:T(8,128)(2,1)} %collective-permute-done.3), channel_id=1, source_target_pairs={{16,24},{17,25},{18,26},{19,27},{20,28},{21,29},{22,30},{23,31}} | collective-permute-start | bytes 3047432 | tf_op jit(solution)/shard_map/ppermute | solution.py:664
  76.9 26.5 %collective-permute-start.8 = (bf16[496,1024]{1,0:T(8,128)(2,1)}, bf16[496,1024]{1,0:T(8,128)(2,1)}, u32[]{:S(2)}, u32[]{:S(2)}) collective-permute-start(bf16[496,1024]{1,0:T(8,128)(2,1)} %collective-permute-done.4), channel_id=1, source_target_pairs={{8,0},{9,1},{10,2},{11,3},{12,4},{13,5},{14,6},{15,7}} | collective-permute-start | bytes 3047432 | tf_op jit(solution)/shard_map/ppermute | solution.py:664
  95.1 12.7 %copy-start.1 = (bf16[496,1024]{1,0:T(8,128)(2,1)S(1)}, bf16[496,1024]{1,0:T(8,128)(2,1)}, u32[]{:S(2)}) copy-start(bf16[496,1024]{1,0:T(8,128)(2,1)} %copy-done) | copy-start | bytes 3047428
  98.0 29.1 %copy-start.7 = (bf16[496,1024]{1,0:T(8,128)(2,1)}, bf16[496,1024]{1,0:T(8,128)(2,1)S(1)}, u32[]{:S(2)}) copy-start(bf16[496,1024]{1,0:T(8,128)(2,1)S(1)} %collective-permute-done.11.refs_2_) | copy-start | bytes 3047428
  104.7 7.5 %collective-permute-start.12 = (bf16[496,1024]{1,0:T(8,128)(2,1)S(1)}, bf16[496,1024]{1,0:T(8,128)(2,1)}, u32[]{:S(2)}, u32[]{:S(2)}) collective-permute-start(bf16[496,1024]{1,0:T(8,128)(2,1)S(1)} %broadcast_select_fusion.6), channel_id=1, source_target_pairs={{0,1},{1,0},{2,3},{3,2},{4,5},{5,4},{6,7},{7,6},{8,9},{9,8},{10,11... | collective-permute-start | bytes 3047432 | tf_op jit(solution)/shard_map/ppermute | solution.py:667
  106.2 6.0 %copy-start.2 = (bf16[496,1024]{1,0:T(8,128)(2,1)}, bf16[496,1024]{1,0:T(8,128)(2,1)S(1)}, u32[]{:S(2)}) copy-start(bf16[496,1024]{1,0:T(8,128)(2,1)S(1)} %select_select_fusion.2.refs_0_) | copy-start | bytes 3047428
  106.2 24.9 %collective-permute-start.14 = (bf16[496,1024]{1,0:T(8,128)(2,1)S(1)}, bf16[496,1024]{1,0:T(8,128)(2,1)S(1)}, u32[]{:S(2)}, u32[]{:S(2)}) collective-permute-start(bf16[496,1024]{1,0:T(8,128)(2,1)S(1)} %select_select_fusion.2.refs_0_), channel_id=1, source_target_pairs={{0,2},{1,3},{2,0},{3,1},{4,6},{5,7},{6,4},{7,5},{8,10},{9,11},{10,... | collective-permute-start | bytes 3047432 | tf_op jit(solution)/shard_map/ppermute | solution.py:667
  108.9 24.8 %collective-permute-start.13 = (bf16[496,1024]{1,0:T(8,128)(2,1)}, bf16[496,1024]{1,0:T(8,128)(2,1)S(1)}, u32[]{:S(2)}, u32[]{:S(2)}) collective-permute-start(bf16[496,1024]{1,0:T(8,128)(2,1)} %broadcast_select_fusion.1), channel_id=1, source_target_pairs={{0,4},{1,5},{2,6},{3,7},{4,0},{5,1},{6,2},{7,3},{8,12},{9,13},{10,... | collective-permute-start | bytes 3047432 | tf_op jit(solution)/shard_map/ppermute | solution.py:667
  112.2 22.7 %copy-start.13 = (bf16[256,3]{0,1:T(4,128)(2,1)S(1)}, bf16[256,3]{0,1:T(4,128)(2,1)}, u32[]{:S(2)}) copy-start(bf16[256,3]{0,1:T(4,128)(2,1)} %param.13) | copy-start | bytes 4612
  131.1 18.6 %copy-start.8 = (bf16[496,1024]{1,0:T(8,128)(2,1)}, bf16[496,1024]{1,0:T(8,128)(2,1)S(1)}, u32[]{:S(2)}) copy-start(bf16[496,1024]{1,0:T(8,128)(2,1)S(1)} %collective-permute-done.14.refs_2_) | copy-start | bytes 3047428
  133.7 6.2 %copy-start.10 = (bf16[496,1024]{1,0:T(8,128)(2,1)}, bf16[496,1024]{1,0:T(8,128)(2,1)S(1)}, u32[]{:S(2)}) copy-start(bf16[496,1024]{1,0:T(8,128)(2,1)S(1)} %collective-permute-done.13.refs_1_) | copy-start | bytes 3047428
  134.9 5.0 %collective-permute-start.15 = (bf16[496,1024]{1,0:T(8,128)(2,1)}, bf16[496,1024]{1,0:T(8,128)(2,1)}, u32[]{:S(2)}, u32[]{:S(2)}) collective-permute-start(bf16[496,1024]{1,0:T(8,128)(2,1)} %broadcast_select_fusion.5), channel_id=1, source_target_pairs={{0,1},{1,0},{2,3},{3,2},{4,5},{5,4},{6,7},{7,6},{8,9},{9,8},{10,11... | collective-permute-start | bytes 3047432 | tf_op jit(solution)/shard_map/ppermute | solution.py:667
  138.3 40.4 %collective-permute-start.16 = (bf16[496,1024]{1,0:T(8,128)(2,1)S(1)}, bf16[496,1024]{1,0:T(8,128)(2,1)S(1)}, u32[]{:S(2)}, u32[]{:S(2)}) collective-permute-start(bf16[496,1024]{1,0:T(8,128)(2,1)S(1)} %broadcast_select_fusion), channel_id=1, source_target_pairs={{0,4},{1,5},{2,6},{3,7},{4,0},{5,1},{6,2},{7,3},{8,12},{9,13},{10,... | collective-permute-start | bytes 3047432 | tf_op jit(solution)/shard_map/ppermute | solution.py:667
  178.6 2.8 %copy-start.11 = (bf16[496,1024]{1,0:T(8,128)(2,1)}, bf16[496,1024]{1,0:T(8,128)(2,1)S(1)}, u32[]{:S(2)}) copy-start(bf16[496,1024]{1,0:T(8,128)(2,1)S(1)} %collective-permute-done.16.refs_1_) | copy-start | bytes 3047428
  178.8 2.7 %collective-permute-start.17 = (bf16[496,1024]{1,0:T(8,128)(2,1)S(1)}, bf16[496,1024]{1,0:T(8,128)(2,1)S(1)}, u32[]{:S(2)}, u32[]{:S(2)}) collective-permute-start(bf16[496,1024]{1,0:T(8,128)(2,1)S(1)} %broadcast_select_fusion.4), channel_id=1, source_target_pairs={{0,1},{1,0},{2,3},{3,2},{4,5},{5,4},{6,7},{7,6},{8,9},{9,8},{10,11... | collective-permute-start | bytes 3047432 | tf_op jit(solution)/shard_map/ppermute | solution.py:667
  181.5 1.0 copy-start.12

commit v2 on v1

--- a/solution.py
+++ b/solution.py
@@ -130,7 +130,7 @@
     out_ref[pix:, :] = extra.astype(BF16)
 
 
-def block_kernel(plan, n_cand, aliased, meta, *refs):
+def block_kernel(plan, n_cand, n_slots, aliased, meta, *refs):
     rows, cols, c_in, c_out = plan.rows, plan.cols, plan.c_in, plan.c_out
     pix = plan.pix
     cands = refs[:n_cand]
@@ -138,14 +138,16 @@
     refs = refs[n_cand + 1 + (4 if aliased else 0):]
     xt_out, cat_out, s_out, aux_out = refs[:4]
     xin, wbuf, xtb, catb, sb, res, sem_x, sem_w, sem_o, sem_s = refs[4:]
-    xbuf = xin.at[pl.ds(0, pix)]
     step = pl.program_id(0)
-    source, block, field = meta[step, 0], meta[step, 1], meta[step, 2]
-
-    for c in range(n_cand):
-        @pl.when(source == c)
-        def _(c=c):
-            pltpu.make_async_copy(cands[c], xin, sem_x).start()
+    block, field = meta[step, 1], meta[step, 2]
+    now = lax.rem(step, 2)
+    xbuf = xin.at[now, pl.ds(0, pix)]
+
+    def fetch(at, slot):
+        for c in range(n_cand):
+            @pl.when(meta[at, 0] == c)
+            def _(c=c):
+                pltpu.make_async_copy(cands[c], xin.at[slot], sem_x.at[slot]).start()
 
     def weights(group, taps):
         return [
@@ -157,15 +159,21 @@
 
     @pl.when(step == 0)
     def _():
+        fetch(0, 0)
         for group, taps in enumerate(plan.loads):
             for copy in weights(group, taps):
                 copy.start()
         res[:, :EDGE, :] = jnp.zeros((rows, EDGE, res.shape[2]), F32)
         res[:, EDGE + cols:, :] = jnp.zeros((rows, EDGE, res.shape[2]), F32)
 
-    pltpu.make_async_copy(cands[0], xin, sem_x).wait()
+    if n_slots > 1:
+        @pl.when(step + 1 < n_slots)
+        def _():
+            fetch(step + 1, 1 - now)
+
+    pltpu.make_async_copy(cands[0], xin.at[now], sem_x.at[now]).wait()
     aux_copy = pltpu.make_async_copy(
-        xin.at[pl.ds(pix, EXTRA)], aux_out.at[field, block], sem_o.at[2]
+        xin.at[now, pl.ds(pix, EXTRA)], aux_out.at[field, block], sem_o.at[2]
     )
     aux_copy.start()
     eye = identity(256)
@@ -252,14 +260,8 @@
                 shifted_copy(3 * at + a).wait()
 
 
-def run_blocks(plan, slots, w_in, state):
-    arrays, meta = [], []
-    for cands, (source, block, field) in slots:
-        meta.append(jnp.stack([
-            jnp.asarray(v, jnp.int32) for v in (source + len(arrays), block, field)
-        ]))
-        arrays.extend(cands)
-    meta = jnp.stack(meta)
+def run_blocks(plan, slots, meta, w_in, state):
+    arrays = [value for cands in slots for value in cands]
     n, rows, cols, pix = plan.n, plan.rows, plan.cols, plan.pix
     c_in, c_out, n_sh = plan.c_in, plan.c_out, plan.n_sh
     shapes = [
@@ -268,25 +270,25 @@
         jax.ShapeDtypeStruct((3 * n_sh, 2, n * rows, cols, c_out), F32),
         jax.ShapeDtypeStruct((2, n, EXTRA, c_in), BF16),
     ]
+    widest = max(len(g) for g in plan.loads) * c_out
     aliased = state is not None
     operands = [*arrays, w_in] + (list(state) if aliased else [])
     aliases = {1 + len(arrays) + 1 + i: i for i in range(4)} if aliased else {}
-    widest = max(len(g) for g in plan.loads) * c_out
     return pl.pallas_call(
-        functools.partial(block_kernel, plan, len(arrays), aliased),
+        functools.partial(block_kernel, plan, len(arrays), len(slots), aliased),
         grid_spec=pltpu.PrefetchScalarGridSpec(
             num_scalar_prefetch=1,
             grid=(len(slots),),
             in_specs=[pl.BlockSpec(memory_space=pl.ANY)] * len(operands),
             out_specs=[pl.BlockSpec(memory_space=pl.ANY)] * 4,
             scratch_shapes=[
-                pltpu.VMEM((pix + EXTRA, c_in), BF16),
+                pltpu.VMEM((2, pix + EXTRA, c_in), BF16),
                 pltpu.VMEM((len(plan.loads), c_in, widest), BF16),
                 pltpu.VMEM((c_in, pix), BF16),
                 pltpu.VMEM((pix, len(plan.direct) * c_out), BF16),
                 pltpu.VMEM((3 * n_sh, rows, cols, c_out), F32),
                 pltpu.VMEM((rows, cols + 2 * EDGE, widest), F32),
-                pltpu.SemaphoreType.DMA,
+                pltpu.SemaphoreType.DMA((2,)),
                 pltpu.SemaphoreType.DMA((len(plan.loads), 4)),
                 pltpu.SemaphoreType.DMA((3,)),
                 pltpu.SemaphoreType.DMA((3 * n_sh,)),
@@ -321,7 +323,7 @@
         prev_g, prev_p, prev_c = refs[:3]
         refs = refs[3:]
     g_out, p_out, c_ref_out = refs[:3]
-    dbuf, pad, mean, gpt, gp, gc, sdy, spool, pact, cat5, acc, stage, sems = refs[3:]
+    (dbuf, pad, mean, ybuf, lbuf, dybuf, gp, spool, pact, catall, acc, stage, sems) = refs[3:]
     step = pl.program_id(0)
     edge_rows = rows - 1
 
@@ -338,9 +340,6 @@
         dbuf[edge_rows + plan.height:] = zero
         pad[:, :EDGE, :] = jnp.zeros((rows, EDGE, c_out), F32)
         pad[:, EDGE + cols:, :] = jnp.zeros((rows, EDGE, c_out), F32)
-        gpt[...] = jnp.zeros_like(gpt)
-        gc[...] = jnp.zeros_like(gc)
-        sdy[...] = jnp.zeros_like(sdy)
         total = jnp.zeros((1, c_in), F32)
         for j in range(n):
             extra = all_ref[j].astype(F32)
@@ -352,6 +351,7 @@
     @pl.when(step < n)
     def _():
         block = step
+        cat5 = catall.at[block]
         for k in range(4):
             part = slice(k * c_out, (k + 1) * c_out)
             if k in plan.shifted:
@@ -388,10 +388,9 @@
             live, (prob - onehot) * weight * (LOSS_SCALE / plan.total), 0.0
         ).astype(BF16)
         d_y = jnp.where(y_pre > 0, nt(d_logits, wcls_ref[...]), 0.0).astype(BF16)
-        sdy[0:1, :] += jnp.sum(d_y.astype(F32), axis=0, keepdims=True)
-        window = pl.ds(pl.multiple_of(tab[flags + n + 13], 128), plan.window)
-        gpt[...] += nn(nt(identity(c_out), d_y).astype(BF16), cat5[:, window])
-        gc[...] += nn(nt(identity(128), d_logits).astype(BF16), y_act)
+        ybuf[block] = y_act
+        lbuf[block] = d_logits
+        dybuf[block] = d_y
         for k in range(4):
             want = [tab[flags + n + 3 * k + b] for b in range(3)]
             part = slice(k * c_out, (k + 1) * c_out)
@@ -419,19 +418,28 @@
 
     @pl.when(step == n - 1)
     def _():
+        all_dy = dybuf[...].reshape(n * pix, c_out)
         pool = wproj_ref[4 * c_out:, :]
-        rest = sdy[...]
-        total = jnp.zeros(sdy.shape, F32)
+        rest = nn(jnp.ones((16, n * pix), BF16), all_dy)
+        total = jnp.zeros(rest.shape, F32)
         for _i in range(3):
             head = rest.astype(BF16)
             total = total + nt(head, pool)
             rest = rest - head.astype(F32)
         spool[...] = jnp.where(pact[...] > 0, jnp.broadcast_to(total[0:1, :], total.shape), 0.0)
-        gp[:plan.window, :] = gpt[...].T
+        window = pl.ds(pl.multiple_of(tab[flags + n + 13], 128), plan.window)
+        g_proj = jnp.zeros((c_out, plan.window), F32)
+        g_cls = jnp.zeros((128, c_out), F32)
+        for j in range(n):
+            g_proj = g_proj + nn(
+                nt(identity(c_out), dybuf[j]).astype(BF16), catall[j, :, window]
+            )
+            g_cls = g_cls + nn(nt(identity(128), lbuf[j]).astype(BF16), ybuf[j])
+        gp[:plan.window, :] = g_proj.T
         index = tab[flags + n + 12]
         first = pl.multiple_of(index * plan.proj_rows - tab[flags + n + 13], 32)
         p_out[...] = finish(gp[pl.ds(first, plan.proj_rows), :], prev_p[...] if last else None)
-        gp[:c_out, :128] = gc[...].T
+        gp[:c_out, :128] = g_cls.T
         first = pl.multiple_of(index * plan.cls_rows, plan.cls_rows)
         c_ref_out[...] = finish(
             gp[pl.ds(first, plan.cls_rows), :128], prev_c[...] if last else None
@@ -608,13 +616,13 @@
                 pltpu.VMEM((plan.height + 2 * (rows - 1), cols, plan.n_slots * c_out), BF16),
                 pltpu.VMEM((rows, cols + 2 * EDGE, c_out), F32),
                 pltpu.VMEM((16, c_in), F32),
-                pltpu.VMEM((c_out, plan.window), F32),
+                pltpu.VMEM((n, pix, c_out), BF16),
+                pltpu.VMEM((n, pix, 128), BF16),
+                pltpu.VMEM((n, pix, c_out), BF16),
                 pltpu.VMEM((max(plan.window, c_out), c_out), F32),
-                pltpu.VMEM((128, c_out), F32),
                 pltpu.VMEM((16, c_out), F32),
                 pltpu.VMEM((16, c_out), F32),
-                pltpu.VMEM((16, c_out), F32),
-                pltpu.VMEM((pix, 5 * c_out), BF16),
+                pltpu.VMEM((n, pix, 5 * c_out), BF16),
                 pltpu.VMEM((unit_rows, 3 * c_out), F32),
                 pltpu.VMEM((2, depth if last else 1, unit_rows, c_out), F32),
                 pltpu.SemaphoreType.DMA((2, depth)),
@@ -682,8 +690,23 @@
     common = (w_in, w_proj, wcls, class_weight)
     hops = list(range(1, n_bits)) + [0]
     rounds = n + n_bits - 1
-    up = down = x
     ups, downs = [x], [x]
+    turns = []
+    for t in range(1, rounds + 1):
+        turn = [(t - 1, 0)] if t - 1 < n else []
+        if t == rounds:
+            turn += [(q, 1) for q in range(max(0, n + 1 - n_bits), n)]
+        elif t >= n_bits and t <= n:
+            turn.append((t - n_bits, 1))
+        turns.append(turn)
+    metas = [
+        jnp.stack([
+            jnp.stack([(top if f else 0) + jnp.int32(n_bits * at if f and turn[0][1] else at),
+                       blocks[q], jnp.int32(f)])
+            for at, (q, f) in enumerate(turn)
+        ]) if turn else None
+        for turn in turns
+    ]
     values, moves = {0: x}, {q: [] for q in range(n)}
     state, grads = None, None
     for t in range(1, rounds + 1):
@@ -693,24 +716,21 @@
         for i in range(1, n_bits):
             if 0 <= q - i < n:
                 values[q - i] = jnp.where(bits[hops[i - 1]], moves[q - i][0], values[q - i])
+        for i in reversed(range(n_bits)):
+            if 0 <= q - i < n:
+                moves[q - i].insert(0, hop(values[q - i], hops[i]))
         if t < n:
             ups.append(along(ups[-1], 1, t))
             downs.append(along(downs[-1], -1, t))
-        for i in range(n_bits):
-            if 0 <= q - i < n:
-                moves[q - i].insert(0, hop(values[q - i], hops[i]))
-        slots = []
-        if q < n:
-            slots.append(([values[q]], (0, blocks[q], 0)))
-        if t >= n_bits:
-            at = t - n_bits
-            slots.append((moves[at], (top, blocks[at], 1)))
-        state = run_blocks(plan, slots, w_in, state)
+        slots = [moves[at] if f else [values[at]] for at, f in turns[q]]
+        if slots:
+            state = run_blocks(plan, slots, metas[q], w_in, state)
         if q == min(n, rounds - 1):
             grads = tuple(run_field(plan, 0, tab, state, *common, None))
         if t < rounds:
-            live = (ups, downs, values, moves, state, grads)
-            ups, downs, values, moves, state, grads = lax.optimization_barrier(live)
+            live = (ups, downs, values, moves, state, grads, metas, tab, wcls)
+            live = lax.optimization_barrier(live)
+            ups, downs, values, moves, state, grads, metas, tab, wcls = live
     avg_in, avg_proj, avg_cls = run_field(plan, 1, tab, state, *common, grads)
     return avg_in[None], avg_proj[None], avg_cls[None, :, :plan.classes]
 

time: 227 us -> 219 us (0.965)
  Pallas kernels: 132 us -> 126 us
  waiting for transfers between devices: 39.7 us -> 35.7 us
    ppermute x6, waiting for transfers between devices: 19.1 us -> 11 us  [along(): return lax.ppermute(value, 'space', pairs)]
    ppermute x12, waiting for transfers between devices: 20.6 us -> 24.7 us  [hop(): return lax.ppermute(value, 'rep', [(r, r ^ 1 << b) for r in range(reps)])]
    pallas_call x6 -> x5, Pallas kernels: 70 us -> 66.5 us  [run_blocks(): pl.pallas_call(functools.partial(block_kernel, plan, len(arrays), len(slo...]
    pallas_call x2, Pallas kernels: 59.3 us -> 56.7 us  [run_field(): pl.pallas_call(functools.partial(field_kernel, plan, last), grid_spec=plt...]
  transfers between devices with their start and end apart: 18 -> 18, of which waited for: 11 -> 9; matrix products, arithmetic and copies ran while one was open for 8% -> 10% of each run, Pallas kernels for 40% -> 36%
where the time goes in v2:
time: 219 us; the launch traced here: 217 us
  Pallas kernels  126 us (58%)
  waiting for transfers between devices  35.7 us (16%)
  starting transfers between devices  23.4 us (11%)
  other arithmetic  22 us (10%)
  local copies, waits for them, and re-layouts  7.17 us (3%)
  between operations  2.92 us (1%)
    pallas_call x5, Pallas kernels, run_blocks(): pl.pallas_call(functools.partial(block_kernel, plan, len(arrays), len(slo...  66.5 us
    pallas_call x2, Pallas kernels, run_field(): pl.pallas_call(functools.partial(field_kernel, plan, last), grid_spec=plt...  56.7 us
    ppermute x12, waiting for transfers between devices, hop(): return lax.ppermute(value, 'rep', [(r, r ^ 1 << b) for r in range(reps)])  24.7 us
    ppermute x6, starting transfers between devices, along(): return lax.ppermute(value, 'space', pairs)  13.2 us
    ppermute x6, waiting for transfers between devices, along(): return lax.ppermute(value, 'space', pairs)  11 us
    ppermute x12, starting transfers between devices, hop(): return lax.ppermute(value, 'rep', [(r, r ^ 1 << b) for r in range(reps)])  10.2 us
    select_n x8, other arithmetic, per_device(): values[q - i] = jnp.where(bits[hops[i - 1]], moves[q - i][0], values[q - i])  8.37 us
    another operation x7, other arithmetic, per_device(): jnp.stack([jnp.stack([(top if f else 0) + jnp.int32(n_bits * at if f and...  7.8 us
  transfers between devices with their start and end apart: 18, of which 9 were waited for; matrix products, arithmetic and copies ran while one was open for 10% of the time, Pallas kernels for 36%

profile of v2, /device:TPU:0, one launch (start us, length us, event | category | flops | bytes accessed | tf_op | source)
XLA Modules:
  0.0 216.7 jit_solution(116982286681958510)
XLA Ops:
  0.6 0.7 convert_reduce_fusion
  2.0 2.3 %pack.1.refs_0_ = bf16[496,1024]{1,0:T(8,128)(2,1)} custom-call(bf16[480,1024]{1,0:T(8,128)(2,1)} %bitcast.33, f32[1,1024]{1,0:T(1,128)} %pad.8.lab_ref), custom_call_target="tpu_custom_call" | custom-call | tf_op jit(solution)/shard_map/pack/pallas_call | solution.py:653
  4.3 5.9 %collective-permute-start = (bf16[496,1024]{1,0:T(8,128)(2,1)}, bf16[496,1024]{1,0:T(8,128)(2,1)}, u32[]{:S(2)}, u32[]{:S(2)}) collective-permute-start(bf16[496,1024]{1,0:T(8,128)(2,1)} %pack.1.refs_0_), channel_id=1, source_target_pairs={{0,8},{8,16},{16,24},{1,9},{9,17},{17,25},{2,10},{10,18},{18,26},{... | collective-permute-start | bytes 3047432 | tf_op jit(solution)/shard_map/ppermute | solution.py:672
  10.2 1.3 collective-permute-start.1
  11.5 1.6 collective-permute-start.2
  15.0 0.7 constant_dynamic-slice_fusion.1
  15.7 0.7 fusion.9
  16.4 2.0 fusion.5
  18.4 1.4 fusion.1
  19.8 0.8 copy.28
  20.6 0.6 pad.9.refs_16_
  21.3 1.3 constant_dynamic-slice_fusion
  22.5 1.4 fusion.7
  23.9 1.4 fusion.3
  26.9 10.4 %block_forward.5 = (bf16[2,4,1024,480]{3,2,1,0:T(8,128)(2,1)}, bf16[2,4,480,768]{3,2,1,0:T(8,128)(2,1)}, f32[3,2,20,96,256]{4,3,2,1,0:T(8,128)}, bf16[2,4,16,1024]{3,2,1,0:T(8,128)(2,1)}) custom-call(s32[1,3]{1,0:T(1,128)} %get-tuple-element.208.meta, bf16[496,1024]{1,0:T(8,128)(2,1)} %pack.1.refs_0_, bf16[29,1024,256]{2,1,0:T(8,128)(2,1)} %refs_14_.3), custom_call_target="tpu_custom_call" | custom-call | flops 4026531840 | bytes 40000000 | tf_op jit(solution)/shard_map/block_forward/pallas_call | solution.py:277
  37.3 2.0 select_select_fusion.1.refs_0_
  40.0 1.1 broadcast_select_fusion.3
  41.0 1.5 collective-permute-start.5
  42.5 1.6 collective-permute-start.3
  44.2 1.3 collective-permute-start.4
  45.5 10.2 %block_forward.6 = (bf16[2,4,1024,480]{3,2,1,0:T(8,128)(2,1)}, bf16[2,4,480,768]{3,2,1,0:T(8,128)(2,1)}, f32[3,2,20,96,256]{4,3,2,1,0:T(8,128)}, bf16[2,4,16,1024]{3,2,1,0:T(8,128)(2,1)}) custom-call(s32[1,3]{1,0:T(1,128)} %get-tuple-element.108.meta, ...), custom_call_target="tpu_custom_call", output_to_operand_aliasing={{0}: (3, {}), {1}: (4, {}), {2}: (5, {}), {3}: (6, {})} | custom-call | flops 4026531840 | bytes 40000000 | tf_op jit(solution)/shard_map/block_forward/pallas_call | solution.py:277
  55.7 7.3 %collective-permute-done.6.refs_3_ = bf16[496,1024]{1,0:T(8,128)(2,1)S(1)} collective-permute-done((bf16[496,1024]{1,0:T(8,128)(2,1)S(1)}, bf16[496,1024]{1,0:T(8,128)(2,1)S(1)}, u32[]{:S(2)}, u32[]{:S(2)}) %collective-permute-start.6) | collective-permute-done | bytes 1015840 | tf_op jit(solution)/shard_map/ppermute | solution.py:675
  63.1 1.5 collective-permute-done.5.refs_2_
  64.6 7.1 %collective-permute-done.4 = bf16[496,1024]{1,0:T(8,128)(2,1)} collective-permute-done((bf16[496,1024]{1,0:T(8,128)(2,1)}, bf16[496,1024]{1,0:T(8,128)(2,1)}, u32[]{:S(2)}, u32[]{:S(2)}) %collective-permute-start.4) | collective-permute-done | bytes 1015840 | tf_op jit(solution)/shard_map/ppermute | solution.py:672
  71.9 1.7 fusion.refs_0_
  73.6 1.6 collective-permute-start.11
  75.1 2.3 %broadcast_select_fusion.2 = bf16[496,1024]{1,0:T(8,128)(2,1)} fusion(bf16[496,1024]{1,0:T(8,128)(2,1)S(1)} %collective-permute-done.6.refs_3_, bf16[496,1024]{1,0:T(8,128)(2,1)} %copy-done.2, pred[]{:T(512)} %bitcast.9), kind=kLoop, calls=%fused_computation.6 | loop fusion | flops 507904 | bytes 3047425 | tf_op jit(solution)/shard_map/jit(_where)/select_n | solution.py:718
  77.9 1.7 collective-permute-start.7
  79.6 1.5 collective-permute-start.8
  81.1 15.4 %block_forward.7 = (bf16[2,4,1024,480]{3,2,1,0:T(8,128)(2,1)}, bf16[2,4,480,768]{3,2,1,0:T(8,128)(2,1)}, f32[3,2,20,96,256]{4,3,2,1,0:T(8,128)}, bf16[2,4,16,1024]{3,2,1,0:T(8,128)(2,1)}) custom-call(s32[2,3]{1,0:T(2,128)} %pad_add_fusion.meta, bf16[496,1024]{1,0:T(8,128)(2,1)} %copy-done, ...), custom_call_target="tpu_custom_call", output_to_operand_aliasing={{0}: (6, {}), {1}: (7, {}), {2}: (8, {}), {3}: (9, {})} | custom-call | flops 8053063680 | bytes 60000000 | tf_op jit(solution)/shard_map/block_forward/pallas_call | solution.py:277
  96.5 1.9 collective-permute-done.11.refs_2_
  98.5 3.7 %collective-permute-done.10.refs_2_ = bf16[496,1024]{1,0:T(8,128)(2,1)S(1)} collective-permute-done((bf16[496,1024]{1,0:T(8,128)(2,1)}, bf16[496,1024]{1,0:T(8,128)(2,1)S(1)}, u32[]{:S(2)}, u32[]{:S(2)}) %collective-permute-start.10) | collective-permute-done | bytes 1015840 | tf_op jit(solution)/shard_map/ppermute | solution.py:675
  102.2 3.9 %collective-permute-done.8 = bf16[496,1024]{1,0:T(8,128)(2,1)} collective-permute-done((bf16[496,1024]{1,0:T(8,128)(2,1)}, bf16[496,1024]{1,0:T(8,128)(2,1)}, u32[]{:S(2)}, u32[]{:S(2)}) %collective-permute-start.8) | collective-permute-done | bytes 1015840 | tf_op jit(solution)/shard_map/ppermute | solution.py:672
  106.2 1.4 select_select_fusion.2.refs_0_
  108.3 1.1 broadcast_select_fusion.1
  109.4 1.5 collective-permute-start.13
  110.9 15.4 %block_forward.8 = (bf16[2,4,1024,480]{3,2,1,0:T(8,128)(2,1)}, bf16[2,4,480,768]{3,2,1,0:T(8,128)(2,1)}, f32[3,2,20,96,256]{4,3,2,1,0:T(8,128)}, bf16[2,4,16,1024]{3,2,1,0:T(8,128)(2,1)}) custom-call(s32[2,3]{1,0:T(2,128)} %pad_add_fusion.1.meta, ...), custom_call_target="tpu_custom_call", output_to_operand_aliasing={{0}: (6, {}), {1}: (7, {}), {2}: (8, {}), {3}: (9, {})} | custom-call | flops 8053063680 | bytes 60000000 | tf_op jit(solution)/shard_map/block_forward/pallas_call | solution.py:277
  126.3 6.2 %collective-permute-done.14.refs_5_ = bf16[496,1024]{1,0:T(8,128)(2,1)S(1)} collective-permute-done((bf16[496,1024]{1,0:T(8,128)(2,1)S(1)}, bf16[496,1024]{1,0:T(8,128)(2,1)S(1)}, u32[]{:S(2)}, u32[]{:S(2)}) %collective-permute-start.14) | collective-permute-done | bytes 1015840 | tf_op jit(solution)/shard_map/ppermute | solution.py:675
  132.6 1.7 collective-permute-done.13.refs_1_
  134.3 1.3 broadcast_select_fusion
  135.6 1.6 collective-permute-start.16
  137.2 2.3 %broadcast_select_fusion.5 = bf16[496,1024]{1,0:T(8,128)(2,1)} fusion(bf16[496,1024]{1,0:T(8,128)(2,1)} %collective-permute-done.13.refs_1_, bf16[496,1024]{1,0:T(8,128)(2,1)} %broadcast_select_fusion.1, pred[]{:T(512)} %bitcast), kind=kLoop, calls=%fused_computation.9 | loop fusion | flops 507904 | bytes 3047425 | tf_op jit(solution)/shard_map/jit(_where)/select_n | solution.py:718
  139.4 27.5 %field_grads.2 = (bf16[4,8,256,256]{3,2,1,0:T(8,128)(2,1)}, bf16[320,256]{1,0:T(8,128)(2,1)}, bf16[64,128]{1,0:T(8,128)(2,1)}) custom-call(s32[210]{0:T(256)} %bitcast.34, bf16[2,4,480,768]{3,2,1,0:T(8,128)(2,1)} %get-tuple-element.184.refs_0_.refs_8_, ...), custom_call_target="tpu_custom_call" | custom-call | flops 10000000000 | bytes 90000000 | tf_op jit(solution)/shard_map/field_grads/pallas_call | solution.py:608
  167.7 2.2 %collective-permute-done.17.refs_3_ = bf16[496,1024]{1,0:T(8,128)(2,1)S(1)} collective-permute-done((bf16[496,1024]{1,0:T(8,128)(2,1)S(1)}, bf16[496,1024]{1,0:T(8,128)(2,1)S(1)}, u32[]{:S(2)}, u32[]{:S(2)}) %collective-permute-start.17) | collective-permute-done | bytes 1015840 | tf_op jit(solution)/shard_map/ppermute | solution.py:675
  170.0 1.0 copy-done.13
  170.9 15.1 %block_forward.9 = (bf16[2,4,1024,480]{3,2,1,0:T(8,128)(2,1)}, bf16[2,4,480,768]{3,2,1,0:T(8,128)(2,1)}, f32[3,2,20,96,256]{4,3,2,1,0:T(8,128)}, bf16[2,4,16,1024]{3,2,1,0:T(8,128)(2,1)}) custom-call(s32[2,3]{1,0:T(2,128)} %pad_add_fusion.2.meta, ...), custom_call_target="tpu_custom_call", output_to_operand_aliasing={{0}: (8, {}), {1}: (9, {}), {2}: (10, {}), {3}: (11, {})} | custom-call | flops 8053063680 | bytes 60000000 | tf_op jit(solution)/shard_map/block_forward/pallas_call | solution.py:277
  186.1 29.2 %field_grads.3 = (f32[7424,256]{1,0:T(8,128)}, f32[320,256]{1,0:T(8,128)}, f32[64,128]{1,0:T(8,128)}) custom-call(s32[210]{0:T(256)} %bitcast.35, bf16[2,4,480,768]{3,2,1,0:T(8,128)(2,1)} %get-tuple-element.187.refs_0_, f32[3,2,20,96,256]{4,3,2,1,0:T(8,128)} %get-tuple-element.188.refs_1_.refs_2_.refs_3_.refs_4_.refs_5_.refs_6_.refs_7_.refs_8_.refs_9_.refs_10_.refs_11_, ...), custom_call_target="tpu_custom_call" | custom-call | flops 10000000000 | bytes 90000000 | tf_op jit(solution)/shard_map/field_grads/pallas_call | solution.py:608
  215.3 0.8 slice_bitcast_fusion
  (52 shorter events, 5.8 us)
Async XLA Ops:
  4.3 32.9 %collective-permute-start = (bf16[496,1024]{1,0:T(8,128)(2,1)}, bf16[496,1024]{1,0:T(8,128)(2,1)}, u32[]{:S(2)}, u32[]{:S(2)}) collective-permute-start(bf16[496,1024]{1,0:T(8,128)(2,1)} %pack.1.refs_0_), channel_id=1, source_target_pairs={{0,8},{8,16},{16,24},{1,9},{9,17},{17,25},{2,10},{10,18},{18,26},{... | collective-permute-start | bytes 3047432 | tf_op jit(solution)/shard_map/ppermute | solution.py:672
  10.2 27.1 %collective-permute-start.1 = (bf16[496,1024]{1,0:T(8,128)(2,1)}, bf16[496,1024]{1,0:T(8,128)(2,1)}, u32[]{:S(2)}, u32[]{:S(2)}) collective-permute-start(bf16[496,1024]{1,0:T(8,128)(2,1)} %pack.1.refs_0_), channel_id=1, source_target_pairs={{8,0},{16,8},{24,16},{9,1},{17,9},{25,17},{10,2},{18,10},{26,18},{... | collective-permute-start | bytes 3047432 | tf_op jit(solution)/shard_map/ppermute | solution.py:672
  11.5 25.8 %collective-permute-start.2 = (bf16[496,1024]{1,0:T(8,128)(2,1)}, bf16[496,1024]{1,0:T(8,128)(2,1)S(1)}, u32[]{:S(2)}, u32[]{:S(2)}) collective-permute-start(bf16[496,1024]{1,0:T(8,128)(2,1)} %pack.1.refs_0_), channel_id=1, source_target_pairs={{0,2},{1,3},{2,0},{3,1},{4,6},{5,7},{6,4},{7,5},{8,10},{9,11},{10,... | collective-permute-start | bytes 3047432 | tf_op jit(solution)/shard_map/ppermute | solution.py:675
  26.9 13.0 %copy-start.4 = (bf16[496,1024]{1,0:T(8,128)(2,1)S(1)}, bf16[496,1024]{1,0:T(8,128)(2,1)}, u32[]{:S(2)}) copy-start(bf16[496,1024]{1,0:T(8,128)(2,1)} %pack.1.refs_0_) | copy-start | bytes 3047428
  37.3 18.4 %copy-start.5 = (bf16[496,1024]{1,0:T(8,128)(2,1)}, bf16[496,1024]{1,0:T(8,128)(2,1)S(1)}, u32[]{:S(2)}) copy-start(bf16[496,1024]{1,0:T(8,128)(2,1)S(1)} %collective-permute-done.2.refs_3_) | copy-start | bytes 3047428
  39.3 6.1 %copy-start.2 = (bf16[496,1024]{1,0:T(8,128)(2,1)}, bf16[496,1024]{1,0:T(8,128)(2,1)S(1)}, u32[]{:S(2)}) copy-start(bf16[496,1024]{1,0:T(8,128)(2,1)S(1)} %select_select_fusion.1.refs_0_) | copy-start | bytes 3047428
  39.3 23.7 %collective-permute-start.6 = (bf16[496,1024]{1,0:T(8,128)(2,1)S(1)}, bf16[496,1024]{1,0:T(8,128)(2,1)S(1)}, u32[]{:S(2)}, u32[]{:S(2)}) collective-permute-start(bf16[496,1024]{1,0:T(8,128)(2,1)S(1)} %select_select_fusion.1.refs_0_), channel_id=1, source_target_pairs={{0,2},{1,3},{2,0},{3,1},{4,6},{5,7},{6,4},{7,5},{8,10},{9,11},{10,... | collective-permute-start | bytes 3047432 | tf_op jit(solution)/shard_map/ppermute | solution.py:675
  41.0 23.6 %collective-permute-start.5 = (bf16[496,1024]{1,0:T(8,128)(2,1)}, bf16[496,1024]{1,0:T(8,128)(2,1)S(1)}, u32[]{:S(2)}, u32[]{:S(2)}) collective-permute-start(bf16[496,1024]{1,0:T(8,128)(2,1)} %broadcast_select_fusion.3), channel_id=1, source_target_pairs={{0,4},{1,5},{2,6},{3,7},{4,0},{5,1},{6,2},{7,3},{8,12},{9,13},{10,... | collective-permute-start | bytes 3047432 | tf_op jit(solution)/shard_map/ppermute | solution.py:675
  42.5 22.0 %collective-permute-start.3 = (bf16[496,1024]{1,0:T(8,128)(2,1)}, bf16[496,1024]{1,0:T(8,128)(2,1)}, u32[]{:S(2)}, u32[]{:S(2)}) collective-permute-start(bf16[496,1024]{1,0:T(8,128)(2,1)} %collective-permute-done), channel_id=1, source_target_pairs={{8,16},{16,24},{9,17},{17,25},{10,18},{18,26},{11,19},{19,27},{12,... | collective-permute-start | bytes 3047432 | tf_op jit(solution)/shard_map/ppermute | solution.py:672
  44.2 27.5 %collective-permute-start.4 = (bf16[496,1024]{1,0:T(8,128)(2,1)}, bf16[496,1024]{1,0:T(8,128)(2,1)}, u32[]{:S(2)}, u32[]{:S(2)}) collective-permute-start(bf16[496,1024]{1,0:T(8,128)(2,1)} %collective-permute-done.1), channel_id=1, source_target_pairs={{8,0},{16,8},{9,1},{17,9},{10,2},{18,10},{11,3},{19,11},{12,4},{20... | collective-permute-start | bytes 3047432 | tf_op jit(solution)/shard_map/ppermute | solution.py:672
  63.1 33.4 %copy-start.7 = (bf16[496,1024]{1,0:T(8,128)(2,1)}, bf16[496,1024]{1,0:T(8,128)(2,1)S(1)}, u32[]{:S(2)}) copy-start(bf16[496,1024]{1,0:T(8,128)(2,1)S(1)} %collective-permute-done.6.refs_3_) | copy-start | bytes 3047428
  64.6 7.3 %copy-start.10 = (bf16[496,1024]{1,0:T(8,128)(2,1)}, bf16[496,1024]{1,0:T(8,128)(2,1)S(1)}, u32[]{:S(2)}) copy-start(bf16[496,1024]{1,0:T(8,128)(2,1)S(1)} %collective-permute-done.5.refs_2_) | copy-start | bytes 3047428
  71.8 9.3 %collective-permute-start.9 = (bf16[496,1024]{1,0:T(8,128)(2,1)S(1)}, bf16[496,1024]{1,0:T(8,128)(2,1)}, u32[]{:S(2)}, u32[]{:S(2)}) collective-permute-start(bf16[496,1024]{1,0:T(8,128)(2,1)S(1)} %broadcast_select_fusion.7), channel_id=1, source_target_pairs={{0,1},{1,0},{2,3},{3,2},{4,5},{5,4},{6,7},{7,6},{8,9},{9,8},{10,11... | collective-permute-start | bytes 3047432 | tf_op jit(solution)/shard_map/ppermute | solution.py:675
  73.5 7.5 %copy-start = (bf16[496,1024]{1,0:T(8,128)(2,1)}, bf16[496,1024]{1,0:T(8,128)(2,1)S(1)}, u32[]{:S(2)}) copy-start(bf16[496,1024]{1,0:T(8,128)(2,1)S(1)} %fusion.refs_0_) | copy-start | bytes 3047428
  73.6 24.9 %collective-permute-start.11 = (bf16[496,1024]{1,0:T(8,128)(2,1)S(1)}, bf16[496,1024]{1,0:T(8,128)(2,1)S(1)}, u32[]{:S(2)}, u32[]{:S(2)}) collective-permute-start(bf16[496,1024]{1,0:T(8,128)(2,1)S(1)} %fusion.refs_0_), channel_id=1, source_target_pairs={{0,2},{1,3},{2,0},{3,1},{4,6},{5,7},{6,4},{7,5},{8,10},{9,11},{10,... | collective-permute-start | bytes 3047432 | tf_op jit(solution)/shard_map/ppermute | solution.py:675
  77.4 24.8 %collective-permute-start.10 = (bf16[496,1024]{1,0:T(8,128)(2,1)}, bf16[496,1024]{1,0:T(8,128)(2,1)S(1)}, u32[]{:S(2)}, u32[]{:S(2)}) collective-permute-start(bf16[496,1024]{1,0:T(8,128)(2,1)} %broadcast_select_fusion.2), channel_id=1, source_target_pairs={{0,4},{1,5},{2,6},{3,7},{4,0},{5,1},{6,2},{7,3},{8,12},{9,13},{10,... | collective-permute-start | bytes 3047432 | tf_op jit(solution)/shard_map/ppermute | solution.py:675
  77.9 24.3 %collective-permute-start.7 = (bf16[496,1024]{1,0:T(8,128)(2,1)}, bf16[496,1024]{1,0:T(8,128)(2,1)}, u32[]{:S(2)}, u32[]{:S(2)}) collective-permute-start(bf16[496,1024]{1,0:T(8,128)(2,1)} %collective-permute-done.3), channel_id=1, source_target_pairs={{16,24},{17,25},{18,26},{19,27},{20,28},{21,29},{22,30},{23,31}} | collective-permute-start | bytes 3047432 | tf_op jit(solution)/shard_map/ppermute | solution.py:672
  79.6 26.5 %collective-permute-start.8 = (bf16[496,1024]{1,0:T(8,128)(2,1)}, bf16[496,1024]{1,0:T(8,128)(2,1)}, u32[]{:S(2)}, u32[]{:S(2)}) collective-permute-start(bf16[496,1024]{1,0:T(8,128)(2,1)} %collective-permute-done.4), channel_id=1, source_target_pairs={{8,0},{9,1},{10,2},{11,3},{12,4},{13,5},{14,6},{15,7}} | collective-permute-start | bytes 3047432 | tf_op jit(solution)/shard_map/ppermute | solution.py:672
  96.5 11.8 %copy-start.1 = (bf16[496,1024]{1,0:T(8,128)(2,1)S(1)}, bf16[496,1024]{1,0:T(8,128)(2,1)}, u32[]{:S(2)}) copy-start(bf16[496,1024]{1,0:T(8,128)(2,1)} %copy-done) | copy-start | bytes 3047428
  98.5 27.9 %copy-start.6 = (bf16[496,1024]{1,0:T(8,128)(2,1)}, bf16[496,1024]{1,0:T(8,128)(2,1)S(1)}, u32[]{:S(2)}) copy-start(bf16[496,1024]{1,0:T(8,128)(2,1)S(1)} %collective-permute-done.11.refs_2_) | copy-start | bytes 3047428
  102.2 8.7 %copy-start.8 = (bf16[496,1024]{1,0:T(8,128)(2,1)}, bf16[496,1024]{1,0:T(8,128)(2,1)S(1)}, u32[]{:S(2)}) copy-start(bf16[496,1024]{1,0:T(8,128)(2,1)S(1)} %collective-permute-done.10.refs_2_) | copy-start | bytes 3047428
  106.2 4.8 %collective-permute-start.12 = (bf16[496,1024]{1,0:T(8,128)(2,1)S(1)}, bf16[496,1024]{1,0:T(8,128)(2,1)}, u32[]{:S(2)}, u32[]{:S(2)}) collective-permute-start(bf16[496,1024]{1,0:T(8,128)(2,1)S(1)} %broadcast_select_fusion.6), channel_id=1, source_target_pairs={{0,1},{1,0},{2,3},{3,2},{4,5},{5,4},{6,7},{7,6},{8,9},{9,8},{10,11... | collective-permute-start | bytes 3047432 | tf_op jit(solution)/shard_map/ppermute | solution.py:675
  107.7 3.3 %copy-start.3 = (bf16[496,1024]{1,0:T(8,128)(2,1)}, bf16[496,1024]{1,0:T(8,128)(2,1)S(1)}, u32[]{:S(2)}) copy-start(bf16[496,1024]{1,0:T(8,128)(2,1)S(1)} %select_select_fusion.2.refs_0_) | copy-start | bytes 3047428
  107.7 24.9 %collective-permute-start.14 = (bf16[496,1024]{1,0:T(8,128)(2,1)S(1)}, bf16[496,1024]{1,0:T(8,128)(2,1)S(1)}, u32[]{:S(2)}, u32[]{:S(2)}) collective-permute-start(bf16[496,1024]{1,0:T(8,128)(2,1)S(1)} %select_select_fusion.2.refs_0_), channel_id=1, source_target_pairs={{0,2},{1,3},{2,0},{3,1},{4,6},{5,7},{6,4},{7,5},{8,10},{9,11},{10,... | collective-permute-start | bytes 3047432 | tf_op jit(solution)/shard_map/ppermute | solution.py:675
  109.4 24.9 %collective-permute-start.13 = (bf16[496,1024]{1,0:T(8,128)(2,1)}, bf16[496,1024]{1,0:T(8,128)(2,1)}, u32[]{:S(2)}, u32[]{:S(2)}) collective-permute-start(bf16[496,1024]{1,0:T(8,128)(2,1)} %broadcast_select_fusion.1), channel_id=1, source_target_pairs={{0,4},{1,5},{2,6},{3,7},{4,0},{5,1},{6,2},{7,3},{8,12},{9,13},{10,... | collective-permute-start | bytes 3047432 | tf_op jit(solution)/shard_map/ppermute | solution.py:675
  132.6 34.4 %copy-start.9 = (bf16[496,1024]{1,0:T(8,128)(2,1)}, bf16[496,1024]{1,0:T(8,128)(2,1)S(1)}, u32[]{:S(2)}) copy-start(bf16[496,1024]{1,0:T(8,128)(2,1)S(1)} %collective-permute-done.14.refs_5_) | copy-start | bytes 3047428
  135.6 31.4 %collective-permute-start.16 = (bf16[496,1024]{1,0:T(8,128)(2,1)S(1)}, bf16[496,1024]{1,0:T(8,128)(2,1)S(1)}, u32[]{:S(2)}, u32[]{:S(2)}) collective-permute-start(bf16[496,1024]{1,0:T(8,128)(2,1)S(1)} %broadcast_select_fusion), channel_id=1, source_target_pairs={{0,4},{1,5},{2,6},{3,7},{4,0},{5,1},{6,2},{7,3},{8,12},{9,13},{10,... | collective-permute-start | bytes 3047432 | tf_op jit(solution)/shard_map/ppermute | solution.py:675
  139.4 27.6 %collective-permute-start.15 = (bf16[496,1024]{1,0:T(8,128)(2,1)}, bf16[496,1024]{1,0:T(8,128)(2,1)S(1)}, u32[]{:S(2)}, u32[]{:S(2)}) collective-permute-start(bf16[496,1024]{1,0:T(8,128)(2,1)} %broadcast_select_fusion.5), channel_id=1, source_target_pairs={{0,1},{1,0},{2,3},{3,2},{4,5},{5,4},{6,7},{7,6},{8,9},{9,8},{10,11... | collective-permute-start | bytes 3047432 | tf_op jit(solution)/shard_map/ppermute | solution.py:675
  167.0 3.0 %copy-start.11 = (bf16[496,1024]{1,0:T(8,128)(2,1)}, bf16[496,1024]{1,0:T(8,128)(2,1)S(1)}, u32[]{:S(2)}) copy-start(bf16[496,1024]{1,0:T(8,128)(2,1)S(1)} %collective-permute-done.16.refs_4_) | copy-start | bytes 3047428
  167.0 2.9 %copy-start.12 = (bf16[496,1024]{1,0:T(8,128)(2,1)}, bf16[496,1024]{1,0:T(8,128)(2,1)S(1)}, u32[]{:S(2)}) copy-start(bf16[496,1024]{1,0:T(8,128)(2,1)S(1)} %collective-permute-done.15.refs_0_) | copy-start | bytes 3047428
  167.2 2.8 %collective-permute-start.17 = (bf16[496,1024]{1,0:T(8,128)(2,1)S(1)}, bf16[496,1024]{1,0:T(8,128)(2,1)S(1)}, u32[]{:S(2)}, u32[]{:S(2)}) collective-permute-start(bf16[496,1024]{1,0:T(8,128)(2,1)S(1)} %broadcast_select_fusion.4), channel_id=1, source_target_pairs={{0,1},{1,0},{2,3},{3,2},{4,5},{5,4},{6,7},{7,6},{8,9},{9,8},{10,11... | collective-permute-start | bytes 3047432 | tf_op jit(solution)/shard_map/ppermute | solution.py:675
  170.0 1.0 copy-start.13

commit v3 on v2

--- a/solution.py
+++ b/solution.py
@@ -14,8 +14,8 @@
 EXTRA = 16
 BF16 = jnp.bfloat16
 F32 = jnp.float32
-BLOCK_VMEM = 60 * 1024 * 1024
-FIELD_VMEM = 60 * 1024 * 1024
+BLOCK_VMEM = 50 * 1024 * 1024
+FIELD_VMEM = 50 * 1024 * 1024
 
 
 def nn(a, b):
@@ -24,6 +24,10 @@
 
 def nt(a, b):
     return lax.dot_general(a, b, (((1,), (1,)), ((), ())), preferred_element_type=F32)
+
+
+def tn(a, b):
+    return lax.dot_general(a, b, (((0,), (0,)), ((), ())), preferred_element_type=F32)
 
 
 def identity(size):
@@ -308,7 +312,7 @@
     )(meta, *operands)
 
 
-def field_kernel(plan, last, tab, *refs):
+def field_kernel(plan, field, last, tab, *refs):
     n, rows, cols, pix = plan.n, plan.rows, plan.cols, plan.pix
     c_in, c_out, n_sh = plan.c_in, plan.c_out, plan.n_sh
     n_rows_in = 2 * n_sh * rows
@@ -317,13 +321,15 @@
     mid_refs = refs[1:1 + n_sh]
     s_refs = refs[1 + n_sh:1 + n_sh + n_rows_in]
     refs = refs[1 + n_sh + n_rows_in:]
-    aux_ref, all_ref, w28_ref, wproj_ref, wcls_ref, cw_ref, xt_ref = refs[:7]
+    aux_ref, all_ref, w28_ref, wproj_ref, wcls_ref, cw_ref, xt_hbm = refs[:7]
     refs = refs[7:]
     if last:
         prev_g, prev_p, prev_c = refs[:3]
         refs = refs[3:]
     g_out, p_out, c_ref_out = refs[:3]
-    (dbuf, pad, mean, ybuf, lbuf, dybuf, gp, spool, pact, catall, acc, stage, sems) = refs[3:]
+    (dbuf, pad, mean, ybuf, lbuf, dybuf, gp, spool, pact, catall, acc, stage, xt_ref, sem_xt,
+     sems) = refs[3:]
+    xt_copy = pltpu.make_async_copy(xt_hbm.at[field], xt_ref, sem_xt)
     step = pl.program_id(0)
     edge_rows = rows - 1
 
@@ -335,6 +341,7 @@
 
     @pl.when(step == 0)
     def _():
+        xt_copy.start()
         zero = jnp.zeros((edge_rows, cols, dbuf.shape[2]), BF16)
         dbuf[:edge_rows] = zero
         dbuf[edge_rows + plan.height:] = zero
@@ -373,21 +380,20 @@
         cat5[:, 4 * c_out:] = jnp.broadcast_to(pool_act, (pix, c_out))
         y_pre = nn(cat5[...], wproj_ref[...])
         y_act = jnp.maximum(y_pre, 0.0).astype(BF16)
-        logits = nn(y_act, wcls_ref[...])
-        lane = lax.broadcasted_iota(jnp.int32, (pix, 128), 1)
-        live = lane < plan.classes
+        logits = nt(wcls_ref[...], y_act)
+        row = lax.broadcasted_iota(jnp.int32, (16, pix), 0)
+        live = row < plan.classes
         expo = jnp.where(live, jnp.exp(logits), 0.0)
-        prob = expo / jnp.sum(expo, axis=1, keepdims=True)
-        names = aux_ref[3:4, :512].astype(F32)
-        label = jnp.broadcast_to(names, (128, 512)).T[:pix]
-        onehot = jnp.where(label == lane.astype(F32), 1.0, 0.0)
-        weight = jnp.zeros((pix, 128), F32)
+        prob = expo / jnp.sum(expo, axis=0, keepdims=True)
+        label = jnp.broadcast_to(aux_ref[3:4, :pix].astype(F32), (16, pix))
+        onehot = jnp.where(label == row.astype(F32), 1.0, 0.0)
+        weight = jnp.zeros((16, pix), F32)
         for c in range(plan.classes):
             weight = jnp.where(label == float(c), cw_ref[c], weight)
         d_logits = jnp.where(
             live, (prob - onehot) * weight * (LOSS_SCALE / plan.total), 0.0
         ).astype(BF16)
-        d_y = jnp.where(y_pre > 0, nt(d_logits, wcls_ref[...]), 0.0).astype(BF16)
+        d_y = jnp.where(y_pre > 0, tn(d_logits, wcls_ref[...]), 0.0).astype(BF16)
         ybuf[block] = y_act
         lbuf[block] = d_logits
         dybuf[block] = d_y
@@ -429,17 +435,17 @@
         spool[...] = jnp.where(pact[...] > 0, jnp.broadcast_to(total[0:1, :], total.shape), 0.0)
         window = pl.ds(pl.multiple_of(tab[flags + n + 13], 128), plan.window)
         g_proj = jnp.zeros((c_out, plan.window), F32)
-        g_cls = jnp.zeros((128, c_out), F32)
+        g_cls = jnp.zeros((16, c_out), F32)
         for j in range(n):
             g_proj = g_proj + nn(
                 nt(identity(c_out), dybuf[j]).astype(BF16), catall[j, :, window]
             )
-            g_cls = g_cls + nn(nt(identity(128), lbuf[j]).astype(BF16), ybuf[j])
+            g_cls = g_cls + nn(lbuf[j], ybuf[j])
         gp[:plan.window, :] = g_proj.T
         index = tab[flags + n + 12]
         first = pl.multiple_of(index * plan.proj_rows - tab[flags + n + 13], 32)
         p_out[...] = finish(gp[pl.ds(first, plan.proj_rows), :], prev_p[...] if last else None)
-        gp[:c_out, :128] = g_cls.T
+        gp[:c_out, :128] = jnp.concatenate([g_cls, jnp.zeros((112, c_out), F32)], axis=0).T
         first = pl.multiple_of(index * plan.cls_rows, plan.cls_rows)
         c_ref_out[...] = finish(
             gp[pl.ds(first, plan.cls_rows), :128], prev_c[...] if last else None
@@ -453,10 +459,15 @@
             sems.at[slot, t],
         )
 
+    @pl.when(step == n)
+    def _():
+        xt_copy.wait()
+
     @pl.when(step >= n)
     def _():
         part = step - n
         parity = lax.rem(part, 2)
+        mine = pl.ds(pl.multiple_of(part * unit_rows, unit_rows), unit_rows)
 
         def one(t, _):
             base = (part * depth + t) * 6
@@ -469,7 +480,7 @@
 
                 def term(j):
                     first = j * rows - move + edge_rows
-                    return nn(xt_ref[j], dbuf[pl.ds(first, rows), :, lanes].reshape(pix, width))
+                    return nn(xt_ref[j, mine, :], dbuf[pl.ds(first, rows), :, lanes].reshape(pix, width))
 
                 whole = jnp.logical_and(low == 0, high == n)
 
@@ -586,9 +597,9 @@
         pl.BlockSpec((None, n, EXTRA, c_in), lambda i, t: (field, 0, 0, 0)),
         pl.BlockSpec((1, c_in, c_out), lambda i, t: (28, 0, 0)),
         pl.BlockSpec((5 * c_out, c_out), lambda i, t: (0, 0)),
-        pl.BlockSpec((c_out, 128), lambda i, t: (0, 0)),
+        pl.BlockSpec((16, c_out), lambda i, t: (0, 0)),
         pl.BlockSpec(memory_space=pltpu.SMEM),
-        pl.BlockSpec((None, n, unit_rows, pix), lambda i, t: (field, 0, part(i), 0)),
+        pl.BlockSpec(memory_space=pl.ANY),
     ]
     operands += [aux, aux, w_in, w_proj, wcls, cw, xt]
     kind = F32 if last else BF16
@@ -606,7 +617,7 @@
         main_spec = inner
         main_shape = jax.ShapeDtypeStruct((n, depth, unit_rows, c_out), BF16)
     return pl.pallas_call(
-        functools.partial(field_kernel, plan, last),
+        functools.partial(field_kernel, plan, field, last),
         grid_spec=pltpu.PrefetchScalarGridSpec(
             num_scalar_prefetch=1,
             grid=(2 * n,),
@@ -617,7 +628,7 @@
                 pltpu.VMEM((rows, cols + 2 * EDGE, c_out), F32),
                 pltpu.VMEM((16, c_in), F32),
                 pltpu.VMEM((n, pix, c_out), BF16),
-                pltpu.VMEM((n, pix, 128), BF16),
+                pltpu.VMEM((n, 16, pix), BF16),
                 pltpu.VMEM((n, pix, c_out), BF16),
                 pltpu.VMEM((max(plan.window, c_out), c_out), F32),
                 pltpu.VMEM((16, c_out), F32),
@@ -625,6 +636,8 @@
                 pltpu.VMEM((n, pix, 5 * c_out), BF16),
                 pltpu.VMEM((unit_rows, 3 * c_out), F32),
                 pltpu.VMEM((2, depth if last else 1, unit_rows, c_out), F32),
+                pltpu.VMEM((n, c_in, pix), BF16),
+                pltpu.SemaphoreType.DMA,
                 pltpu.SemaphoreType.DMA((2, depth)),
             ],
         ),
@@ -662,7 +675,7 @@
     for at, b in enumerate(list(range(1, n_bits)) + [0]):
         top = jnp.where(bits[b], n_bits - 1 - at, top)
     tab = jnp.asarray(plan.tables)[here]
-    wcls = jnp.pad(w_cls, ((0, 0), (0, 128 - plan.classes)))
+    wcls = jnp.pad(w_cls.T, ((0, 16 - plan.classes), (0, 0)))
 
     def along(value, way, step):
         pairs = [
@@ -690,7 +703,7 @@
     common = (w_in, w_proj, wcls, class_weight)
     hops = list(range(1, n_bits)) + [0]
     rounds = n + n_bits - 1
-    ups, downs = [x], [x]
+    ups, downs, raw = [x], [x], (x, x)
     turns = []
     for t in range(1, rounds + 1):
         turn = [(t - 1, 0)] if t - 1 < n else []
@@ -720,8 +733,9 @@
             if 0 <= q - i < n:
                 moves[q - i].insert(0, hop(values[q - i], hops[i]))
         if t < n:
-            ups.append(along(ups[-1], 1, t))
-            downs.append(along(downs[-1], -1, t))
+            raw = along(raw[0], 1, t), along(raw[1], -1, t)
+            ups.append(raw[0])
+            downs.append(raw[1])
         slots = [moves[at] if f else [values[at]] for at, f in turns[q]]
         if slots:
             state = run_blocks(plan, slots, metas[q], w_in, state)

time: 219 us -> 195 us (0.89); the launches traced: 217 us -> 195 us
  other arithmetic: 22 us -> 7.66 us
  Pallas kernels: 126 us -> 112 us
  waiting for transfers between devices: 35.7 us -> 44.3 us
    pallas_call x5, Pallas kernels: 66.5 us -> 56.3 us  [run_blocks(): pl.pallas_call(functools.partial(block_kernel, plan, len(arrays), len(slo...]
    select_n x8, other arithmetic: 8.37 us -> 0.95 us  [per_device(): values[q - i] = jnp.where(bits[hops[i - 1]], moves[q - i][0], values[q - i])]
    ppermute x12, waiting for transfers between devices: 24.7 us -> 31.4 us  [hop(): return lax.ppermute(value, 'rep', [(r, r ^ 1 << b) for r in range(reps)])]
    select_n x3, other arithmetic: 5.1 us -> 0.55 us  [arrival(): value = arrived if value is None else jnp.where(here == s, arrived, value)]
    pallas_call x2, Pallas kernels: 56.7 us -> 53.5 us  [run_field(): pl.pallas_call(functools.partial(field_kernel, plan, field, last), grid_s...]
    ppermute x6, starting transfers between devices: 13.2 us -> 10.5 us  [along(): return lax.ppermute(value, 'space', pairs)]
    another operation x7, other arithmetic: 7.8 us -> 5.46 us  [per_device(): jnp.stack([jnp.stack([(top if f else 0) + jnp.int32(n_bits * at if f and...]
  transfers between devices with their start and end apart: 18 -> 18, of which waited for: 9 -> 10; matrix products, arithmetic and copies ran while one was open for 10% -> 5% of each run, Pallas kernels for 36% -> 35%
where the time goes in v3:
time: 195 us
  Pallas kernels  112 us (57%)
  waiting for transfers between devices  44.3 us (23%)
  starting transfers between devices  21.8 us (11%)
  other arithmetic  7.66 us (4%)
  local copies, waits for them, and re-layouts  6.24 us (3%)
  between operations  2.91 us (1%)
    pallas_call x5, Pallas kernels, run_blocks(): pl.pallas_call(functools.partial(block_kernel, plan, len(arrays), len(slo...  56.3 us
    pallas_call x2, Pallas kernels, run_field(): pl.pallas_call(functools.partial(field_kernel, plan, field, last), grid_s...  53.5 us
    ppermute x12, waiting for transfers between devices, hop(): return lax.ppermute(value, 'rep', [(r, r ^ 1 << b) for r in range(reps)])  31.4 us
    ppermute x6, waiting for transfers between devices, along(): return lax.ppermute(value, 'space', pairs)  12.9 us
    ppermute x12, starting transfers between devices, hop(): return lax.ppermute(value, 'rep', [(r, r ^ 1 << b) for r in range(reps)])  11.3 us
    ppermute x6, starting transfers between devices, along(): return lax.ppermute(value, 'space', pairs)  10.5 us
    another operation x7, other arithmetic, per_device(): jnp.stack([jnp.stack([(top if f else 0) + jnp.int32(n_bits * at if f and...  5.46 us
  transfers between devices with their start and end apart: 18, of which 10 were waited for; matrix products, arithmetic and copies ran while one was open for 5% of the time, Pallas kernels for 35%

profile of v3, /device:TPU:0, one launch (start us, length us, event | category | flops | bytes accessed | tf_op | source)
XLA Modules:
  0.0 195.0 jit_solution(3793991532949728215)
XLA Ops:
  0.6 0.7 convert_reduce_fusion
  1.4 0.6 pad.8.lab_ref
  2.0 2.3 %pack.1.refs_0_ = bf16[496,1024]{1,0:T(8,128)(2,1)} custom-call(bf16[480,1024]{1,0:T(8,128)(2,1)} %bitcast.36, f32[1,1024]{1,0:T(1,128)} %pad.8.lab_ref), custom_call_target="tpu_custom_call" | custom-call | tf_op jit(solution)/shard_map/pack/pallas_call | solution.py:666
  4.3 5.0 %collective-permute-start = (bf16[496,1024]{1,0:T(8,128)(2,1)}, bf16[496,1024]{1,0:T(8,128)(2,1)S(1)}, u32[]{:S(2)}, u32[]{:S(2)}) collective-permute-start(bf16[496,1024]{1,0:T(8,128)(2,1)} %pack.1.refs_0_), channel_id=1, source_target_pairs={{0,8},{8,16},{16,24},{1,9},{9,17},{17,25},{2,10},{10,18},{18,26},{... | collective-permute-start | bytes 3047432 | tf_op jit(solution)/shard_map/ppermute | solution.py:685
  9.3 1.3 collective-permute-start.1
  10.6 1.6 collective-permute-start.2
  14.2 0.7 constant_dynamic-slice_fusion.1
  14.8 0.7 fusion.9
  15.5 1.3 fusion.5
  16.8 1.3 fusion.1
  18.1 0.7 pad.9.refs_16_
  18.8 0.7 constant_dynamic-slice_fusion
  19.5 1.4 fusion.7
  20.9 1.4 fusion.3
  22.4 1.2 copy-done
  23.6 7.9 %block_forward.5 = (bf16[2,4,1024,480]{3,2,1,0:T(8,128)(2,1)}, bf16[2,4,480,768]{3,2,1,0:T(8,128)(2,1)}, f32[3,2,20,96,256]{4,3,2,1,0:T(8,128)}, bf16[2,4,16,1024]{3,2,1,0:T(8,128)(2,1)S(1)}) custom-call(s32[1,3]{1,0:T(1,128)S(1)} %get-tuple-element.208.meta, bf16[496,1024]{1,0:T(8,128)(2,1)S(1)} %copy-done, bf16[29,1024,256]{2,1,0:T(8,128)(2,1)} %refs_14_.3), custom_call_target="tpu_custom_call" | custom-call | flops 4026531840 | bytes 40000000 | tf_op jit(solution)/shard_map/block_forward/pallas_call | solution.py:281
  31.5 3.9 %collective-permute-done.1 = bf16[496,1024]{1,0:T(8,128)(2,1)S(1)} collective-permute-done((bf16[496,1024]{1,0:T(8,128)(2,1)}, bf16[496,1024]{1,0:T(8,128)(2,1)S(1)}, u32[]{:S(2)}, u32[]{:S(2)}) %collective-permute-start.1) | collective-permute-done | bytes 1015840 | tf_op jit(solution)/shard_map/ppermute | solution.py:685
  35.5 1.6 collective-permute-start.6
  37.1 1.6 collective-permute-start.5
  38.7 0.7 collective-permute-start.3
  39.4 1.3 collective-permute-start.4
  40.7 7.9 %block_forward.6 = (bf16[2,4,1024,480]{3,2,1,0:T(8,128)(2,1)}, bf16[2,4,480,768]{3,2,1,0:T(8,128)(2,1)}, f32[3,2,20,96,256]{4,3,2,1,0:T(8,128)}, bf16[2,4,16,1024]{3,2,1,0:T(8,128)(2,1)S(1)}) custom-call(s32[1,3]{1,0:T(1,128)S(1)} %get-tuple-element.108.meta, ...), custom_call_target="tpu_custom_call", output_to_operand_aliasing={{0}: (3, {}), {1}: (4, {}), {2}: (5, {}), {3}: (6, {})} | custom-call | flops 4026531840 | bytes 40000000 | tf_op jit(solution)/shard_map/block_forward/pallas_call | solution.py:281
  48.7 9.9 %collective-permute-done.6.refs_3_ = bf16[496,1024]{1,0:T(8,128)(2,1)S(1)} collective-permute-done((bf16[496,1024]{1,0:T(8,128)(2,1)S(1)}, bf16[496,1024]{1,0:T(8,128)(2,1)S(1)}, u32[]{:S(2)}, u32[]{:S(2)}) %collective-permute-start.6) | collective-permute-done | bytes 1015840 | tf_op jit(solution)/shard_map/ppermute | solution.py:688
  58.5 1.4 collective-permute-done.5.refs_2_
  59.9 6.2 %collective-permute-done.4 = bf16[496,1024]{1,0:T(8,128)(2,1)S(1)} collective-permute-done((bf16[496,1024]{1,0:T(8,128)(2,1)S(1)}, bf16[496,1024]{1,0:T(8,128)(2,1)S(1)}, u32[]{:S(2)}, u32[]{:S(2)}) %collective-permute-start.4) | collective-permute-done | bytes 1015840 | tf_op jit(solution)/shard_map/ppermute | solution.py:685
  66.3 0.3 fusion.refs_0_
  66.6 0.6 collective-permute-start.11
  67.3 0.6 collective-permute-start.10
  67.9 0.7 collective-permute-start.7
  68.6 1.5 collective-permute-start.8
  70.1 13.5 %block_forward.7 = (bf16[2,4,1024,480]{3,2,1,0:T(8,128)(2,1)}, bf16[2,4,480,768]{3,2,1,0:T(8,128)(2,1)}, f32[3,2,20,96,256]{4,3,2,1,0:T(8,128)}, bf16[2,4,16,1024]{3,2,1,0:T(8,128)(2,1)S(1)}) custom-call(s32[2,3]{1,0:T(2,128)S(1)} %pad_add_fusion.meta, ...), custom_call_target="tpu_custom_call", output_to_operand_aliasing={{0}: (6, {}), {1}: (7, {}), {2}: (8, {}), {3}: (9, {})} | custom-call | flops 8053063680 | bytes 60000000 | tf_op jit(solution)/shard_map/block_forward/pallas_call | solution.py:281
  83.6 7.9 %collective-permute-done.11.refs_2_ = bf16[496,1024]{1,0:T(8,128)(2,1)S(1)} collective-permute-done((bf16[496,1024]{1,0:T(8,128)(2,1)S(1)}, bf16[496,1024]{1,0:T(8,128)(2,1)S(1)}, u32[]{:S(2)}, u32[]{:S(2)}) %collective-permute-start.11) | collective-permute-done | bytes 1015840 | tf_op jit(solution)/shard_map/ppermute | solution.py:688
  91.5 0.5 collective-permute-done.10.refs_2_
  91.9 2.8 %collective-permute-done.8 = bf16[496,1024]{1,0:T(8,128)(2,1)S(1)} collective-permute-done((bf16[496,1024]{1,0:T(8,128)(2,1)S(1)}, bf16[496,1024]{1,0:T(8,128)(2,1)S(1)}, u32[]{:S(2)}, u32[]{:S(2)}) %collective-permute-start.8) | collective-permute-done | bytes 1015840 | tf_op jit(solution)/shard_map/ppermute | solution.py:685
  95.0 0.2 select_select_fusion.2.refs_0_
  95.2 1.6 collective-permute-start.14
  96.9 1.6 collective-permute-start.13
  98.5 13.5 %block_forward.8 = (bf16[2,4,1024,480]{3,2,1,0:T(8,128)(2,1)}, bf16[2,4,480,768]{3,2,1,0:T(8,128)(2,1)}, f32[3,2,20,96,256]{4,3,2,1,0:T(8,128)}, bf16[2,4,16,1024]{3,2,1,0:T(8,128)(2,1)S(1)}) custom-call(s32[2,3]{1,0:T(2,128)S(1)} %pad_add_fusion.1.meta, ...), custom_call_target="tpu_custom_call", output_to_operand_aliasing={{0}: (6, {}), {1}: (7, {}), {2}: (8, {}), {3}: (9, {})} | custom-call | flops 8053063680 | bytes 60000000 | tf_op jit(solution)/shard_map/block_forward/pallas_call | solution.py:281
  111.9 8.1 %collective-permute-done.14.refs_5_ = bf16[496,1024]{1,0:T(8,128)(2,1)S(1)} collective-permute-done((bf16[496,1024]{1,0:T(8,128)(2,1)S(1)}, bf16[496,1024]{1,0:T(8,128)(2,1)S(1)}, u32[]{:S(2)}, u32[]{:S(2)}) %collective-permute-start.14) | collective-permute-done | bytes 1015840 | tf_op jit(solution)/shard_map/ppermute | solution.py:688
  120.1 1.4 collective-permute-done.13.refs_1_
  121.6 1.6 collective-permute-start.16
  123.5 25.9 %field_grads.2 = (bf16[4,8,256,256]{3,2,1,0:T(8,128)(2,1)}, bf16[320,256]{1,0:T(8,128)(2,1)S(1)}, bf16[64,128]{1,0:T(8,128)(2,1)S(1)}) custom-call(s32[210]{0:T(256)S(1)} %bitcast.34, bf16[2,4,480,768]{3,2,1,0:T(8,128)(2,1)} %get-tuple-element.184.refs_0_.refs_8_, ...), custom_call_target="tpu_custom_call" | custom-call | flops 10000000000 | bytes 90000000 | tf_op jit(solution)/shard_map/field_grads/pallas_call | solution.py:619
  149.6 0.5 collective-permute-start.17
  150.1 2.2 %collective-permute-done.17.refs_3_ = bf16[496,1024]{1,0:T(8,128)(2,1)S(1)} collective-permute-done((bf16[496,1024]{1,0:T(8,128)(2,1)S(1)}, bf16[496,1024]{1,0:T(8,128)(2,1)S(1)}, u32[]{:S(2)}, u32[]{:S(2)}) %collective-permute-start.17) | collective-permute-done | bytes 1015840 | tf_op jit(solution)/shard_map/ppermute | solution.py:688
  152.3 1.0 copy-done.7
  153.3 13.5 %block_forward.9 = (bf16[2,4,1024,480]{3,2,1,0:T(8,128)(2,1)}, bf16[2,4,480,768]{3,2,1,0:T(8,128)(2,1)}, f32[3,2,20,96,256]{4,3,2,1,0:T(8,128)}, bf16[2,4,16,1024]{3,2,1,0:T(8,128)(2,1)S(1)}) custom-call(s32[2,3]{1,0:T(2,128)S(1)} %pad_add_fusion.2.meta, ...), custom_call_target="tpu_custom_call", output_to_operand_aliasing={{0}: (8, {}), {1}: (9, {}), {2}: (10, {}), {3}: (11, {})} | custom-call | flops 8053063680 | bytes 60000000 | tf_op jit(solution)/shard_map/block_forward/pallas_call | solution.py:281
  166.7 27.6 %field_grads.3 = (f32[7424,256]{1,0:T(8,128)}, f32[320,256]{1,0:T(8,128)}, f32[64,128]{1,0:T(8,128)S(1)}) custom-call(s32[210]{0:T(256)S(1)} %bitcast.35, bf16[2,4,480,768]{3,2,1,0:T(8,128)(2,1)} %get-tuple-element.187.refs_0_, ...), custom_call_target="tpu_custom_call" | custom-call | flops 10000000000 | bytes 90000000 | tf_op jit(solution)/shard_map/field_grads/pallas_call | solution.py:619
  194.3 0.6 copy.28
  (39 shorter events, 1.4 us)
Async XLA Ops:
  4.3 27.1 %collective-permute-start = (bf16[496,1024]{1,0:T(8,128)(2,1)}, bf16[496,1024]{1,0:T(8,128)(2,1)S(1)}, u32[]{:S(2)}, u32[]{:S(2)}) collective-permute-start(bf16[496,1024]{1,0:T(8,128)(2,1)} %pack.1.refs_0_), channel_id=1, source_target_pairs={{0,8},{8,16},{16,24},{1,9},{9,17},{17,25},{2,10},{10,18},{18,26},{... | collective-permute-start | bytes 3047432 | tf_op jit(solution)/shard_map/ppermute | solution.py:685
  9.3 26.0 %collective-permute-start.1 = (bf16[496,1024]{1,0:T(8,128)(2,1)}, bf16[496,1024]{1,0:T(8,128)(2,1)S(1)}, u32[]{:S(2)}, u32[]{:S(2)}) collective-permute-start(bf16[496,1024]{1,0:T(8,128)(2,1)} %pack.1.refs_0_), channel_id=1, source_target_pairs={{8,0},{16,8},{24,16},{9,1},{17,9},{25,17},{10,2},{18,10},{26,18},{... | collective-permute-start | bytes 3047432 | tf_op jit(solution)/shard_map/ppermute | solution.py:685
  10.6 24.7 %collective-permute-start.2 = (bf16[496,1024]{1,0:T(8,128)(2,1)}, bf16[496,1024]{1,0:T(8,128)(2,1)S(1)}, u32[]{:S(2)}, u32[]{:S(2)}) collective-permute-start(bf16[496,1024]{1,0:T(8,128)(2,1)} %pack.1.refs_0_), channel_id=1, source_target_pairs={{0,2},{1,3},{2,0},{3,1},{4,6},{5,7},{6,4},{7,5},{8,10},{9,11},{10,... | collective-permute-start | bytes 3047432 | tf_op jit(solution)/shard_map/ppermute | solution.py:688
  22.4 1.2 copy-start
  35.4 13.3 %copy-start.3 = (bf16[496,1024]{1,0:T(8,128)(2,1)}, bf16[496,1024]{1,0:T(8,128)(2,1)S(1)}, u32[]{:S(2)}) copy-start(bf16[496,1024]{1,0:T(8,128)(2,1)S(1)} %collective-permute-done.2.refs_3_) | copy-start | bytes 3047428
  35.5 23.1 %collective-permute-start.6 = (bf16[496,1024]{1,0:T(8,128)(2,1)S(1)}, bf16[496,1024]{1,0:T(8,128)(2,1)S(1)}, u32[]{:S(2)}, u32[]{:S(2)}) collective-permute-start(bf16[496,1024]{1,0:T(8,128)(2,1)S(1)} %select_select_fusion.1.refs_0_), channel_id=1, source_target_pairs={{0,2},{1,3},{2,0},{3,1},{4,6},{5,7},{6,4},{7,5},{8,10},{9,11},{10,... | collective-permute-start | bytes 3047432 | tf_op jit(solution)/shard_map/ppermute | solution.py:688
  37.1 22.8 %collective-permute-start.5 = (bf16[496,1024]{1,0:T(8,128)(2,1)S(1)}, bf16[496,1024]{1,0:T(8,128)(2,1)S(1)}, u32[]{:S(2)}, u32[]{:S(2)}) collective-permute-start(bf16[496,1024]{1,0:T(8,128)(2,1)S(1)} %broadcast_select_fusion.3), channel_id=1, source_target_pairs={{0,4},{1,5},{2,6},{3,7},{4,0},{5,1},{6,2},{7,3},{8,12},{9,13},{10,... | collective-permute-start | bytes 3047432 | tf_op jit(solution)/shard_map/ppermute | solution.py:688
  38.7 21.2 %collective-permute-start.3 = (bf16[496,1024]{1,0:T(8,128)(2,1)S(1)}, bf16[496,1024]{1,0:T(8,128)(2,1)S(1)}, u32[]{:S(2)}, u32[]{:S(2)}) collective-permute-start(bf16[496,1024]{1,0:T(8,128)(2,1)S(1)} %collective-permute-done), channel_id=1, source_target_pairs={{8,16},{16,24},{9,17},{17,25},{10,18},{18,26},{11,19},{19,27},{12,... | collective-permute-start | bytes 3047432 | tf_op jit(solution)/shard_map/ppermute | solution.py:685
  39.4 26.7 %collective-permute-start.4 = (bf16[496,1024]{1,0:T(8,128)(2,1)S(1)}, bf16[496,1024]{1,0:T(8,128)(2,1)S(1)}, u32[]{:S(2)}, u32[]{:S(2)}) collective-permute-start(bf16[496,1024]{1,0:T(8,128)(2,1)S(1)} %collective-permute-done.1), channel_id=1, source_target_pairs={{8,0},{16,8},{9,1},{17,9},{10,2},{18,10},{11,3},{19,11},{12,4},{20... | collective-permute-start | bytes 3047432 | tf_op jit(solution)/shard_map/ppermute | solution.py:685
  58.5 25.1 %copy-start.4 = (bf16[496,1024]{1,0:T(8,128)(2,1)}, bf16[496,1024]{1,0:T(8,128)(2,1)S(1)}, u32[]{:S(2)}) copy-start(bf16[496,1024]{1,0:T(8,128)(2,1)S(1)} %collective-permute-done.6.refs_3_) | copy-start | bytes 3047428
  66.2 3.8 %collective-permute-start.9 = (bf16[496,1024]{1,0:T(8,128)(2,1)S(1)}, bf16[496,1024]{1,0:T(8,128)(2,1)S(1)}, u32[]{:S(2)}, u32[]{:S(2)}) collective-permute-start(bf16[496,1024]{1,0:T(8,128)(2,1)S(1)} %broadcast_select_fusion.7), channel_id=1, source_target_pairs={{0,1},{1,0},{2,3},{3,2},{4,5},{5,4},{6,7},{7,6},{8,9},{9,8},{10,11... | collective-permute-start | bytes 3047432 | tf_op jit(solution)/shard_map/ppermute | solution.py:688
  66.6 24.9 %collective-permute-start.11 = (bf16[496,1024]{1,0:T(8,128)(2,1)S(1)}, bf16[496,1024]{1,0:T(8,128)(2,1)S(1)}, u32[]{:S(2)}, u32[]{:S(2)}) collective-permute-start(bf16[496,1024]{1,0:T(8,128)(2,1)S(1)} %fusion.refs_0_), channel_id=1, source_target_pairs={{0,2},{1,3},{2,0},{3,1},{4,6},{5,7},{6,4},{7,5},{8,10},{9,11},{10,... | collective-permute-start | bytes 3047432 | tf_op jit(solution)/shard_map/ppermute | solution.py:688
  67.3 24.6 %collective-permute-start.10 = (bf16[496,1024]{1,0:T(8,128)(2,1)S(1)}, bf16[496,1024]{1,0:T(8,128)(2,1)S(1)}, u32[]{:S(2)}, u32[]{:S(2)}) collective-permute-start(bf16[496,1024]{1,0:T(8,128)(2,1)S(1)} %broadcast_select_fusion.2), channel_id=1, source_target_pairs={{0,4},{1,5},{2,6},{3,7},{4,0},{5,1},{6,2},{7,3},{8,12},{9,13},{10,... | collective-permute-start | bytes 3047432 | tf_op jit(solution)/shard_map/ppermute | solution.py:688
  67.9 24.1 %collective-permute-start.7 = (bf16[496,1024]{1,0:T(8,128)(2,1)S(1)}, bf16[496,1024]{1,0:T(8,128)(2,1)S(1)}, u32[]{:S(2)}, u32[]{:S(2)}) collective-permute-start(bf16[496,1024]{1,0:T(8,128)(2,1)S(1)} %collective-permute-done.3), channel_id=1, source_target_pairs={{16,24},{17,25},{18,26},{19,27},{20,28},{21,29},{22,30},{23,31}} | collective-permute-start | bytes 3047432 | tf_op jit(solution)/shard_map/ppermute | solution.py:685
  68.6 26.2 %collective-permute-start.8 = (bf16[496,1024]{1,0:T(8,128)(2,1)S(1)}, bf16[496,1024]{1,0:T(8,128)(2,1)S(1)}, u32[]{:S(2)}, u32[]{:S(2)}) collective-permute-start(bf16[496,1024]{1,0:T(8,128)(2,1)S(1)} %collective-permute-done.4), channel_id=1, source_target_pairs={{8,0},{9,1},{10,2},{11,3},{12,4},{13,5},{14,6},{15,7}} | collective-permute-start | bytes 3047432 | tf_op jit(solution)/shard_map/ppermute | solution.py:685
  94.9 3.5 %collective-permute-start.12 = (bf16[496,1024]{1,0:T(8,128)(2,1)S(1)}, bf16[496,1024]{1,0:T(8,128)(2,1)S(1)}, u32[]{:S(2)}, u32[]{:S(2)}) collective-permute-start(bf16[496,1024]{1,0:T(8,128)(2,1)S(1)} %broadcast_select_fusion.6), channel_id=1, source_target_pairs={{0,1},{1,0},{2,3},{3,2},{4,5},{5,4},{6,7},{7,6},{8,9},{9,8},{10,11... | collective-permute-start | bytes 3047432 | tf_op jit(solution)/shard_map/ppermute | solution.py:688
  95.2 24.9 %collective-permute-start.14 = (bf16[496,1024]{1,0:T(8,128)(2,1)S(1)}, bf16[496,1024]{1,0:T(8,128)(2,1)S(1)}, u32[]{:S(2)}, u32[]{:S(2)}) collective-permute-start(bf16[496,1024]{1,0:T(8,128)(2,1)S(1)} %select_select_fusion.2.refs_0_), channel_id=1, source_target_pairs={{0,2},{1,3},{2,0},{3,1},{4,6},{5,7},{6,4},{7,5},{8,10},{9,11},{10,... | collective-permute-start | bytes 3047432 | tf_op jit(solution)/shard_map/ppermute | solution.py:688
  96.8 26.6 %copy-start.1 = (bf16[1280,256]{1,0:T(8,128)(2,1)S(1)}, bf16[1280,256]{1,0:T(8,128)(2,1)}, u32[]{:S(2)}) copy-start(bf16[1280,256]{1,0:T(8,128)(2,1)} %refs_15_.3) | copy-start | bytes 1966084
  96.9 26.6 %copy-start.2 = (f32[3]{0:T(128)S(1)}, f32[3]{0:T(128)}, u32[]{:S(2)}) copy-start(f32[3]{0:T(128)} %refs_17_.3) | copy-start | bytes 40
  96.9 24.6 %collective-permute-start.13 = (bf16[496,1024]{1,0:T(8,128)(2,1)S(1)}, bf16[496,1024]{1,0:T(8,128)(2,1)S(1)}, u32[]{:S(2)}, u32[]{:S(2)}) collective-permute-start(bf16[496,1024]{1,0:T(8,128)(2,1)S(1)} %broadcast_select_fusion.1), channel_id=1, source_target_pairs={{0,4},{1,5},{2,6},{3,7},{4,0},{5,1},{6,2},{7,3},{8,12},{9,13},{10,... | collective-permute-start | bytes 3047432 | tf_op jit(solution)/shard_map/ppermute | solution.py:688
  120.1 29.3 %copy-start.5 = (bf16[496,1024]{1,0:T(8,128)(2,1)}, bf16[496,1024]{1,0:T(8,128)(2,1)S(1)}, u32[]{:S(2)}) copy-start(bf16[496,1024]{1,0:T(8,128)(2,1)S(1)} %collective-permute-done.14.refs_5_) | copy-start | bytes 3047428
  121.6 27.8 %collective-permute-start.16 = (bf16[496,1024]{1,0:T(8,128)(2,1)S(1)}, bf16[496,1024]{1,0:T(8,128)(2,1)S(1)}, u32[]{:S(2)}, u32[]{:S(2)}) collective-permute-start(bf16[496,1024]{1,0:T(8,128)(2,1)S(1)} %broadcast_select_fusion), channel_id=1, source_target_pairs={{0,4},{1,5},{2,6},{3,7},{4,0},{5,1},{6,2},{7,3},{8,12},{9,13},{10,... | collective-permute-start | bytes 3047432 | tf_op jit(solution)/shard_map/ppermute | solution.py:688
  123.4 26.1 %collective-permute-start.15 = (bf16[496,1024]{1,0:T(8,128)(2,1)S(1)}, bf16[496,1024]{1,0:T(8,128)(2,1)S(1)}, u32[]{:S(2)}, u32[]{:S(2)}) collective-permute-start(bf16[496,1024]{1,0:T(8,128)(2,1)S(1)} %broadcast_select_fusion.5), channel_id=1, source_target_pairs={{0,1},{1,0},{2,3},{3,2},{4,5},{5,4},{6,7},{7,6},{8,9},{9,8},{10,11... | collective-permute-start | bytes 3047432 | tf_op jit(solution)/shard_map/ppermute | solution.py:688
  149.4 2.9 %copy-start.6 = (bf16[496,1024]{1,0:T(8,128)(2,1)}, bf16[496,1024]{1,0:T(8,128)(2,1)S(1)}, u32[]{:S(2)}) copy-start(bf16[496,1024]{1,0:T(8,128)(2,1)S(1)} %collective-permute-done.16.refs_4_) | copy-start | bytes 3047428
  149.6 2.8 %collective-permute-start.17 = (bf16[496,1024]{1,0:T(8,128)(2,1)S(1)}, bf16[496,1024]{1,0:T(8,128)(2,1)S(1)}, u32[]{:S(2)}, u32[]{:S(2)}) collective-permute-start(bf16[496,1024]{1,0:T(8,128)(2,1)S(1)} %broadcast_select_fusion.4), channel_id=1, source_target_pairs={{0,1},{1,0},{2,3},{3,2},{4,5},{5,4},{6,7},{7,6},{8,9},{9,8},{10,11... | collective-permute-start | bytes 3047432 | tf_op jit(solution)/shard_map/ppermute | solution.py:688
  152.3 1.0 copy-start.7

commit v4 on v3

--- a/solution.py
+++ b/solution.py
@@ -315,20 +315,20 @@
 def field_kernel(plan, field, last, tab, *refs):
     n, rows, cols, pix = plan.n, plan.rows, plan.cols, plan.pix
     c_in, c_out, n_sh = plan.c_in, plan.c_out, plan.n_sh
-    n_rows_in = 2 * n_sh * rows
     unit_rows, depth, flags = plan.unit_rows, plan.depth, plan.flags
     cat_ref = refs[0]
     mid_refs = refs[1:1 + n_sh]
-    s_refs = refs[1 + n_sh:1 + n_sh + n_rows_in]
-    refs = refs[1 + n_sh + n_rows_in:]
+    s_hbm = refs[1 + n_sh]
+    refs = refs[2 + n_sh:]
     aux_ref, all_ref, w28_ref, wproj_ref, wcls_ref, cw_ref, xt_hbm = refs[:7]
     refs = refs[7:]
     if last:
         prev_g, prev_p, prev_c = refs[:3]
         refs = refs[3:]
     g_out, p_out, c_ref_out = refs[:3]
+    side_refs = refs[3:3 + 2 * n_sh]
     (dbuf, pad, mean, ybuf, lbuf, dybuf, gp, spool, pact, catall, acc, stage, xt_ref, sem_xt,
-     sems) = refs[3:]
+     sems, sem_s) = refs[3 + 2 * n_sh:]
     xt_copy = pltpu.make_async_copy(xt_hbm.at[field], xt_ref, sem_xt)
     step = pl.program_id(0)
     edge_rows = rows - 1
@@ -339,8 +339,21 @@
             return grad
         return (prev.astype(F32) + grad.astype(F32)) * 0.5
 
+    def side_copies():
+        copies = []
+        for at, k in enumerate(plan.shifted):
+            for side in range(2):
+                first, count = side * RATE * k, plan.height - RATE * k
+                copies.append(pltpu.make_async_copy(
+                    s_hbm.at[3 * at + 2 * side, field, pl.ds(first, count)],
+                    side_refs[2 * at + side], sem_s.at[2 * at + side],
+                ))
+        return copies
+
     @pl.when(step == 0)
     def _():
+        for copy in side_copies():
+            copy.start()
         xt_copy.start()
         zero = jnp.zeros((edge_rows, cols, dbuf.shape[2]), BF16)
         dbuf[:edge_rows] = zero
@@ -354,6 +367,8 @@
         mean_in = (total / plan.total).astype(BF16)
         mean[...] = jnp.broadcast_to(mean_in.astype(F32), (16, c_in))
         pact[...] = nn(mean[...].astype(BF16), w28_ref[0])
+        for copy in side_copies():
+            copy.wait()
 
     @pl.when(step < n)
     def _():
@@ -368,10 +383,11 @@
                 for i in range(rows):
                     h = block * rows + i
                     line = pre[i]
-                    for side, src in ((0, h - r), (1, h + r)):
-                        ok = jnp.logical_and(src >= 0, src < plan.height)
-                        ref = s_refs[(2 * at + side) * rows + i]
-                        line = line + jnp.where(ok, ref[...], 0.0)
+                    for side, src in ((0, h - r), (1, h)):
+                        last_row = plan.height - r - 1
+                        ok = jnp.logical_and(src >= 0, src <= last_row)
+                        got = side_refs[2 * at + side][jnp.clip(src, 0, last_row)]
+                        line = line + jnp.where(ok, got, 0.0)
                     cat5[i * cols:(i + 1) * cols, part] = jnp.maximum(line, 0.0).astype(BF16)
             else:
                 at = plan.direct.index(k)
@@ -583,15 +599,8 @@
             lambda i, t, at=at: (3 * at + 1, field, blk(i), 0, 0),
         ))
         operands.append(s)
-    for at, k in enumerate(plan.shifted):
-        for side in range(2):
-            move = (2 * side - 1) * RATE * k
-            for row in range(rows):
-                def index(i, t, at=at, side=side, move=move, row=row):
-                    h = jnp.clip(blk(i) * rows + row + move, 0, plan.height - 1)
-                    return (3 * at + 2 * side, field, h, 0, 0)
-                in_specs.append(pl.BlockSpec((None, None, None, cols, c_out), index))
-                operands.append(s)
+    in_specs.append(pl.BlockSpec(memory_space=pl.ANY))
+    operands.append(s)
     in_specs += [
         pl.BlockSpec((None, None, EXTRA, c_in), lambda i, t: (field, blk(i), 0, 0)),
         pl.BlockSpec((None, n, EXTRA, c_in), lambda i, t: (field, 0, 0, 0)),
@@ -624,6 +633,9 @@
             in_specs=in_specs,
             out_specs=[main_spec] + small,
             scratch_shapes=[
+                pltpu.VMEM((plan.height - RATE * k, cols, c_out), F32)
+                for k in plan.shifted for _ in range(2)
+            ] + [
                 pltpu.VMEM((plan.height + 2 * (rows - 1), cols, plan.n_slots * c_out), BF16),
                 pltpu.VMEM((rows, cols + 2 * EDGE, c_out), F32),
                 pltpu.VMEM((16, c_in), F32),
@@ -639,6 +651,7 @@
                 pltpu.VMEM((n, c_in, pix), BF16),
                 pltpu.SemaphoreType.DMA,
                 pltpu.SemaphoreType.DMA((2, depth)),
+                pltpu.SemaphoreType.DMA((2 * n_sh,)),
             ],
         ),
         out_shape=[

time: 195 us -> 194 us (level)
  Pallas kernels: 112 us -> 110 us
where the time goes in v4:
time: 194 us; the launch traced here: 193 us
  Pallas kernels  110 us (57%)
  waiting for transfers between devices  44.4 us (23%)
  starting transfers between devices  21.8 us (11%)
  other arithmetic  7.66 us (4%)
  local copies, waits for them, and re-layouts  6.24 us (3%)
  between operations  2.91 us (2%)
    pallas_call x5, Pallas kernels, run_blocks(): pl.pallas_call(functools.partial(block_kernel, plan, len(arrays), len(slo...  56.2 us
    pallas_call x2, Pallas kernels, run_field(): pl.pallas_call(functools.partial(field_kernel, plan, field, last), grid_s...  51.9 us
    ppermute x12, waiting for transfers between devices, hop(): return lax.ppermute(value, 'rep', [(r, r ^ 1 << b) for r in range(reps)])  31.5 us
    ppermute x6, waiting for transfers between devices, along(): return lax.ppermute(value, 'space', pairs)  12.9 us
    ppermute x12, starting transfers between devices, hop(): return lax.ppermute(value, 'rep', [(r, r ^ 1 << b) for r in range(reps)])  11.3 us
    ppermute x6, starting transfers between devices, along(): return lax.ppermute(value, 'space', pairs)  10.5 us
    another operation x7, other arithmetic, per_device(): jnp.stack([jnp.stack([(top if f else 0) + jnp.int32(n_bits * at if f and...  5.46 us
  transfers between devices with their start and end apart: 18, of which 10 were waited for; matrix products, arithmetic and copies ran while one was open for 5% of the time, Pallas kernels for 35%

profile of v4, /device:TPU:0, one launch (start us, length us, event | category | flops | bytes accessed | tf_op | source)
XLA Modules:
  0.0 193.3 jit_solution(8520613956904620670)
XLA Ops:
  0.6 0.7 convert_reduce_fusion
  1.4 0.6 pad.8.lab_ref
  2.0 2.3 %pack.1.refs_0_ = bf16[496,1024]{1,0:T(8,128)(2,1)} custom-call(bf16[480,1024]{1,0:T(8,128)(2,1)} %bitcast.36, f32[1,1024]{1,0:T(1,128)} %pad.8.lab_ref), custom_call_target="tpu_custom_call" | custom-call | tf_op jit(solution)/shard_map/pack/pallas_call | solution.py:679
  4.3 5.0 %collective-permute-start = (bf16[496,1024]{1,0:T(8,128)(2,1)}, bf16[496,1024]{1,0:T(8,128)(2,1)S(1)}, u32[]{:S(2)}, u32[]{:S(2)}) collective-permute-start(bf16[496,1024]{1,0:T(8,128)(2,1)} %pack.1.refs_0_), channel_id=1, source_target_pairs={{0,8},{8,16},{16,24},{1,9},{9,17},{17,25},{2,10},{10,18},{18,26},{... | collective-permute-start | bytes 3047432 | tf_op jit(solution)/shard_map/ppermute | solution.py:698
  9.3 1.3 collective-permute-start.1
  10.6 1.6 collective-permute-start.2
  14.2 0.7 constant_dynamic-slice_fusion.1
  14.8 0.7 fusion.9
  15.5 1.3 fusion.5
  16.8 1.3 fusion.1
  18.1 0.7 pad.9.refs_7_
  18.8 0.7 constant_dynamic-slice_fusion
  19.5 1.4 fusion.7
  20.9 1.4 fusion.3
  22.4 1.2 copy-done
  23.6 7.9 %block_forward.5 = (bf16[2,4,1024,480]{3,2,1,0:T(8,128)(2,1)}, bf16[2,4,480,768]{3,2,1,0:T(8,128)(2,1)}, f32[3,2,20,96,256]{4,3,2,1,0:T(8,128)}, bf16[2,4,16,1024]{3,2,1,0:T(8,128)(2,1)S(1)}) custom-call(s32[1,3]{1,0:T(1,128)S(1)} %get-tuple-element.208.meta, bf16[496,1024]{1,0:T(8,128)(2,1)S(1)} %copy-done, bf16[29,1024,256]{2,1,0:T(8,128)(2,1)} %refs_5_.3), custom_call_target="tpu_custom_call" | custom-call | flops 4026531840 | bytes 40000000 | tf_op jit(solution)/shard_map/block_forward/pallas_call | solution.py:281
  31.5 3.9 %collective-permute-done.1 = bf16[496,1024]{1,0:T(8,128)(2,1)S(1)} collective-permute-done((bf16[496,1024]{1,0:T(8,128)(2,1)}, bf16[496,1024]{1,0:T(8,128)(2,1)S(1)}, u32[]{:S(2)}, u32[]{:S(2)}) %collective-permute-start.1) | collective-permute-done | bytes 1015840 | tf_op jit(solution)/shard_map/ppermute | solution.py:698
  35.5 1.6 collective-permute-start.6
  37.1 1.6 collective-permute-start.5
  38.7 0.7 collective-permute-start.3
  39.4 1.3 collective-permute-start.4
  40.7 7.9 %block_forward.6 = (bf16[2,4,1024,480]{3,2,1,0:T(8,128)(2,1)}, bf16[2,4,480,768]{3,2,1,0:T(8,128)(2,1)}, f32[3,2,20,96,256]{4,3,2,1,0:T(8,128)}, bf16[2,4,16,1024]{3,2,1,0:T(8,128)(2,1)S(1)}) custom-call(s32[1,3]{1,0:T(1,128)S(1)} %get-tuple-element.108.meta, ...), custom_call_target="tpu_custom_call", output_to_operand_aliasing={{0}: (3, {}), {1}: (4, {}), {2}: (5, {}), {3}: (6, {})} | custom-call | flops 4026531840 | bytes 40000000 | tf_op jit(solution)/shard_map/block_forward/pallas_call | solution.py:281
  48.7 9.9 %collective-permute-done.6.refs_3_ = bf16[496,1024]{1,0:T(8,128)(2,1)S(1)} collective-permute-done((bf16[496,1024]{1,0:T(8,128)(2,1)S(1)}, bf16[496,1024]{1,0:T(8,128)(2,1)S(1)}, u32[]{:S(2)}, u32[]{:S(2)}) %collective-permute-start.6) | collective-permute-done | bytes 1015840 | tf_op jit(solution)/shard_map/ppermute | solution.py:701
  58.5 1.4 collective-permute-done.5.refs_2_
  59.9 6.2 %collective-permute-done.4 = bf16[496,1024]{1,0:T(8,128)(2,1)S(1)} collective-permute-done((bf16[496,1024]{1,0:T(8,128)(2,1)S(1)}, bf16[496,1024]{1,0:T(8,128)(2,1)S(1)}, u32[]{:S(2)}, u32[]{:S(2)}) %collective-permute-start.4) | collective-permute-done | bytes 1015840 | tf_op jit(solution)/shard_map/ppermute | solution.py:698
  66.3 0.3 fusion.refs_0_
  66.6 0.6 collective-permute-start.11
  67.3 0.6 collective-permute-start.10
  67.9 0.7 collective-permute-start.7
  68.6 1.5 collective-permute-start.8
  70.1 13.5 %block_forward.7 = (bf16[2,4,1024,480]{3,2,1,0:T(8,128)(2,1)}, bf16[2,4,480,768]{3,2,1,0:T(8,128)(2,1)}, f32[3,2,20,96,256]{4,3,2,1,0:T(8,128)}, bf16[2,4,16,1024]{3,2,1,0:T(8,128)(2,1)S(1)}) custom-call(s32[2,3]{1,0:T(2,128)S(1)} %pad_add_fusion.meta, ...), custom_call_target="tpu_custom_call", output_to_operand_aliasing={{0}: (6, {}), {1}: (7, {}), {2}: (8, {}), {3}: (9, {})} | custom-call | flops 8053063680 | bytes 60000000 | tf_op jit(solution)/shard_map/block_forward/pallas_call | solution.py:281
  83.6 7.9 %collective-permute-done.11.refs_2_ = bf16[496,1024]{1,0:T(8,128)(2,1)S(1)} collective-permute-done((bf16[496,1024]{1,0:T(8,128)(2,1)S(1)}, bf16[496,1024]{1,0:T(8,128)(2,1)S(1)}, u32[]{:S(2)}, u32[]{:S(2)}) %collective-permute-start.11) | collective-permute-done | bytes 1015840 | tf_op jit(solution)/shard_map/ppermute | solution.py:701
  91.5 0.5 collective-permute-done.10.refs_2_
  91.9 2.8 %collective-permute-done.8 = bf16[496,1024]{1,0:T(8,128)(2,1)S(1)} collective-permute-done((bf16[496,1024]{1,0:T(8,128)(2,1)S(1)}, bf16[496,1024]{1,0:T(8,128)(2,1)S(1)}, u32[]{:S(2)}, u32[]{:S(2)}) %collective-permute-start.8) | collective-permute-done | bytes 1015840 | tf_op jit(solution)/shard_map/ppermute | solution.py:698
  95.0 0.2 select_select_fusion.2.refs_0_
  95.2 1.6 collective-permute-start.14
  96.9 1.6 collective-permute-start.13
  98.5 13.4 %block_forward.8 = (bf16[2,4,1024,480]{3,2,1,0:T(8,128)(2,1)}, bf16[2,4,480,768]{3,2,1,0:T(8,128)(2,1)}, f32[3,2,20,96,256]{4,3,2,1,0:T(8,128)}, bf16[2,4,16,1024]{3,2,1,0:T(8,128)(2,1)S(1)}) custom-call(s32[2,3]{1,0:T(2,128)S(1)} %pad_add_fusion.1.meta, ...), custom_call_target="tpu_custom_call", output_to_operand_aliasing={{0}: (6, {}), {1}: (7, {}), {2}: (8, {}), {3}: (9, {})} | custom-call | flops 8053063680 | bytes 60000000 | tf_op jit(solution)/shard_map/block_forward/pallas_call | solution.py:281
  111.9 8.2 %collective-permute-done.14.refs_5_ = bf16[496,1024]{1,0:T(8,128)(2,1)S(1)} collective-permute-done((bf16[496,1024]{1,0:T(8,128)(2,1)S(1)}, bf16[496,1024]{1,0:T(8,128)(2,1)S(1)}, u32[]{:S(2)}, u32[]{:S(2)}) %collective-permute-start.14) | collective-permute-done | bytes 1015840 | tf_op jit(solution)/shard_map/ppermute | solution.py:701
  120.1 1.4 collective-permute-done.13.refs_1_
  121.6 1.6 collective-permute-start.16
  123.5 25.0 %field_grads.2 = (bf16[4,8,256,256]{3,2,1,0:T(8,128)(2,1)}, bf16[320,256]{1,0:T(8,128)(2,1)S(1)}, bf16[64,128]{1,0:T(8,128)(2,1)S(1)}) custom-call(s32[210]{0:T(256)S(1)} %bitcast.34, bf16[2,4,480,768]{3,2,1,0:T(8,128)(2,1)} %get-tuple-element.184.refs_0_.refs_8_, f32[3,2,20,96,256]{4,3,2,1,0:T(8,128)} %get-tuple-element.185.refs_1_.refs_2_.refs_9_, ...), custom_call_target="tpu_custom_call" | custom-call | flops 10000000000 | bytes 90000000 | tf_op jit(solution)/shard_map/field_grads/pallas_call | solution.py:628
  148.7 0.5 collective-permute-start.17
  149.2 2.2 %collective-permute-done.17.refs_3_ = bf16[496,1024]{1,0:T(8,128)(2,1)S(1)} collective-permute-done((bf16[496,1024]{1,0:T(8,128)(2,1)S(1)}, bf16[496,1024]{1,0:T(8,128)(2,1)S(1)}, u32[]{:S(2)}, u32[]{:S(2)}) %collective-permute-start.17) | collective-permute-done | bytes 1015840 | tf_op jit(solution)/shard_map/ppermute | solution.py:701
  151.4 1.0 copy-done.7
  152.4 13.5 %block_forward.9 = (bf16[2,4,1024,480]{3,2,1,0:T(8,128)(2,1)}, bf16[2,4,480,768]{3,2,1,0:T(8,128)(2,1)}, f32[3,2,20,96,256]{4,3,2,1,0:T(8,128)}, bf16[2,4,16,1024]{3,2,1,0:T(8,128)(2,1)S(1)}) custom-call(s32[2,3]{1,0:T(2,128)S(1)} %pad_add_fusion.2.meta, ...), custom_call_target="tpu_custom_call", output_to_operand_aliasing={{0}: (8, {}), {1}: (9, {}), {2}: (10, {}), {3}: (11, {})} | custom-call | flops 8053063680 | bytes 60000000 | tf_op jit(solution)/shard_map/block_forward/pallas_call | solution.py:281
  165.9 26.8 %field_grads.3 = (f32[7424,256]{1,0:T(8,128)}, f32[320,256]{1,0:T(8,128)}, f32[64,128]{1,0:T(8,128)S(1)}) custom-call(s32[210]{0:T(256)S(1)} %bitcast.35, bf16[2,4,480,768]{3,2,1,0:T(8,128)(2,1)} %get-tuple-element.187.refs_0_, f32[3,2,20,96,256]{4,3,2,1,0:T(8,128)} %get-tuple-element.188.refs_1_.refs_2_, ...), custom_call_target="tpu_custom_call" | custom-call | flops 10000000000 | bytes 90000000 | tf_op jit(solution)/shard_map/field_grads/pallas_call | solution.py:628
  192.7 0.6 copy.28
  (39 shorter events, 1.4 us)
Async XLA Ops:
  4.3 27.1 %collective-permute-start = (bf16[496,1024]{1,0:T(8,128)(2,1)}, bf16[496,1024]{1,0:T(8,128)(2,1)S(1)}, u32[]{:S(2)}, u32[]{:S(2)}) collective-permute-start(bf16[496,1024]{1,0:T(8,128)(2,1)} %pack.1.refs_0_), channel_id=1, source_target_pairs={{0,8},{8,16},{16,24},{1,9},{9,17},{17,25},{2,10},{10,18},{18,26},{... | collective-permute-start | bytes 3047432 | tf_op jit(solution)/shard_map/ppermute | solution.py:698
  9.3 26.0 %collective-permute-start.1 = (bf16[496,1024]{1,0:T(8,128)(2,1)}, bf16[496,1024]{1,0:T(8,128)(2,1)S(1)}, u32[]{:S(2)}, u32[]{:S(2)}) collective-permute-start(bf16[496,1024]{1,0:T(8,128)(2,1)} %pack.1.refs_0_), channel_id=1, source_target_pairs={{8,0},{16,8},{24,16},{9,1},{17,9},{25,17},{10,2},{18,10},{26,18},{... | collective-permute-start | bytes 3047432 | tf_op jit(solution)/shard_map/ppermute | solution.py:698
  10.6 24.7 %collective-permute-start.2 = (bf16[496,1024]{1,0:T(8,128)(2,1)}, bf16[496,1024]{1,0:T(8,128)(2,1)S(1)}, u32[]{:S(2)}, u32[]{:S(2)}) collective-permute-start(bf16[496,1024]{1,0:T(8,128)(2,1)} %pack.1.refs_0_), channel_id=1, source_target_pairs={{0,2},{1,3},{2,0},{3,1},{4,6},{5,7},{6,4},{7,5},{8,10},{9,11},{10,... | collective-permute-start | bytes 3047432 | tf_op jit(solution)/shard_map/ppermute | solution.py:701
  22.4 1.2 copy-start
  35.4 13.3 %copy-start.3 = (bf16[496,1024]{1,0:T(8,128)(2,1)}, bf16[496,1024]{1,0:T(8,128)(2,1)S(1)}, u32[]{:S(2)}) copy-start(bf16[496,1024]{1,0:T(8,128)(2,1)S(1)} %collective-permute-done.2.refs_3_) | copy-start | bytes 3047428
  35.5 23.1 %collective-permute-start.6 = (bf16[496,1024]{1,0:T(8,128)(2,1)S(1)}, bf16[496,1024]{1,0:T(8,128)(2,1)S(1)}, u32[]{:S(2)}, u32[]{:S(2)}) collective-permute-start(bf16[496,1024]{1,0:T(8,128)(2,1)S(1)} %select_select_fusion.1.refs_0_), channel_id=1, source_target_pairs={{0,2},{1,3},{2,0},{3,1},{4,6},{5,7},{6,4},{7,5},{8,10},{9,11},{10,... | collective-permute-start | bytes 3047432 | tf_op jit(solution)/shard_map/ppermute | solution.py:701
  37.1 22.8 %collective-permute-start.5 = (bf16[496,1024]{1,0:T(8,128)(2,1)S(1)}, bf16[496,1024]{1,0:T(8,128)(2,1)S(1)}, u32[]{:S(2)}, u32[]{:S(2)}) collective-permute-start(bf16[496,1024]{1,0:T(8,128)(2,1)S(1)} %broadcast_select_fusion.3), channel_id=1, source_target_pairs={{0,4},{1,5},{2,6},{3,7},{4,0},{5,1},{6,2},{7,3},{8,12},{9,13},{10,... | collective-permute-start | bytes 3047432 | tf_op jit(solution)/shard_map/ppermute | solution.py:701
  38.7 21.2 %collective-permute-start.3 = (bf16[496,1024]{1,0:T(8,128)(2,1)S(1)}, bf16[496,1024]{1,0:T(8,128)(2,1)S(1)}, u32[]{:S(2)}, u32[]{:S(2)}) collective-permute-start(bf16[496,1024]{1,0:T(8,128)(2,1)S(1)} %collective-permute-done), channel_id=1, source_target_pairs={{8,16},{16,24},{9,17},{17,25},{10,18},{18,26},{11,19},{19,27},{12,... | collective-permute-start | bytes 3047432 | tf_op jit(solution)/shard_map/ppermute | solution.py:698
  39.4 26.7 %collective-permute-start.4 = (bf16[496,1024]{1,0:T(8,128)(2,1)S(1)}, bf16[496,1024]{1,0:T(8,128)(2,1)S(1)}, u32[]{:S(2)}, u32[]{:S(2)}) collective-permute-start(bf16[496,1024]{1,0:T(8,128)(2,1)S(1)} %collective-permute-done.1), channel_id=1, source_target_pairs={{8,0},{16,8},{9,1},{17,9},{10,2},{18,10},{11,3},{19,11},{12,4},{20... | collective-permute-start | bytes 3047432 | tf_op jit(solution)/shard_map/ppermute | solution.py:698
  58.5 25.0 %copy-start.4 = (bf16[496,1024]{1,0:T(8,128)(2,1)}, bf16[496,1024]{1,0:T(8,128)(2,1)S(1)}, u32[]{:S(2)}) copy-start(bf16[496,1024]{1,0:T(8,128)(2,1)S(1)} %collective-permute-done.6.refs_3_) | copy-start | bytes 3047428
  66.2 3.8 %collective-permute-start.9 = (bf16[496,1024]{1,0:T(8,128)(2,1)S(1)}, bf16[496,1024]{1,0:T(8,128)(2,1)S(1)}, u32[]{:S(2)}, u32[]{:S(2)}) collective-permute-start(bf16[496,1024]{1,0:T(8,128)(2,1)S(1)} %broadcast_select_fusion.7), channel_id=1, source_target_pairs={{0,1},{1,0},{2,3},{3,2},{4,5},{5,4},{6,7},{7,6},{8,9},{9,8},{10,11... | collective-permute-start | bytes 3047432 | tf_op jit(solution)/shard_map/ppermute | solution.py:701
  66.6 24.9 %collective-permute-start.11 = (bf16[496,1024]{1,0:T(8,128)(2,1)S(1)}, bf16[496,1024]{1,0:T(8,128)(2,1)S(1)}, u32[]{:S(2)}, u32[]{:S(2)}) collective-permute-start(bf16[496,1024]{1,0:T(8,128)(2,1)S(1)} %fusion.refs_0_), channel_id=1, source_target_pairs={{0,2},{1,3},{2,0},{3,1},{4,6},{5,7},{6,4},{7,5},{8,10},{9,11},{10,... | collective-permute-start | bytes 3047432 | tf_op jit(solution)/shard_map/ppermute | solution.py:701
  67.3 24.6 %collective-permute-start.10 = (bf16[496,1024]{1,0:T(8,128)(2,1)S(1)}, bf16[496,1024]{1,0:T(8,128)(2,1)S(1)}, u32[]{:S(2)}, u32[]{:S(2)}) collective-permute-start(bf16[496,1024]{1,0:T(8,128)(2,1)S(1)} %broadcast_select_fusion.2), channel_id=1, source_target_pairs={{0,4},{1,5},{2,6},{3,7},{4,0},{5,1},{6,2},{7,3},{8,12},{9,13},{10,... | collective-permute-start | bytes 3047432 | tf_op jit(solution)/shard_map/ppermute | solution.py:701
  67.9 24.1 %collective-permute-start.7 = (bf16[496,1024]{1,0:T(8,128)(2,1)S(1)}, bf16[496,1024]{1,0:T(8,128)(2,1)S(1)}, u32[]{:S(2)}, u32[]{:S(2)}) collective-permute-start(bf16[496,1024]{1,0:T(8,128)(2,1)S(1)} %collective-permute-done.3), channel_id=1, source_target_pairs={{16,24},{17,25},{18,26},{19,27},{20,28},{21,29},{22,30},{23,31}} | collective-permute-start | bytes 3047432 | tf_op jit(solution)/shard_map/ppermute | solution.py:698
  68.6 26.2 %collective-permute-start.8 = (bf16[496,1024]{1,0:T(8,128)(2,1)S(1)}, bf16[496,1024]{1,0:T(8,128)(2,1)S(1)}, u32[]{:S(2)}, u32[]{:S(2)}) collective-permute-start(bf16[496,1024]{1,0:T(8,128)(2,1)S(1)} %collective-permute-done.4), channel_id=1, source_target_pairs={{8,0},{9,1},{10,2},{11,3},{12,4},{13,5},{14,6},{15,7}} | collective-permute-start | bytes 3047432 | tf_op jit(solution)/shard_map/ppermute | solution.py:698
  94.9 3.5 %collective-permute-start.12 = (bf16[496,1024]{1,0:T(8,128)(2,1)S(1)}, bf16[496,1024]{1,0:T(8,128)(2,1)S(1)}, u32[]{:S(2)}, u32[]{:S(2)}) collective-permute-start(bf16[496,1024]{1,0:T(8,128)(2,1)S(1)} %broadcast_select_fusion.6), channel_id=1, source_target_pairs={{0,1},{1,0},{2,3},{3,2},{4,5},{5,4},{6,7},{7,6},{8,9},{9,8},{10,11... | collective-permute-start | bytes 3047432 | tf_op jit(solution)/shard_map/ppermute | solution.py:701
  95.2 24.9 %collective-permute-start.14 = (bf16[496,1024]{1,0:T(8,128)(2,1)S(1)}, bf16[496,1024]{1,0:T(8,128)(2,1)S(1)}, u32[]{:S(2)}, u32[]{:S(2)}) collective-permute-start(bf16[496,1024]{1,0:T(8,128)(2,1)S(1)} %select_select_fusion.2.refs_0_), channel_id=1, source_target_pairs={{0,2},{1,3},{2,0},{3,1},{4,6},{5,7},{6,4},{7,5},{8,10},{9,11},{10,... | collective-permute-start | bytes 3047432 | tf_op jit(solution)/shard_map/ppermute | solution.py:701
  96.8 26.6 %copy-start.1 = (bf16[1280,256]{1,0:T(8,128)(2,1)S(1)}, bf16[1280,256]{1,0:T(8,128)(2,1)}, u32[]{:S(2)}) copy-start(bf16[1280,256]{1,0:T(8,128)(2,1)} %refs_6_.5) | copy-start | bytes 1966084
  96.9 26.6 %copy-start.2 = (f32[3]{0:T(128)S(1)}, f32[3]{0:T(128)}, u32[]{:S(2)}) copy-start(f32[3]{0:T(128)} %refs_8_.3) | copy-start | bytes 40
  96.9 24.6 %collective-permute-start.13 = (bf16[496,1024]{1,0:T(8,128)(2,1)S(1)}, bf16[496,1024]{1,0:T(8,128)(2,1)S(1)}, u32[]{:S(2)}, u32[]{:S(2)}) collective-permute-start(bf16[496,1024]{1,0:T(8,128)(2,1)S(1)} %broadcast_select_fusion.1), channel_id=1, source_target_pairs={{0,4},{1,5},{2,6},{3,7},{4,0},{5,1},{6,2},{7,3},{8,12},{9,13},{10,... | collective-permute-start | bytes 3047432 | tf_op jit(solution)/shard_map/ppermute | solution.py:701
  120.1 28.4 %copy-start.5 = (bf16[496,1024]{1,0:T(8,128)(2,1)}, bf16[496,1024]{1,0:T(8,128)(2,1)S(1)}, u32[]{:S(2)}) copy-start(bf16[496,1024]{1,0:T(8,128)(2,1)S(1)} %collective-permute-done.14.refs_5_) | copy-start | bytes 3047428
  121.6 26.9 %collective-permute-start.16 = (bf16[496,1024]{1,0:T(8,128)(2,1)S(1)}, bf16[496,1024]{1,0:T(8,128)(2,1)S(1)}, u32[]{:S(2)}, u32[]{:S(2)}) collective-permute-start(bf16[496,1024]{1,0:T(8,128)(2,1)S(1)} %broadcast_select_fusion), channel_id=1, source_target_pairs={{0,4},{1,5},{2,6},{3,7},{4,0},{5,1},{6,2},{7,3},{8,12},{9,13},{10,... | collective-permute-start | bytes 3047432 | tf_op jit(solution)/shard_map/ppermute | solution.py:701
  123.4 25.2 %collective-permute-start.15 = (bf16[496,1024]{1,0:T(8,128)(2,1)S(1)}, bf16[496,1024]{1,0:T(8,128)(2,1)S(1)}, u32[]{:S(2)}, u32[]{:S(2)}) collective-permute-start(bf16[496,1024]{1,0:T(8,128)(2,1)S(1)} %broadcast_select_fusion.5), channel_id=1, source_target_pairs={{0,1},{1,0},{2,3},{3,2},{4,5},{5,4},{6,7},{7,6},{8,9},{9,8},{10,11... | collective-permute-start | bytes 3047432 | tf_op jit(solution)/shard_map/ppermute | solution.py:701
  148.5 2.9 %copy-start.6 = (bf16[496,1024]{1,0:T(8,128)(2,1)}, bf16[496,1024]{1,0:T(8,128)(2,1)S(1)}, u32[]{:S(2)}) copy-start(bf16[496,1024]{1,0:T(8,128)(2,1)S(1)} %collective-permute-done.16.refs_4_) | copy-start | bytes 3047428
  148.7 2.8 %collective-permute-start.17 = (bf16[496,1024]{1,0:T(8,128)(2,1)S(1)}, bf16[496,1024]{1,0:T(8,128)(2,1)S(1)}, u32[]{:S(2)}, u32[]{:S(2)}) collective-permute-start(bf16[496,1024]{1,0:T(8,128)(2,1)S(1)} %broadcast_select_fusion.4), channel_id=1, source_target_pairs={{0,1},{1,0},{2,3},{3,2},{4,5},{5,4},{6,7},{7,6},{8,9},{9,8},{10,11... | collective-permute-start | bytes 3047432 | tf_op jit(solution)/shard_map/ppermute | solution.py:701
  151.4 1.0 copy-start.7

commit v5 on v4

--- a/solution.py
+++ b/solution.py
@@ -46,6 +46,7 @@
         self.shifted = [k for k in (1, 2, 3) if RATE * k < self.height]
         self.direct = [k for k in range(4) if k not in self.shifted]
         self.n_sh = len(self.shifted)
+        self.together = 2 if n % 2 == 0 and self.n_sh == 1 else 1
         row = lambda k, a: [1 + 9 * (k - 1) + 3 * a + b for b in range(3)]
         still = [row(k, 1) for k in self.direct[1:]]
         self.loads = [[0] + (still[0] if still else [])] + still[1:]
@@ -320,8 +321,8 @@
     mid_refs = refs[1:1 + n_sh]
     s_hbm = refs[1 + n_sh]
     refs = refs[2 + n_sh:]
-    aux_ref, all_ref, w28_ref, wproj_ref, wcls_ref, cw_ref, xt_hbm = refs[:7]
-    refs = refs[7:]
+    aux_ref, all_ref, w28_ref, wproj_ref, wturn_ref, wcls_ref, cw_ref, xt_hbm = refs[:8]
+    refs = refs[8:]
     if last:
         prev_g, prev_p, prev_c = refs[:3]
         refs = refs[3:]
@@ -332,6 +333,7 @@
     xt_copy = pltpu.make_async_copy(xt_hbm.at[field], xt_ref, sem_xt)
     step = pl.program_id(0)
     edge_rows = rows - 1
+    nb, turns = plan.together, n // plan.together
 
     def finish(value, prev):
         grad = value.astype(BF16)
@@ -358,8 +360,8 @@
         zero = jnp.zeros((edge_rows, cols, dbuf.shape[2]), BF16)
         dbuf[:edge_rows] = zero
         dbuf[edge_rows + plan.height:] = zero
-        pad[:, :EDGE, :] = jnp.zeros((rows, EDGE, c_out), F32)
-        pad[:, EDGE + cols:, :] = jnp.zeros((rows, EDGE, c_out), F32)
+        pad[:, :EDGE, :] = jnp.zeros((nb * rows, EDGE, c_out), F32)
+        pad[:, EDGE + cols:, :] = jnp.zeros((nb * rows, EDGE, c_out), F32)
         total = jnp.zeros((1, c_in), F32)
         for j in range(n):
             extra = all_ref[j].astype(F32)
@@ -370,18 +372,17 @@
         for copy in side_copies():
             copy.wait()
 
-    @pl.when(step < n)
+    @pl.when(step < turns)
     def _():
-        block = step
-        cat5 = catall.at[block]
+        cat5 = catall.at[step]
         for k in range(4):
             part = slice(k * c_out, (k + 1) * c_out)
             if k in plan.shifted:
                 at = plan.shifted.index(k)
                 r = RATE * k
                 pre = mid_refs[at]
-                for i in range(rows):
-                    h = block * rows + i
+                for i in range(nb * rows):
+                    h = step * nb * rows + i
                     line = pre[i]
                     for side, src in ((0, h - r), (1, h)):
                         last_row = plan.height - r - 1
@@ -391,40 +392,44 @@
                     cat5[i * cols:(i + 1) * cols, part] = jnp.maximum(line, 0.0).astype(BF16)
             else:
                 at = plan.direct.index(k)
-                cat5[:, part] = cat_ref[:, at * c_out:(at + 1) * c_out]
+                cat5[:, part] = cat_ref[:, :, at * c_out:(at + 1) * c_out].reshape(nb * pix, c_out)
         pool_act = jnp.maximum(pact[0:1, :], 0.0).astype(BF16)
-        cat5[:, 4 * c_out:] = jnp.broadcast_to(pool_act, (pix, c_out))
+        cat5[:, 4 * c_out:] = jnp.broadcast_to(pool_act, (nb * pix, c_out))
         y_pre = nn(cat5[...], wproj_ref[...])
         y_act = jnp.maximum(y_pre, 0.0).astype(BF16)
-        logits = nt(wcls_ref[...], y_act)
+        ybuf[step] = y_act
         row = lax.broadcasted_iota(jnp.int32, (16, pix), 0)
         live = row < plan.classes
-        expo = jnp.where(live, jnp.exp(logits), 0.0)
-        prob = expo / jnp.sum(expo, axis=0, keepdims=True)
-        label = jnp.broadcast_to(aux_ref[3:4, :pix].astype(F32), (16, pix))
-        onehot = jnp.where(label == row.astype(F32), 1.0, 0.0)
-        weight = jnp.zeros((16, pix), F32)
-        for c in range(plan.classes):
-            weight = jnp.where(label == float(c), cw_ref[c], weight)
-        d_logits = jnp.where(
-            live, (prob - onehot) * weight * (LOSS_SCALE / plan.total), 0.0
-        ).astype(BF16)
-        d_y = jnp.where(y_pre > 0, tn(d_logits, wcls_ref[...]), 0.0).astype(BF16)
-        ybuf[block] = y_act
-        lbuf[block] = d_logits
-        dybuf[block] = d_y
+        for sub in range(nb):
+            cells = slice(sub * pix, (sub + 1) * pix)
+            logits = nt(wcls_ref[...], y_act[cells])
+            expo = jnp.where(live, jnp.exp(logits), 0.0)
+            prob = expo / jnp.sum(expo, axis=0, keepdims=True)
+            label = jnp.broadcast_to(aux_ref[sub, 3:4, :pix].astype(F32), (16, pix))
+            onehot = jnp.where(label == row.astype(F32), 1.0, 0.0)
+            weight = jnp.zeros((16, pix), F32)
+            for c in range(plan.classes):
+                weight = jnp.where(label == float(c), cw_ref[c], weight)
+            d_logits = jnp.where(
+                live, (prob - onehot) * weight * (LOSS_SCALE / plan.total), 0.0
+            ).astype(BF16)
+            lbuf[step * nb + sub] = d_logits
+            dybuf[step, cells] = jnp.where(
+                y_pre[cells] > 0, tn(d_logits, wcls_ref[...]), 0.0
+            ).astype(BF16)
+        d_y = dybuf[step]
         for k in range(4):
             want = [tab[flags + n + 3 * k + b] for b in range(3)]
             part = slice(k * c_out, (k + 1) * c_out)
 
             @pl.when((want[0] >= 0) | (want[1] >= 0) | (want[2] >= 0))
             def _(k=k, want=want, part=part):
-                d_cat = nt(d_y, wproj_ref[part, :])
+                d_cat = nn(d_y, wturn_ref[:, part])
                 d_k = jnp.where(cat5[:, part] > 0, d_cat, 0.0).astype(BF16)
-                d_k = d_k.reshape(rows, cols, c_out)
+                d_k = d_k.reshape(nb * rows, cols, c_out)
                 if k > 0:
                     pad[:, EDGE:EDGE + cols, :] = d_k.astype(F32)
-                at = pl.ds(block * rows + edge_rows, rows)
+                at = pl.ds(step * nb * rows + edge_rows, nb * rows)
                 for b in range(3):
                     if k == 0 and b != 1:
                         continue
@@ -438,7 +443,7 @@
                             first = EDGE + (1 - b) * RATE * k
                             dbuf[at, :, lanes] = pad[:, first:first + cols, :].astype(BF16)
 
-    @pl.when(step == n - 1)
+    @pl.when(step == turns - 1)
     def _():
         all_dy = dybuf[...].reshape(n * pix, c_out)
         pool = wproj_ref[4 * c_out:, :]
@@ -452,11 +457,13 @@
         window = pl.ds(pl.multiple_of(tab[flags + n + 13], 128), plan.window)
         g_proj = jnp.zeros((c_out, plan.window), F32)
         g_cls = jnp.zeros((16, c_out), F32)
-        for j in range(n):
+        for j in range(turns):
             g_proj = g_proj + nn(
                 nt(identity(c_out), dybuf[j]).astype(BF16), catall[j, :, window]
             )
-            g_cls = g_cls + nn(lbuf[j], ybuf[j])
+        for j in range(n):
+            cells = slice(j % nb * pix, (j % nb + 1) * pix)
+            g_cls = g_cls + nn(lbuf[j], ybuf[j // nb, cells])
         gp[:plan.window, :] = g_proj.T
         index = tab[flags + n + 12]
         first = pl.multiple_of(index * plan.proj_rows - tab[flags + n + 13], 32)
@@ -475,13 +482,13 @@
             sems.at[slot, t],
         )
 
-    @pl.when(step == n)
+    @pl.when(step == turns)
     def _():
         xt_copy.wait()
 
-    @pl.when(step >= n)
+    @pl.when(step >= turns)
     def _():
-        part = step - n
+        part = step - turns
         parity = lax.rem(part, 2)
         mine = pl.ds(pl.multiple_of(part * unit_rows, unit_rows), unit_rows)
 
@@ -574,43 +581,45 @@
                 drain(part, parity)
 
 
-def run_field(plan, field, tab, state, w_in, w_proj, wcls, cw, prev):
+def run_field(plan, field, tab, state, w_in, w_proj, w_turn, wcls, cw, prev):
     n, rows, cols, pix = plan.n, plan.rows, plan.cols, plan.pix
     c_in, c_out, n_sh = plan.c_in, plan.c_out, plan.n_sh
     unit_rows, depth = plan.unit_rows, plan.depth
     last = prev is not None
+    nb, turns = plan.together, n // plan.together
     xt, cat, s, aux = state
 
     def blk(i):
-        return jnp.minimum(i, n - 1)
+        return jnp.minimum(i, turns - 1)
 
     def part(i):
-        return jnp.maximum(i - n, 0)
+        return jnp.maximum(i - turns, 0)
 
     in_specs = [
         pl.BlockSpec(
-            (None, None, pix, len(plan.direct) * c_out), lambda i, t: (field, blk(i), 0, 0)
+            (None, nb, pix, len(plan.direct) * c_out), lambda i, t: (field, blk(i), 0, 0)
         ),
     ]
     operands = [cat]
     for at in range(n_sh):
         in_specs.append(pl.BlockSpec(
-            (None, None, rows, cols, c_out),
+            (None, None, nb * rows, cols, c_out),
             lambda i, t, at=at: (3 * at + 1, field, blk(i), 0, 0),
         ))
         operands.append(s)
     in_specs.append(pl.BlockSpec(memory_space=pl.ANY))
     operands.append(s)
     in_specs += [
-        pl.BlockSpec((None, None, EXTRA, c_in), lambda i, t: (field, blk(i), 0, 0)),
+        pl.BlockSpec((None, nb, EXTRA, c_in), lambda i, t: (field, blk(i), 0, 0)),
         pl.BlockSpec((None, n, EXTRA, c_in), lambda i, t: (field, 0, 0, 0)),
         pl.BlockSpec((1, c_in, c_out), lambda i, t: (28, 0, 0)),
         pl.BlockSpec((5 * c_out, c_out), lambda i, t: (0, 0)),
+        pl.BlockSpec((c_out, 4 * c_out), lambda i, t: (0, 0)),
         pl.BlockSpec((16, c_out), lambda i, t: (0, 0)),
         pl.BlockSpec(memory_space=pltpu.SMEM),
         pl.BlockSpec(memory_space=pl.ANY),
     ]
-    operands += [aux, aux, w_in, w_proj, wcls, cw, xt]
+    operands += [aux, aux, w_in, w_proj, w_turn, wcls, cw, xt]
     kind = F32 if last else BF16
     inner = pl.BlockSpec((None, depth, unit_rows, c_out), lambda i, t: (part(i), 0, 0, 0))
     small = [
@@ -629,7 +638,7 @@
         functools.partial(field_kernel, plan, field, last),
         grid_spec=pltpu.PrefetchScalarGridSpec(
             num_scalar_prefetch=1,
-            grid=(2 * n,),
+            grid=(turns + n,),
             in_specs=in_specs,
             out_specs=[main_spec] + small,
             scratch_shapes=[
@@ -637,15 +646,15 @@
                 for k in plan.shifted for _ in range(2)
             ] + [
                 pltpu.VMEM((plan.height + 2 * (rows - 1), cols, plan.n_slots * c_out), BF16),
-                pltpu.VMEM((rows, cols + 2 * EDGE, c_out), F32),
+                pltpu.VMEM((nb * rows, cols + 2 * EDGE, c_out), F32),
                 pltpu.VMEM((16, c_in), F32),
-                pltpu.VMEM((n, pix, c_out), BF16),
+                pltpu.VMEM((turns, nb * pix, c_out), BF16),
                 pltpu.VMEM((n, 16, pix), BF16),
-                pltpu.VMEM((n, pix, c_out), BF16),
+                pltpu.VMEM((turns, nb * pix, c_out), BF16),
                 pltpu.VMEM((max(plan.window, c_out), c_out), F32),
                 pltpu.VMEM((16, c_out), F32),
                 pltpu.VMEM((16, c_out), F32),
-                pltpu.VMEM((n, pix, 5 * c_out), BF16),
+                pltpu.VMEM((turns, nb * pix, 5 * c_out), BF16),
                 pltpu.VMEM((unit_rows, 3 * c_out), F32),
                 pltpu.VMEM((2, depth if last else 1, unit_rows, c_out), F32),
                 pltpu.VMEM((n, c_in, pix), BF16),
@@ -713,7 +722,7 @@
             value = arrived if value is None else jnp.where(here == s, arrived, value)
         return value
 
-    common = (w_in, w_proj, wcls, class_weight)
+    w_turn = w_proj[:4 * plan.c_out].T
     hops = list(range(1, n_bits)) + [0]
     rounds = n + n_bits - 1
     ups, downs, raw = [x], [x], (x, x)
@@ -753,12 +762,16 @@
         if slots:
             state = run_blocks(plan, slots, metas[q], w_in, state)
         if q == min(n, rounds - 1):
-            grads = tuple(run_field(plan, 0, tab, state, *common, None))
+            grads = tuple(run_field(
+                plan, 0, tab, state, w_in, w_proj, w_turn, wcls, class_weight, None
+            ))
         if t < rounds:
-            live = (ups, downs, values, moves, state, grads, metas, tab, wcls)
+            live = (ups, downs, values, moves, state, grads, metas, tab, wcls, w_turn)
             live = lax.optimization_barrier(live)
-            ups, downs, values, moves, state, grads, metas, tab, wcls = live
-    avg_in, avg_proj, avg_cls = run_field(plan, 1, tab, state, *common, grads)
+            ups, downs, values, moves, state, grads, metas, tab, wcls, w_turn = live
+    avg_in, avg_proj, avg_cls = run_field(
+        plan, 1, tab, state, w_in, w_proj, w_turn, wcls, class_weight, grads
+    )
     return avg_in[None], avg_proj[None], avg_cls[None, :, :plan.classes]
 
 

time: 194 us -> 193 us (level)
  waiting for transfers between devices: 44.4 us -> 42.3 us
  Pallas kernels: 110 us -> 108 us
    pallas_call x2, Pallas kernels: 51.9 us -> 49.5 us  [run_field(): pl.pallas_call(functools.partial(field_kernel, plan, field, last), grid_s...]
where the time goes in v5:
time: 193 us
  Pallas kernels  108 us (56%)
  waiting for transfers between devices  42.3 us (22%)
  starting transfers between devices  22.7 us (12%)
  other arithmetic  8.75 us (5%)
  local copies, waits for them, and re-layouts  7.46 us (4%)
  between operations  2.92 us (2%)
    pallas_call x5, Pallas kernels, run_blocks(): pl.pallas_call(functools.partial(block_kernel, plan, len(arrays), len(slo...  56.5 us
    pallas_call x2, Pallas kernels, run_field(): pl.pallas_call(functools.partial(field_kernel, plan, field, last), grid_s...  49.5 us
    ppermute x12, waiting for transfers between devices, hop(): return lax.ppermute(value, 'rep', [(r, r ^ 1 << b) for r in range(reps)])  31.3 us
    ppermute x6, starting transfers between devices, along(): return lax.ppermute(value, 'space', pairs)  11.4 us
    ppermute x12, starting transfers between devices, hop(): return lax.ppermute(value, 'rep', [(r, r ^ 1 << b) for r in range(reps)])  11.3 us
    ppermute x6, waiting for transfers between devices, along(): return lax.ppermute(value, 'space', pairs)  11 us
    another operation x7, other arithmetic, per_device(): jnp.stack([jnp.stack([(top if f else 0) + jnp.int32(n_bits * at if f and...  5.14 us
  transfers between devices with their start and end apart: 18, of which 10 were waited for; matrix products, arithmetic and copies ran while one was open for 5% of the time, Pallas kernels for 35%

profile of v5, /device:TPU:0, one launch (start us, length us, event | category | flops | bytes accessed | tf_op | source)
XLA Modules:
  0.0 192.5 jit_solution(16197322801105701326)
XLA Ops:
  0.6 0.7 convert_reduce_fusion
  1.4 0.6 pad.8.lab_ref
  2.0 2.3 %pack.1.refs_0_ = bf16[496,1024]{1,0:T(8,128)(2,1)} custom-call(bf16[480,1024]{1,0:T(8,128)(2,1)} %bitcast.39, f32[1,1024]{1,0:T(1,128)} %pad.8.lab_ref), custom_call_target="tpu_custom_call" | custom-call | tf_op jit(solution)/shard_map/pack/pallas_call | solution.py:688
  4.3 5.9 %collective-permute-start = (bf16[496,1024]{1,0:T(8,128)(2,1)}, bf16[496,1024]{1,0:T(8,128)(2,1)}, u32[]{:S(2)}, u32[]{:S(2)}) collective-permute-start(bf16[496,1024]{1,0:T(8,128)(2,1)} %pack.1.refs_0_), channel_id=1, source_target_pairs={{0,8},{8,16},{16,24},{1,9},{9,17},{17,25},{2,10},{10,18},{18,26},{... | collective-permute-start | bytes 3047432 | tf_op jit(solution)/shard_map/ppermute | solution.py:707
  10.2 1.3 collective-permute-start.1
  11.5 1.6 collective-permute-start.2
  15.1 0.7 constant_dynamic-slice_fusion.1
  15.8 0.6 fusion.9
  16.3 1.3 fusion.5
  17.6 1.3 fusion.1
  18.9 1.1 slice.48
  20.2 0.7 pad.9.refs_8_
  20.9 0.7 constant_dynamic-slice_fusion
  21.6 1.3 fusion.7
  22.9 1.3 fusion.3
  24.2 1.2 copy-done
  25.4 7.9 %block_forward.5 = (bf16[2,4,1024,480]{3,2,1,0:T(8,128)(2,1)}, bf16[2,4,480,768]{3,2,1,0:T(8,128)(2,1)}, f32[3,2,20,96,256]{4,3,2,1,0:T(8,128)}, bf16[2,4,16,1024]{3,2,1,0:T(8,128)(2,1)S(1)}) custom-call(s32[1,3]{1,0:T(1,128)S(1)} %get-tuple-element.228.meta, bf16[496,1024]{1,0:T(8,128)(2,1)S(1)} %copy-done, bf16[29,1024,256]{2,1,0:T(8,128)(2,1)} %refs_5_.3), custom_call_target="tpu_custom_call" | custom-call | flops 4026531840 | bytes 40000000 | tf_op jit(solution)/shard_map/block_forward/pallas_call | solution.py:282
  33.4 2.9 %collective-permute-done.1 = bf16[496,1024]{1,0:T(8,128)(2,1)S(1)} collective-permute-done((bf16[496,1024]{1,0:T(8,128)(2,1)}, bf16[496,1024]{1,0:T(8,128)(2,1)S(1)}, u32[]{:S(2)}, u32[]{:S(2)}) %collective-permute-start.1) | collective-permute-done | bytes 1015840 | tf_op jit(solution)/shard_map/ppermute | solution.py:707
  36.3 1.7 select_select_fusion.1.refs_0_
  38.0 1.6 collective-permute-start.6
  39.7 1.6 collective-permute-start.5
  41.3 0.7 collective-permute-start.3
  42.0 1.3 collective-permute-start.4
  43.3 8.0 %block_forward.6 = (bf16[2,4,1024,480]{3,2,1,0:T(8,128)(2,1)}, bf16[2,4,480,768]{3,2,1,0:T(8,128)(2,1)}, f32[3,2,20,96,256]{4,3,2,1,0:T(8,128)}, bf16[2,4,16,1024]{3,2,1,0:T(8,128)(2,1)S(1)}) custom-call(s32[1,3]{1,0:T(1,128)S(1)} %get-tuple-element.118.meta, ...), custom_call_target="tpu_custom_call", output_to_operand_aliasing={{0}: (3, {}), {1}: (4, {}), {2}: (5, {}), {3}: (6, {})} | custom-call | flops 4026531840 | bytes 40000000 | tf_op jit(solution)/shard_map/block_forward/pallas_call | solution.py:282
  51.3 9.8 %collective-permute-done.6.refs_3_ = bf16[496,1024]{1,0:T(8,128)(2,1)S(1)} collective-permute-done((bf16[496,1024]{1,0:T(8,128)(2,1)S(1)}, bf16[496,1024]{1,0:T(8,128)(2,1)S(1)}, u32[]{:S(2)}, u32[]{:S(2)}) %collective-permute-start.6) | collective-permute-done | bytes 1015840 | tf_op jit(solution)/shard_map/ppermute | solution.py:710
  61.1 1.4 collective-permute-done.5.refs_2_
  62.5 5.3 %collective-permute-done.4 = bf16[496,1024]{1,0:T(8,128)(2,1)S(1)} collective-permute-done((bf16[496,1024]{1,0:T(8,128)(2,1)S(1)}, bf16[496,1024]{1,0:T(8,128)(2,1)S(1)}, u32[]{:S(2)}, u32[]{:S(2)}) %collective-permute-start.4) | collective-permute-done | bytes 1015840 | tf_op jit(solution)/shard_map/ppermute | solution.py:707
  68.1 0.6 collective-permute-start.11
  68.8 0.6 collective-permute-start.10
  69.4 0.7 collective-permute-start.7
  70.1 1.5 collective-permute-start.8
  71.6 13.5 %block_forward.7 = (bf16[2,4,1024,480]{3,2,1,0:T(8,128)(2,1)}, bf16[2,4,480,768]{3,2,1,0:T(8,128)(2,1)}, f32[3,2,20,96,256]{4,3,2,1,0:T(8,128)}, bf16[2,4,16,1024]{3,2,1,0:T(8,128)(2,1)S(1)}) custom-call(s32[2,3]{1,0:T(2,128)S(1)} %pad_add_fusion.meta, ...), custom_call_target="tpu_custom_call", output_to_operand_aliasing={{0}: (6, {}), {1}: (7, {}), {2}: (8, {}), {3}: (9, {})} | custom-call | flops 8053063680 | bytes 60000000 | tf_op jit(solution)/shard_map/block_forward/pallas_call | solution.py:282
  85.1 7.9 %collective-permute-done.11.refs_2_ = bf16[496,1024]{1,0:T(8,128)(2,1)S(1)} collective-permute-done((bf16[496,1024]{1,0:T(8,128)(2,1)S(1)}, bf16[496,1024]{1,0:T(8,128)(2,1)S(1)}, u32[]{:S(2)}, u32[]{:S(2)}) %collective-permute-start.11) | collective-permute-done | bytes 1015840 | tf_op jit(solution)/shard_map/ppermute | solution.py:710
  93.0 0.4 collective-permute-done.10.refs_2_
  93.4 2.8 %collective-permute-done.8 = bf16[496,1024]{1,0:T(8,128)(2,1)S(1)} collective-permute-done((bf16[496,1024]{1,0:T(8,128)(2,1)S(1)}, bf16[496,1024]{1,0:T(8,128)(2,1)S(1)}, u32[]{:S(2)}, u32[]{:S(2)}) %collective-permute-start.8) | collective-permute-done | bytes 1015840 | tf_op jit(solution)/shard_map/ppermute | solution.py:707
  96.6 1.6 collective-permute-start.14
  98.3 1.6 collective-permute-start.13
  99.9 13.5 %block_forward.8 = (bf16[2,4,1024,480]{3,2,1,0:T(8,128)(2,1)}, bf16[2,4,480,768]{3,2,1,0:T(8,128)(2,1)}, f32[3,2,20,96,256]{4,3,2,1,0:T(8,128)}, bf16[2,4,16,1024]{3,2,1,0:T(8,128)(2,1)S(1)}) custom-call(s32[2,3]{1,0:T(2,128)S(1)} %pad_add_fusion.1.meta, ...), custom_call_target="tpu_custom_call", output_to_operand_aliasing={{0}: (6, {}), {1}: (7, {}), {2}: (8, {}), {3}: (9, {})} | custom-call | flops 8053063680 | bytes 60000000 | tf_op jit(solution)/shard_map/block_forward/pallas_call | solution.py:282
  113.4 8.1 %collective-permute-done.14.refs_5_ = bf16[496,1024]{1,0:T(8,128)(2,1)S(1)} collective-permute-done((bf16[496,1024]{1,0:T(8,128)(2,1)S(1)}, bf16[496,1024]{1,0:T(8,128)(2,1)S(1)}, u32[]{:S(2)}, u32[]{:S(2)}) %collective-permute-start.14) | collective-permute-done | bytes 1015840 | tf_op jit(solution)/shard_map/ppermute | solution.py:710
  121.6 1.4 collective-permute-done.13.refs_1_
  123.1 1.6 collective-permute-start.16
  124.9 23.8 %field_grads.2 = (bf16[4,8,256,256]{3,2,1,0:T(8,128)(2,1)}, bf16[320,256]{1,0:T(8,128)(2,1)S(1)}, bf16[64,128]{1,0:T(8,128)(2,1)S(1)}) custom-call(s32[210]{0:T(256)S(1)} %bitcast.37, bf16[2,4,480,768]{3,2,1,0:T(8,128)(2,1)} %get-tuple-element.202.refs_0_.refs_8_, f32[3,2,20,96,256]{4,3,2,1,0:T(8,128)} %get-tuple-element.203.refs_1_.refs_2_.refs_9_, ...), custom_call_target="tpu_custom_call" | custom-call | flops 10000000000 | bytes 90000000 | tf_op jit(solution)/shard_map/field_grads/pallas_call | solution.py:637
  148.8 0.5 collective-permute-start.17
  149.4 2.2 %collective-permute-done.17.refs_3_ = bf16[496,1024]{1,0:T(8,128)(2,1)S(1)} collective-permute-done((bf16[496,1024]{1,0:T(8,128)(2,1)S(1)}, bf16[496,1024]{1,0:T(8,128)(2,1)S(1)}, u32[]{:S(2)}, u32[]{:S(2)}) %collective-permute-start.17) | collective-permute-done | bytes 1015840 | tf_op jit(solution)/shard_map/ppermute | solution.py:710
  151.6 1.0 copy-done.7
  152.6 13.5 %block_forward.9 = (bf16[2,4,1024,480]{3,2,1,0:T(8,128)(2,1)}, bf16[2,4,480,768]{3,2,1,0:T(8,128)(2,1)}, f32[3,2,20,96,256]{4,3,2,1,0:T(8,128)}, bf16[2,4,16,1024]{3,2,1,0:T(8,128)(2,1)S(1)}) custom-call(s32[2,3]{1,0:T(2,128)S(1)} %pad_add_fusion.2.meta, ...), custom_call_target="tpu_custom_call", output_to_operand_aliasing={{0}: (8, {}), {1}: (9, {}), {2}: (10, {}), {3}: (11, {})} | custom-call | flops 8053063680 | bytes 60000000 | tf_op jit(solution)/shard_map/block_forward/pallas_call | solution.py:282
  166.1 25.8 %field_grads.3 = (f32[7424,256]{1,0:T(8,128)}, f32[320,256]{1,0:T(8,128)}, f32[64,128]{1,0:T(8,128)S(1)}) custom-call(s32[210]{0:T(256)S(1)} %bitcast.38, bf16[2,4,480,768]{3,2,1,0:T(8,128)(2,1)} %get-tuple-element.205.refs_0_, f32[3,2,20,96,256]{4,3,2,1,0:T(8,128)} %get-tuple-element.206.refs_1_.refs_2_, ...), custom_call_target="tpu_custom_call" | custom-call | flops 10000000000 | bytes 90000000 | tf_op jit(solution)/shard_map/field_grads/pallas_call | solution.py:637
  191.9 0.6 copy.29
  (41 shorter events, 1.8 us)
Async XLA Ops:
  4.3 29.0 %collective-permute-start = (bf16[496,1024]{1,0:T(8,128)(2,1)}, bf16[496,1024]{1,0:T(8,128)(2,1)}, u32[]{:S(2)}, u32[]{:S(2)}) collective-permute-start(bf16[496,1024]{1,0:T(8,128)(2,1)} %pack.1.refs_0_), channel_id=1, source_target_pairs={{0,8},{8,16},{16,24},{1,9},{9,17},{17,25},{2,10},{10,18},{18,26},{... | collective-permute-start | bytes 3047432 | tf_op jit(solution)/shard_map/ppermute | solution.py:707
  10.2 26.0 %collective-permute-start.1 = (bf16[496,1024]{1,0:T(8,128)(2,1)}, bf16[496,1024]{1,0:T(8,128)(2,1)S(1)}, u32[]{:S(2)}, u32[]{:S(2)}) collective-permute-start(bf16[496,1024]{1,0:T(8,128)(2,1)} %pack.1.refs_0_), channel_id=1, source_target_pairs={{8,0},{16,8},{24,16},{9,1},{17,9},{25,17},{10,2},{18,10},{26,18},{... | collective-permute-start | bytes 3047432 | tf_op jit(solution)/shard_map/ppermute | solution.py:707
  11.5 24.7 %collective-permute-start.2 = (bf16[496,1024]{1,0:T(8,128)(2,1)}, bf16[496,1024]{1,0:T(8,128)(2,1)S(1)}, u32[]{:S(2)}, u32[]{:S(2)}) collective-permute-start(bf16[496,1024]{1,0:T(8,128)(2,1)} %pack.1.refs_0_), channel_id=1, source_target_pairs={{0,2},{1,3},{2,0},{3,1},{4,6},{5,7},{6,4},{7,5},{8,10},{9,11},{10,... | collective-permute-start | bytes 3047432 | tf_op jit(solution)/shard_map/ppermute | solution.py:710
  24.2 1.2 copy-start
  36.3 15.0 %copy-start.3 = (bf16[496,1024]{1,0:T(8,128)(2,1)}, bf16[496,1024]{1,0:T(8,128)(2,1)S(1)}, u32[]{:S(2)}) copy-start(bf16[496,1024]{1,0:T(8,128)(2,1)S(1)} %collective-permute-done.2.refs_3_) | copy-start | bytes 3047428
  38.0 23.1 %collective-permute-start.6 = (bf16[496,1024]{1,0:T(8,128)(2,1)S(1)}, bf16[496,1024]{1,0:T(8,128)(2,1)S(1)}, u32[]{:S(2)}, u32[]{:S(2)}) collective-permute-start(bf16[496,1024]{1,0:T(8,128)(2,1)S(1)} %select_select_fusion.1.refs_0_), channel_id=1, source_target_pairs={{0,2},{1,3},{2,0},{3,1},{4,6},{5,7},{6,4},{7,5},{8,10},{9,11},{10,... | collective-permute-start | bytes 3047432 | tf_op jit(solution)/shard_map/ppermute | solution.py:710
  39.7 22.8 %collective-permute-start.5 = (bf16[496,1024]{1,0:T(8,128)(2,1)S(1)}, bf16[496,1024]{1,0:T(8,128)(2,1)S(1)}, u32[]{:S(2)}, u32[]{:S(2)}) collective-permute-start(bf16[496,1024]{1,0:T(8,128)(2,1)S(1)} %broadcast_select_fusion.3), channel_id=1, source_target_pairs={{0,4},{1,5},{2,6},{3,7},{4,0},{5,1},{6,2},{7,3},{8,12},{9,13},{10,... | collective-permute-start | bytes 3047432 | tf_op jit(solution)/shard_map/ppermute | solution.py:710
  41.3 21.2 %collective-permute-start.3 = (bf16[496,1024]{1,0:T(8,128)(2,1)}, bf16[496,1024]{1,0:T(8,128)(2,1)S(1)}, u32[]{:S(2)}, u32[]{:S(2)}) collective-permute-start(bf16[496,1024]{1,0:T(8,128)(2,1)} %collective-permute-done), channel_id=1, source_target_pairs={{8,16},{16,24},{9,17},{17,25},{10,18},{18,26},{11,19},{19,27},{12,... | collective-permute-start | bytes 3047432 | tf_op jit(solution)/shard_map/ppermute | solution.py:707
  42.0 25.8 %collective-permute-start.4 = (bf16[496,1024]{1,0:T(8,128)(2,1)S(1)}, bf16[496,1024]{1,0:T(8,128)(2,1)S(1)}, u32[]{:S(2)}, u32[]{:S(2)}) collective-permute-start(bf16[496,1024]{1,0:T(8,128)(2,1)S(1)} %collective-permute-done.1), channel_id=1, source_target_pairs={{8,0},{16,8},{9,1},{17,9},{10,2},{18,10},{11,3},{19,11},{12,4},{20... | collective-permute-start | bytes 3047432 | tf_op jit(solution)/shard_map/ppermute | solution.py:707
  61.1 24.0 %copy-start.4 = (bf16[496,1024]{1,0:T(8,128)(2,1)}, bf16[496,1024]{1,0:T(8,128)(2,1)S(1)}, u32[]{:S(2)}) copy-start(bf16[496,1024]{1,0:T(8,128)(2,1)S(1)} %collective-permute-done.6.refs_3_) | copy-start | bytes 3047428
  67.8 3.7 %collective-permute-start.9 = (bf16[496,1024]{1,0:T(8,128)(2,1)S(1)}, bf16[496,1024]{1,0:T(8,128)(2,1)S(1)}, u32[]{:S(2)}, u32[]{:S(2)}) collective-permute-start(bf16[496,1024]{1,0:T(8,128)(2,1)S(1)} %broadcast_select_fusion.7), channel_id=1, source_target_pairs={{0,1},{1,0},{2,3},{3,2},{4,5},{5,4},{6,7},{7,6},{8,9},{9,8},{10,11... | collective-permute-start | bytes 3047432 | tf_op jit(solution)/shard_map/ppermute | solution.py:710
  68.1 24.9 %collective-permute-start.11 = (bf16[496,1024]{1,0:T(8,128)(2,1)S(1)}, bf16[496,1024]{1,0:T(8,128)(2,1)S(1)}, u32[]{:S(2)}, u32[]{:S(2)}) collective-permute-start(bf16[496,1024]{1,0:T(8,128)(2,1)S(1)} %fusion.refs_0_), channel_id=1, source_target_pairs={{0,2},{1,3},{2,0},{3,1},{4,6},{5,7},{6,4},{7,5},{8,10},{9,11},{10,... | collective-permute-start | bytes 3047432 | tf_op jit(solution)/shard_map/ppermute | solution.py:710
  68.8 24.6 %collective-permute-start.10 = (bf16[496,1024]{1,0:T(8,128)(2,1)S(1)}, bf16[496,1024]{1,0:T(8,128)(2,1)S(1)}, u32[]{:S(2)}, u32[]{:S(2)}) collective-permute-start(bf16[496,1024]{1,0:T(8,128)(2,1)S(1)} %broadcast_select_fusion.2), channel_id=1, source_target_pairs={{0,4},{1,5},{2,6},{3,7},{4,0},{5,1},{6,2},{7,3},{8,12},{9,13},{10,... | collective-permute-start | bytes 3047432 | tf_op jit(solution)/shard_map/ppermute | solution.py:710
  69.4 24.1 %collective-permute-start.7 = (bf16[496,1024]{1,0:T(8,128)(2,1)S(1)}, bf16[496,1024]{1,0:T(8,128)(2,1)S(1)}, u32[]{:S(2)}, u32[]{:S(2)}) collective-permute-start(bf16[496,1024]{1,0:T(8,128)(2,1)S(1)} %collective-permute-done.3), channel_id=1, source_target_pairs={{16,24},{17,25},{18,26},{19,27},{20,28},{21,29},{22,30},{23,31}} | collective-permute-start | bytes 3047432 | tf_op jit(solution)/shard_map/ppermute | solution.py:707
  70.1 26.2 %collective-permute-start.8 = (bf16[496,1024]{1,0:T(8,128)(2,1)S(1)}, bf16[496,1024]{1,0:T(8,128)(2,1)S(1)}, u32[]{:S(2)}, u32[]{:S(2)}) collective-permute-start(bf16[496,1024]{1,0:T(8,128)(2,1)S(1)} %collective-permute-done.4), channel_id=1, source_target_pairs={{8,0},{9,1},{10,2},{11,3},{12,4},{13,5},{14,6},{15,7}} | collective-permute-start | bytes 3047432 | tf_op jit(solution)/shard_map/ppermute | solution.py:707
  96.4 3.5 %collective-permute-start.12 = (bf16[496,1024]{1,0:T(8,128)(2,1)S(1)}, bf16[496,1024]{1,0:T(8,128)(2,1)S(1)}, u32[]{:S(2)}, u32[]{:S(2)}) collective-permute-start(bf16[496,1024]{1,0:T(8,128)(2,1)S(1)} %broadcast_select_fusion.6), channel_id=1, source_target_pairs={{0,1},{1,0},{2,3},{3,2},{4,5},{5,4},{6,7},{7,6},{8,9},{9,8},{10,11... | collective-permute-start | bytes 3047432 | tf_op jit(solution)/shard_map/ppermute | solution.py:710
  96.6 24.9 %collective-permute-start.14 = (bf16[496,1024]{1,0:T(8,128)(2,1)S(1)}, bf16[496,1024]{1,0:T(8,128)(2,1)S(1)}, u32[]{:S(2)}, u32[]{:S(2)}) collective-permute-start(bf16[496,1024]{1,0:T(8,128)(2,1)S(1)} %select_select_fusion.2.refs_0_), channel_id=1, source_target_pairs={{0,2},{1,3},{2,0},{3,1},{4,6},{5,7},{6,4},{7,5},{8,10},{9,11},{10,... | collective-permute-start | bytes 3047432 | tf_op jit(solution)/shard_map/ppermute | solution.py:710
  98.3 26.5 %copy-start.1 = (bf16[1280,256]{1,0:T(8,128)(2,1)S(1)}, bf16[1280,256]{1,0:T(8,128)(2,1)}, u32[]{:S(2)}) copy-start(bf16[1280,256]{1,0:T(8,128)(2,1)} %refs_6_.5) | copy-start | bytes 1966084
  98.3 26.5 %copy-start.2 = (f32[3]{0:T(128)S(1)}, f32[3]{0:T(128)}, u32[]{:S(2)}) copy-start(f32[3]{0:T(128)} %refs_9_.3) | copy-start | bytes 40
  98.3 24.6 %collective-permute-start.13 = (bf16[496,1024]{1,0:T(8,128)(2,1)S(1)}, bf16[496,1024]{1,0:T(8,128)(2,1)S(1)}, u32[]{:S(2)}, u32[]{:S(2)}) collective-permute-start(bf16[496,1024]{1,0:T(8,128)(2,1)S(1)} %broadcast_select_fusion.1), channel_id=1, source_target_pairs={{0,4},{1,5},{2,6},{3,7},{4,0},{5,1},{6,2},{7,3},{8,12},{9,13},{10,... | collective-permute-start | bytes 3047432 | tf_op jit(solution)/shard_map/ppermute | solution.py:710
  121.6 27.1 %copy-start.5 = (bf16[496,1024]{1,0:T(8,128)(2,1)}, bf16[496,1024]{1,0:T(8,128)(2,1)S(1)}, u32[]{:S(2)}) copy-start(bf16[496,1024]{1,0:T(8,128)(2,1)S(1)} %collective-permute-done.14.refs_5_) | copy-start | bytes 3047428
  123.1 25.6 %collective-permute-start.16 = (bf16[496,1024]{1,0:T(8,128)(2,1)S(1)}, bf16[496,1024]{1,0:T(8,128)(2,1)S(1)}, u32[]{:S(2)}, u32[]{:S(2)}) collective-permute-start(bf16[496,1024]{1,0:T(8,128)(2,1)S(1)} %broadcast_select_fusion), channel_id=1, source_target_pairs={{0,4},{1,5},{2,6},{3,7},{4,0},{5,1},{6,2},{7,3},{8,12},{9,13},{10,... | collective-permute-start | bytes 3047432 | tf_op jit(solution)/shard_map/ppermute | solution.py:710
  124.8 23.9 %collective-permute-start.15 = (bf16[496,1024]{1,0:T(8,128)(2,1)S(1)}, bf16[496,1024]{1,0:T(8,128)(2,1)S(1)}, u32[]{:S(2)}, u32[]{:S(2)}) collective-permute-start(bf16[496,1024]{1,0:T(8,128)(2,1)S(1)} %broadcast_select_fusion.5), channel_id=1, source_target_pairs={{0,1},{1,0},{2,3},{3,2},{4,5},{5,4},{6,7},{7,6},{8,9},{9,8},{10,11... | collective-permute-start | bytes 3047432 | tf_op jit(solution)/shard_map/ppermute | solution.py:710
  148.7 2.9 %copy-start.6 = (bf16[496,1024]{1,0:T(8,128)(2,1)}, bf16[496,1024]{1,0:T(8,128)(2,1)S(1)}, u32[]{:S(2)}) copy-start(bf16[496,1024]{1,0:T(8,128)(2,1)S(1)} %collective-permute-done.16.refs_4_) | copy-start | bytes 3047428
  148.8 2.8 %collective-permute-start.17 = (bf16[496,1024]{1,0:T(8,128)(2,1)S(1)}, bf16[496,1024]{1,0:T(8,128)(2,1)S(1)}, u32[]{:S(2)}, u32[]{:S(2)}) collective-permute-start(bf16[496,1024]{1,0:T(8,128)(2,1)S(1)} %broadcast_select_fusion.4), channel_id=1, source_target_pairs={{0,1},{1,0},{2,3},{3,2},{4,5},{5,4},{6,7},{7,6},{8,9},{9,8},{10,11... | collective-permute-start | bytes 3047432 | tf_op jit(solution)/shard_map/ppermute | solution.py:710
  151.6 1.0 copy-start.7

commit v6 on v5

--- a/solution.py
+++ b/solution.py
@@ -14,8 +14,7 @@
 EXTRA = 16
 BF16 = jnp.bfloat16
 F32 = jnp.float32
-BLOCK_VMEM = 50 * 1024 * 1024
-FIELD_VMEM = 50 * 1024 * 1024
+MIB = 1024 * 1024
 
 
 def nn(a, b):
@@ -46,6 +45,7 @@
         self.shifted = [k for k in (1, 2, 3) if RATE * k < self.height]
         self.direct = [k for k in range(4) if k not in self.shifted]
         self.n_sh = len(self.shifted)
+        self.vmem = (40 if self.n_sh == 1 else 50) * MIB
         self.together = 2 if n % 2 == 0 and self.n_sh == 1 else 1
         row = lambda k, a: [1 + 9 * (k - 1) + 3 * a + b for b in range(3)]
         still = [row(k, 1) for k in self.direct[1:]]
@@ -70,7 +70,9 @@
         self.tables = np.concatenate([
             self.tables,
             np.array([
-                [len(c) for c in t[0]] + t[3] + [s, self.starts[s]] for s, t in enumerate(tables)
+                [len(c) for c in t[0]] + t[3] + [s, self.starts[s]]
+                + sum(([len(h)] + h + [0] * (self.depth - len(h)) for h in t[4]), [])
+                for s, t in enumerate(tables)
             ], np.int32),
         ], axis=1)
 
@@ -119,7 +121,8 @@
                 entry[4] = 4
             parts[c].append(entry)
         want = [slots.get((k, b), -1) for k in range(4) for b in range(3)]
-        return parts, len(slots), max(len(c) for c in parts), want
+        heads = [[i for i, e in enumerate(c) if e[4] != 4] for c in parts]
+        return parts, len(slots), max(len(c) for c in parts), want, heads
 
 
 def pack_kernel(pix, x_ref, lab_ref, out_ref):
@@ -302,7 +305,7 @@
         out_shape=shapes,
         input_output_aliases=aliases,
         compiler_params=pltpu.CompilerParams(
-            dimension_semantics=("arbitrary",), vmem_limit_bytes=BLOCK_VMEM
+            dimension_semantics=("arbitrary",), vmem_limit_bytes=plan.vmem
         ),
         cost_estimate=pl.CostEstimate(
             flops=len(slots) * 2 * pix * c_in * c_out * (10 + 6 * n_sh),
@@ -470,9 +473,8 @@
         p_out[...] = finish(gp[pl.ds(first, plan.proj_rows), :], prev_p[...] if last else None)
         gp[:c_out, :128] = jnp.concatenate([g_cls, jnp.zeros((112, c_out), F32)], axis=0).T
         first = pl.multiple_of(index * plan.cls_rows, plan.cls_rows)
-        c_ref_out[...] = finish(
-            gp[pl.ds(first, plan.cls_rows), :128], prev_c[...] if last else None
-        )
+        mine = finish(gp[pl.ds(first, plan.cls_rows), :128], prev_c[...] if last else None)
+        c_ref_out[...] = mine[:, :c_ref_out.shape[1]]
 
     def out_copy(part, slot, t):
         row = tab[(part * depth + t) * 6 + 5] * unit_rows
@@ -492,7 +494,10 @@
         parity = lax.rem(part, 2)
         mine = pl.ds(pl.multiple_of(part * unit_rows, unit_rows), unit_rows)
 
-        def one(t, _):
+        heads = flags + n + 14 + part * (depth + 1)
+
+        def one(i, _):
+            t = tab[heads + 1 + i]
             base = (part * depth + t) * 6
             slot, move, low, high = tab[base], tab[base + 1], tab[base + 2], tab[base + 3]
             kind = tab[base + 4]
@@ -552,9 +557,7 @@
                 else:
                     g_out[at] = finish(acc[:, lanes], None)
 
-            @pl.when(kind != 4)
-            def _():
-                emit(t, slice(0, c_out))
+            emit(t, slice(0, c_out))
 
             @pl.when(kind == 3)
             def _():
@@ -563,7 +566,7 @@
 
             return 0
 
-        lax.fori_loop(0, tab[flags + part], one, 0)
+        lax.fori_loop(0, tab[heads], one, 0)
 
         if last:
             def drain(which, slot):
@@ -621,11 +624,13 @@
     ]
     operands += [aux, aux, w_in, w_proj, w_turn, wcls, cw, xt]
     kind = F32 if last else BF16
+    out_lanes = plan.classes if last else 128
     inner = pl.BlockSpec((None, depth, unit_rows, c_out), lambda i, t: (part(i), 0, 0, 0))
     small = [
         pl.BlockSpec((plan.proj_rows, c_out), lambda i, t: (0, 0)),
         pl.BlockSpec((plan.cls_rows, 128), lambda i, t: (0, 0)),
     ]
+    out_small = [small[0], pl.BlockSpec((plan.cls_rows, out_lanes), lambda i, t: (0, 0))]
     if last:
         in_specs += [inner] + small
         operands += list(prev)
@@ -640,7 +645,7 @@
             num_scalar_prefetch=1,
             grid=(turns + n,),
             in_specs=in_specs,
-            out_specs=[main_spec] + small,
+            out_specs=[main_spec] + out_small,
             scratch_shapes=[
                 pltpu.VMEM((plan.height - RATE * k, cols, c_out), F32)
                 for k in plan.shifted for _ in range(2)
@@ -666,10 +671,10 @@
         out_shape=[
             main_shape,
             jax.ShapeDtypeStruct((plan.proj_rows, c_out), kind),
-            jax.ShapeDtypeStruct((plan.cls_rows, 128), kind),
+            jax.ShapeDtypeStruct((plan.cls_rows, out_lanes), kind),
         ],
         compiler_params=pltpu.CompilerParams(
-            dimension_semantics=("arbitrary",), vmem_limit_bytes=FIELD_VMEM
+            dimension_semantics=("arbitrary",), vmem_limit_bytes=plan.vmem
         ),
         cost_estimate=pl.CostEstimate(
             flops=10_000_000_000, bytes_accessed=90_000_000, transcendentals=0
@@ -772,7 +777,7 @@
     avg_in, avg_proj, avg_cls = run_field(
         plan, 1, tab, state, w_in, w_proj, w_turn, wcls, class_weight, grads
     )
-    return avg_in[None], avg_proj[None], avg_cls[None, :, :plan.classes]
+    return avg_in[None], avg_proj[None], avg_cls[None]
 
 
 def solution(mesh):

time: 193 us -> 189 us (0.979)
    pallas_call x2, Pallas kernels: 49.5 us -> 46.6 us  [run_field(): pl.pallas_call(functools.partial(field_kernel, plan, field, last), grid_s...]
    pallas_call x5, Pallas kernels: 56.5 us -> 58.7 us  [run_blocks(): pl.pallas_call(functools.partial(block_kernel, plan, len(arrays), len(slo...]
  transfers between devices with their start and end apart: 18 -> 18, of which waited for: 10 -> 10; matrix products, arithmetic and copies ran while one was open for 5% -> 5% of each run, Pallas kernels for 35% -> 36%
where the time goes in v6:
time: 189 us
  Pallas kernels  108 us (57%)
  waiting for transfers between devices  40.7 us (22%)
  starting transfers between devices  22.7 us (12%)
  other arithmetic  8.47 us (4%)
  local copies, waits for them, and re-layouts  6.52 us (3%)
  between operations  2.87 us (2%)
    pallas_call x5, Pallas kernels, run_blocks(): pl.pallas_call(functools.partial(block_kernel, plan, len(arrays), len(slo...  58.7 us
    pallas_call x2, Pallas kernels, run_field(): pl.pallas_call(functools.partial(field_kernel, plan, field, last), grid_s...  46.6 us
    ppermute x12, waiting for transfers between devices, hop(): return lax.ppermute(value, 'rep', [(r, r ^ 1 << b) for r in range(reps)])  29.9 us
    ppermute x6, starting transfers between devices, along(): return lax.ppermute(value, 'space', pairs)  11.4 us
    ppermute x12, starting transfers between devices, hop(): return lax.ppermute(value, 'rep', [(r, r ^ 1 << b) for r in range(reps)])  11.3 us
    ppermute x6, waiting for transfers between devices, along(): return lax.ppermute(value, 'space', pairs)  10.8 us
    another operation x7, other arithmetic, per_device(): jnp.stack([jnp.stack([(top if f else 0) + jnp.int32(n_bits * at if f and...  5.09 us
  transfers between devices with their start and end apart: 18, of which 10 were waited for; matrix products, arithmetic and copies ran while one was open for 5% of the time, Pallas kernels for 36%

profile of v6, /device:TPU:0, one launch (start us, length us, event | category | flops | bytes accessed | tf_op | source)
XLA Modules:
  0.0 188.9 jit_solution(4817168631544302539)
XLA Ops:
  0.6 0.7 convert_reduce_fusion
  1.4 0.6 pad.8.lab_ref
  2.0 2.3 %pack.1.refs_0_ = bf16[496,1024]{1,0:T(8,128)(2,1)} custom-call(bf16[480,1024]{1,0:T(8,128)(2,1)} %bitcast.39, f32[1,1024]{1,0:T(1,128)} %pad.8.lab_ref), custom_call_target="tpu_custom_call" | custom-call | tf_op jit(solution)/shard_map/pack/pallas_call | solution.py:693
  4.3 5.9 %collective-permute-start = (bf16[496,1024]{1,0:T(8,128)(2,1)}, bf16[496,1024]{1,0:T(8,128)(2,1)}, u32[]{:S(2)}, u32[]{:S(2)}) collective-permute-start(bf16[496,1024]{1,0:T(8,128)(2,1)} %pack.1.refs_0_), channel_id=1, source_target_pairs={{0,8},{8,16},{16,24},{1,9},{9,17},{17,25},{2,10},{10,18},{18,26},{... | collective-permute-start | bytes 3047432 | tf_op jit(solution)/shard_map/ppermute | solution.py:712
  10.2 1.3 collective-permute-start.1
  11.5 1.6 collective-permute-start.2
  15.0 0.7 constant_dynamic-slice_fusion.1
  15.7 0.6 fusion.9
  16.4 1.2 fusion.5
  17.6 1.2 fusion.1
  18.8 1.1 slice.45
  20.1 0.7 pad.9.refs_8_
  20.8 0.7 constant_dynamic-slice_fusion
  21.5 1.3 fusion.7
  22.8 1.3 fusion.3
  24.1 1.2 copy-done
  25.4 8.2 %block_forward.5 = (bf16[2,4,1024,480]{3,2,1,0:T(8,128)(2,1)}, bf16[2,4,480,768]{3,2,1,0:T(8,128)(2,1)S(1)}, f32[3,2,20,96,256]{4,3,2,1,0:T(8,128)}, bf16[2,4,16,1024]{3,2,1,0:T(8,128)(2,1)S(1)}) custom-call(s32[1,3]{1,0:T(1,128)S(1)} %get-tuple-element.228.meta, bf16[496,1024]{1,0:T(8,128)(2,1)S(1)} %copy-done, bf16[29,1024,256]{2,1,0:T(8,128)(2,1)} %refs_5_.3), custom_call_target="tpu_custom_call" | custom-call | flops 4026531840 | bytes 40000000 | tf_op jit(solution)/shard_map/block_forward/pallas_call | solution.py:285
  33.6 2.7 %collective-permute-done.1 = bf16[496,1024]{1,0:T(8,128)(2,1)S(1)} collective-permute-done((bf16[496,1024]{1,0:T(8,128)(2,1)}, bf16[496,1024]{1,0:T(8,128)(2,1)S(1)}, u32[]{:S(2)}, u32[]{:S(2)}) %collective-permute-start.1) | collective-permute-done | bytes 1015840 | tf_op jit(solution)/shard_map/ppermute | solution.py:712
  36.2 1.4 select_select_fusion.1.refs_0_
  37.6 1.6 collective-permute-start.6
  39.3 1.6 collective-permute-start.5
  40.9 0.7 collective-permute-start.3
  41.6 1.3 collective-permute-start.4
  42.9 8.2 %block_forward.6 = (bf16[2,4,1024,480]{3,2,1,0:T(8,128)(2,1)}, bf16[2,4,480,768]{3,2,1,0:T(8,128)(2,1)S(1)}, f32[3,2,20,96,256]{4,3,2,1,0:T(8,128)}, bf16[2,4,16,1024]{3,2,1,0:T(8,128)(2,1)S(1)}) custom-call(s32[1,3]{1,0:T(1,128)S(1)} %get-tuple-element.118.meta, ...), custom_call_target="tpu_custom_call", output_to_operand_aliasing={{0}: (3, {}), {1}: (4, {}), {2}: (5, {}), {3}: (6, {})} | custom-call | flops 4026531840 | bytes 40000000 | tf_op jit(solution)/shard_map/block_forward/pallas_call | solution.py:285
  51.1 9.6 %collective-permute-done.6.refs_3_ = bf16[496,1024]{1,0:T(8,128)(2,1)S(1)} collective-permute-done((bf16[496,1024]{1,0:T(8,128)(2,1)S(1)}, bf16[496,1024]{1,0:T(8,128)(2,1)S(1)}, u32[]{:S(2)}, u32[]{:S(2)}) %collective-permute-start.6) | collective-permute-done | bytes 1015840 | tf_op jit(solution)/shard_map/ppermute | solution.py:715
  60.7 1.4 collective-permute-done.5.refs_2_
  62.1 5.3 %collective-permute-done.4 = bf16[496,1024]{1,0:T(8,128)(2,1)S(1)} collective-permute-done((bf16[496,1024]{1,0:T(8,128)(2,1)S(1)}, bf16[496,1024]{1,0:T(8,128)(2,1)S(1)}, u32[]{:S(2)}, u32[]{:S(2)}) %collective-permute-start.4) | collective-permute-done | bytes 1015840 | tf_op jit(solution)/shard_map/ppermute | solution.py:712
  67.7 0.6 collective-permute-start.11
  68.4 0.6 collective-permute-start.10
  69.0 0.7 collective-permute-start.7
  69.7 1.5 collective-permute-start.8
  71.2 14.1 %block_forward.7 = (bf16[2,4,1024,480]{3,2,1,0:T(8,128)(2,1)}, bf16[2,4,480,768]{3,2,1,0:T(8,128)(2,1)S(1)}, f32[3,2,20,96,256]{4,3,2,1,0:T(8,128)}, bf16[2,4,16,1024]{3,2,1,0:T(8,128)(2,1)S(1)}) custom-call(s32[2,3]{1,0:T(2,128)S(1)} %pad_add_fusion.meta, ...), custom_call_target="tpu_custom_call", output_to_operand_aliasing={{0}: (6, {}), {1}: (7, {}), {2}: (8, {}), {3}: (9, {})} | custom-call | flops 8053063680 | bytes 60000000 | tf_op jit(solution)/shard_map/block_forward/pallas_call | solution.py:285
  85.3 7.3 %collective-permute-done.11.refs_2_ = bf16[496,1024]{1,0:T(8,128)(2,1)S(1)} collective-permute-done((bf16[496,1024]{1,0:T(8,128)(2,1)S(1)}, bf16[496,1024]{1,0:T(8,128)(2,1)S(1)}, u32[]{:S(2)}, u32[]{:S(2)}) %collective-permute-start.11) | collective-permute-done | bytes 1015840 | tf_op jit(solution)/shard_map/ppermute | solution.py:715
  92.6 0.4 collective-permute-done.10.refs_2_
  93.0 2.8 %collective-permute-done.8 = bf16[496,1024]{1,0:T(8,128)(2,1)S(1)} collective-permute-done((bf16[496,1024]{1,0:T(8,128)(2,1)S(1)}, bf16[496,1024]{1,0:T(8,128)(2,1)S(1)}, u32[]{:S(2)}, u32[]{:S(2)}) %collective-permute-start.8) | collective-permute-done | bytes 1015840 | tf_op jit(solution)/shard_map/ppermute | solution.py:712
  96.1 0.3 select_select_fusion.2.refs_0_
  96.4 1.6 collective-permute-start.14
  98.1 1.6 collective-permute-start.13
  99.6 14.1 %block_forward.8 = (bf16[2,4,1024,480]{3,2,1,0:T(8,128)(2,1)}, bf16[2,4,480,768]{3,2,1,0:T(8,128)(2,1)S(1)}, f32[3,2,20,96,256]{4,3,2,1,0:T(8,128)}, bf16[2,4,16,1024]{3,2,1,0:T(8,128)(2,1)S(1)}) custom-call(s32[2,3]{1,0:T(2,128)S(1)} %pad_add_fusion.1.meta, ...), custom_call_target="tpu_custom_call", output_to_operand_aliasing={{0}: (6, {}), {1}: (7, {}), {2}: (8, {}), {3}: (9, {})} | custom-call | flops 8053063680 | bytes 60000000 | tf_op jit(solution)/shard_map/block_forward/pallas_call | solution.py:285
  113.7 7.6 %collective-permute-done.14.refs_5_ = bf16[496,1024]{1,0:T(8,128)(2,1)S(1)} collective-permute-done((bf16[496,1024]{1,0:T(8,128)(2,1)S(1)}, bf16[496,1024]{1,0:T(8,128)(2,1)S(1)}, u32[]{:S(2)}, u32[]{:S(2)}) %collective-permute-start.14) | collective-permute-done | bytes 1015840 | tf_op jit(solution)/shard_map/ppermute | solution.py:715
  121.3 1.4 collective-permute-done.13.refs_1_
  122.8 1.6 collective-permute-start.16
  124.6 22.7 %field_grads.2 = (bf16[4,8,256,256]{3,2,1,0:T(8,128)(2,1)S(1)}, bf16[320,256]{1,0:T(8,128)(2,1)S(1)}, bf16[64,128]{1,0:T(8,128)(2,1)S(1)}) custom-call(s32[246]{0:T(256)S(1)} %bitcast.37, bf16[2,4,480,768]{3,2,1,0:T(8,128)(2,1)S(1)} %get-tuple-element.202.refs_0_.refs_8_, f32[3,2,20,96,256]{4,3,2,1,0:T(8,128)} %get-tuple-element.203.refs_1_.refs_2_.refs_9_, ...), custom_call_target="tpu_custom_call" | custom-call | flops 10000000000 | bytes 90000000 | tf_op jit(solution)/shard_map/field_grads/pallas_call | solution.py:642
  147.5 0.5 collective-permute-start.17
  148.0 2.2 %collective-permute-done.17.refs_3_ = bf16[496,1024]{1,0:T(8,128)(2,1)S(1)} collective-permute-done((bf16[496,1024]{1,0:T(8,128)(2,1)S(1)}, bf16[496,1024]{1,0:T(8,128)(2,1)S(1)}, u32[]{:S(2)}, u32[]{:S(2)}) %collective-permute-start.17) | collective-permute-done | bytes 1015840 | tf_op jit(solution)/shard_map/ppermute | solution.py:715
  150.2 14.1 %block_forward.9 = (bf16[2,4,1024,480]{3,2,1,0:T(8,128)(2,1)}, bf16[2,4,480,768]{3,2,1,0:T(8,128)(2,1)S(1)}, f32[3,2,20,96,256]{4,3,2,1,0:T(8,128)}, bf16[2,4,16,1024]{3,2,1,0:T(8,128)(2,1)S(1)}) custom-call(s32[2,3]{1,0:T(2,128)S(1)} %pad_add_fusion.2.meta, ...), custom_call_target="tpu_custom_call", output_to_operand_aliasing={{0}: (8, {}), {1}: (9, {}), {2}: (10, {}), {3}: (11, {})} | custom-call | flops 8053063680 | bytes 60000000 | tf_op jit(solution)/shard_map/block_forward/pallas_call | solution.py:285
  164.3 23.9 %field_grads.3 = (f32[7424,256]{1,0:T(8,128)}, f32[320,256]{1,0:T(8,128)}, f32[64,3]{1,0:T(8,128)S(1)}) custom-call(s32[246]{0:T(256)S(1)} %bitcast.38, bf16[2,4,480,768]{3,2,1,0:T(8,128)(2,1)S(1)} %get-tuple-element.205.refs_0_, f32[3,2,20,96,256]{4,3,2,1,0:T(8,128)} %get-tuple-element.206.refs_1_.refs_2_, ...), custom_call_target="tpu_custom_call" | custom-call | flops 10000000000 | bytes 90000000 | tf_op jit(solution)/shard_map/field_grads/pallas_call | solution.py:642
  188.2 0.6 copy.29
  (30 shorter events, 1.6 us)
Async XLA Ops:
  4.3 29.2 %collective-permute-start = (bf16[496,1024]{1,0:T(8,128)(2,1)}, bf16[496,1024]{1,0:T(8,128)(2,1)}, u32[]{:S(2)}, u32[]{:S(2)}) collective-permute-start(bf16[496,1024]{1,0:T(8,128)(2,1)} %pack.1.refs_0_), channel_id=1, source_target_pairs={{0,8},{8,16},{16,24},{1,9},{9,17},{17,25},{2,10},{10,18},{18,26},{... | collective-permute-start | bytes 3047432 | tf_op jit(solution)/shard_map/ppermute | solution.py:712
  10.2 26.0 %collective-permute-start.1 = (bf16[496,1024]{1,0:T(8,128)(2,1)}, bf16[496,1024]{1,0:T(8,128)(2,1)S(1)}, u32[]{:S(2)}, u32[]{:S(2)}) collective-permute-start(bf16[496,1024]{1,0:T(8,128)(2,1)} %pack.1.refs_0_), channel_id=1, source_target_pairs={{8,0},{16,8},{24,16},{9,1},{17,9},{25,17},{10,2},{18,10},{26,18},{... | collective-permute-start | bytes 3047432 | tf_op jit(solution)/shard_map/ppermute | solution.py:712
  11.5 24.7 %collective-permute-start.2 = (bf16[496,1024]{1,0:T(8,128)(2,1)}, bf16[496,1024]{1,0:T(8,128)(2,1)S(1)}, u32[]{:S(2)}, u32[]{:S(2)}) collective-permute-start(bf16[496,1024]{1,0:T(8,128)(2,1)} %pack.1.refs_0_), channel_id=1, source_target_pairs={{0,2},{1,3},{2,0},{3,1},{4,6},{5,7},{6,4},{7,5},{8,10},{9,11},{10,... | collective-permute-start | bytes 3047432 | tf_op jit(solution)/shard_map/ppermute | solution.py:715
  24.1 1.2 copy-start
  37.6 23.1 %collective-permute-start.6 = (bf16[496,1024]{1,0:T(8,128)(2,1)S(1)}, bf16[496,1024]{1,0:T(8,128)(2,1)S(1)}, u32[]{:S(2)}, u32[]{:S(2)}) collective-permute-start(bf16[496,1024]{1,0:T(8,128)(2,1)S(1)} %select_select_fusion.1.refs_0_), channel_id=1, source_target_pairs={{0,2},{1,3},{2,0},{3,1},{4,6},{5,7},{6,4},{7,5},{8,10},{9,11},{10,... | collective-permute-start | bytes 3047432 | tf_op jit(solution)/shard_map/ppermute | solution.py:715
  39.3 22.8 %collective-permute-start.5 = (bf16[496,1024]{1,0:T(8,128)(2,1)S(1)}, bf16[496,1024]{1,0:T(8,128)(2,1)S(1)}, u32[]{:S(2)}, u32[]{:S(2)}) collective-permute-start(bf16[496,1024]{1,0:T(8,128)(2,1)S(1)} %broadcast_select_fusion.3), channel_id=1, source_target_pairs={{0,4},{1,5},{2,6},{3,7},{4,0},{5,1},{6,2},{7,3},{8,12},{9,13},{10,... | collective-permute-start | bytes 3047432 | tf_op jit(solution)/shard_map/ppermute | solution.py:715
  40.9 21.2 %collective-permute-start.3 = (bf16[496,1024]{1,0:T(8,128)(2,1)}, bf16[496,1024]{1,0:T(8,128)(2,1)S(1)}, u32[]{:S(2)}, u32[]{:S(2)}) collective-permute-start(bf16[496,1024]{1,0:T(8,128)(2,1)} %collective-permute-done), channel_id=1, source_target_pairs={{8,16},{16,24},{9,17},{17,25},{10,18},{18,26},{11,19},{19,27},{12,... | collective-permute-start | bytes 3047432 | tf_op jit(solution)/shard_map/ppermute | solution.py:712
  41.6 25.8 %collective-permute-start.4 = (bf16[496,1024]{1,0:T(8,128)(2,1)S(1)}, bf16[496,1024]{1,0:T(8,128)(2,1)S(1)}, u32[]{:S(2)}, u32[]{:S(2)}) collective-permute-start(bf16[496,1024]{1,0:T(8,128)(2,1)S(1)} %collective-permute-done.1), channel_id=1, source_target_pairs={{8,0},{16,8},{9,1},{17,9},{10,2},{18,10},{11,3},{19,11},{12,4},{20... | collective-permute-start | bytes 3047432 | tf_op jit(solution)/shard_map/ppermute | solution.py:712
  67.5 3.7 %collective-permute-start.9 = (bf16[496,1024]{1,0:T(8,128)(2,1)S(1)}, bf16[496,1024]{1,0:T(8,128)(2,1)S(1)}, u32[]{:S(2)}, u32[]{:S(2)}) collective-permute-start(bf16[496,1024]{1,0:T(8,128)(2,1)S(1)} %broadcast_select_fusion.7), channel_id=1, source_target_pairs={{0,1},{1,0},{2,3},{3,2},{4,5},{5,4},{6,7},{7,6},{8,9},{9,8},{10,11... | collective-permute-start | bytes 3047432 | tf_op jit(solution)/shard_map/ppermute | solution.py:715
  67.7 24.9 %collective-permute-start.11 = (bf16[496,1024]{1,0:T(8,128)(2,1)S(1)}, bf16[496,1024]{1,0:T(8,128)(2,1)S(1)}, u32[]{:S(2)}, u32[]{:S(2)}) collective-permute-start(bf16[496,1024]{1,0:T(8,128)(2,1)S(1)} %fusion.refs_0_), channel_id=1, source_target_pairs={{0,2},{1,3},{2,0},{3,1},{4,6},{5,7},{6,4},{7,5},{8,10},{9,11},{10,... | collective-permute-start | bytes 3047432 | tf_op jit(solution)/shard_map/ppermute | solution.py:715
  68.4 24.6 %collective-permute-start.10 = (bf16[496,1024]{1,0:T(8,128)(2,1)S(1)}, bf16[496,1024]{1,0:T(8,128)(2,1)S(1)}, u32[]{:S(2)}, u32[]{:S(2)}) collective-permute-start(bf16[496,1024]{1,0:T(8,128)(2,1)S(1)} %broadcast_select_fusion.2), channel_id=1, source_target_pairs={{0,4},{1,5},{2,6},{3,7},{4,0},{5,1},{6,2},{7,3},{8,12},{9,13},{10,... | collective-permute-start | bytes 3047432 | tf_op jit(solution)/shard_map/ppermute | solution.py:715
  69.0 24.1 %collective-permute-start.7 = (bf16[496,1024]{1,0:T(8,128)(2,1)S(1)}, bf16[496,1024]{1,0:T(8,128)(2,1)S(1)}, u32[]{:S(2)}, u32[]{:S(2)}) collective-permute-start(bf16[496,1024]{1,0:T(8,128)(2,1)S(1)} %collective-permute-done.3), channel_id=1, source_target_pairs={{16,24},{17,25},{18,26},{19,27},{20,28},{21,29},{22,30},{23,31}} | collective-permute-start | bytes 3047432 | tf_op jit(solution)/shard_map/ppermute | solution.py:712
  69.7 26.2 %collective-permute-start.8 = (bf16[496,1024]{1,0:T(8,128)(2,1)S(1)}, bf16[496,1024]{1,0:T(8,128)(2,1)S(1)}, u32[]{:S(2)}, u32[]{:S(2)}) collective-permute-start(bf16[496,1024]{1,0:T(8,128)(2,1)S(1)} %collective-permute-done.4), channel_id=1, source_target_pairs={{8,0},{9,1},{10,2},{11,3},{12,4},{13,5},{14,6},{15,7}} | collective-permute-start | bytes 3047432 | tf_op jit(solution)/shard_map/ppermute | solution.py:712
  96.0 3.6 %collective-permute-start.12 = (bf16[496,1024]{1,0:T(8,128)(2,1)S(1)}, bf16[496,1024]{1,0:T(8,128)(2,1)S(1)}, u32[]{:S(2)}, u32[]{:S(2)}) collective-permute-start(bf16[496,1024]{1,0:T(8,128)(2,1)S(1)} %broadcast_select_fusion.6), channel_id=1, source_target_pairs={{0,1},{1,0},{2,3},{3,2},{4,5},{5,4},{6,7},{7,6},{8,9},{9,8},{10,11... | collective-permute-start | bytes 3047432 | tf_op jit(solution)/shard_map/ppermute | solution.py:715
  96.4 24.9 %collective-permute-start.14 = (bf16[496,1024]{1,0:T(8,128)(2,1)S(1)}, bf16[496,1024]{1,0:T(8,128)(2,1)S(1)}, u32[]{:S(2)}, u32[]{:S(2)}) collective-permute-start(bf16[496,1024]{1,0:T(8,128)(2,1)S(1)} %select_select_fusion.2.refs_0_), channel_id=1, source_target_pairs={{0,2},{1,3},{2,0},{3,1},{4,6},{5,7},{6,4},{7,5},{8,10},{9,11},{10,... | collective-permute-start | bytes 3047432 | tf_op jit(solution)/shard_map/ppermute | solution.py:715
  98.0 26.6 %copy-start.1 = (bf16[1280,256]{1,0:T(8,128)(2,1)S(1)}, bf16[1280,256]{1,0:T(8,128)(2,1)}, u32[]{:S(2)}) copy-start(bf16[1280,256]{1,0:T(8,128)(2,1)} %refs_6_.5) | copy-start | bytes 1966084
  98.0 26.6 %copy-start.2 = (f32[3]{0:T(128)S(1)}, f32[3]{0:T(128)}, u32[]{:S(2)}) copy-start(f32[3]{0:T(128)} %refs_9_.3) | copy-start | bytes 40
  98.1 24.6 %collective-permute-start.13 = (bf16[496,1024]{1,0:T(8,128)(2,1)S(1)}, bf16[496,1024]{1,0:T(8,128)(2,1)S(1)}, u32[]{:S(2)}, u32[]{:S(2)}) collective-permute-start(bf16[496,1024]{1,0:T(8,128)(2,1)S(1)} %broadcast_select_fusion.1), channel_id=1, source_target_pairs={{0,4},{1,5},{2,6},{3,7},{4,0},{5,1},{6,2},{7,3},{8,12},{9,13},{10,... | collective-permute-start | bytes 3047432 | tf_op jit(solution)/shard_map/ppermute | solution.py:715
  122.8 24.5 %collective-permute-start.16 = (bf16[496,1024]{1,0:T(8,128)(2,1)S(1)}, bf16[496,1024]{1,0:T(8,128)(2,1)S(1)}, u32[]{:S(2)}, u32[]{:S(2)}) collective-permute-start(bf16[496,1024]{1,0:T(8,128)(2,1)S(1)} %broadcast_select_fusion), channel_id=1, source_target_pairs={{0,4},{1,5},{2,6},{3,7},{4,0},{5,1},{6,2},{7,3},{8,12},{9,13},{10,... | collective-permute-start | bytes 3047432 | tf_op jit(solution)/shard_map/ppermute | solution.py:715
  124.5 22.8 %collective-permute-start.15 = (bf16[496,1024]{1,0:T(8,128)(2,1)S(1)}, bf16[496,1024]{1,0:T(8,128)(2,1)S(1)}, u32[]{:S(2)}, u32[]{:S(2)}) collective-permute-start(bf16[496,1024]{1,0:T(8,128)(2,1)S(1)} %broadcast_select_fusion.5), channel_id=1, source_target_pairs={{0,1},{1,0},{2,3},{3,2},{4,5},{5,4},{6,7},{7,6},{8,9},{9,8},{10,11... | collective-permute-start | bytes 3047432 | tf_op jit(solution)/shard_map/ppermute | solution.py:715
  147.5 2.8 %collective-permute-start.17 = (bf16[496,1024]{1,0:T(8,128)(2,1)S(1)}, bf16[496,1024]{1,0:T(8,128)(2,1)S(1)}, u32[]{:S(2)}, u32[]{:S(2)}) collective-permute-start(bf16[496,1024]{1,0:T(8,128)(2,1)S(1)} %broadcast_select_fusion.4), channel_id=1, source_target_pairs={{0,1},{1,0},{2,3},{3,2},{4,5},{5,4},{6,7},{7,6},{8,9},{9,8},{10,11... | collective-permute-start | bytes 3047432 | tf_op jit(solution)/shard_map/ppermute | solution.py:715
